TPU v7x, 32 devices: a whole 2x2x4 slice. The times are simulated.
32 devices in a mesh: groups: 2 (over x), tensor: 8 (over z, y), dp: 2 (over core).
Axes of the slice: x: 2, y: 2, z: 4, core: 2. Of those that a mesh axis runs over, the one named last changes fastest.
Arguments:
- cotangent: bfloat16 [2048, 5120], P(('groups', 'dp', 'tensor')), parts along dimension 0, may hold values from -6 to 6
- gate_activation_stored: bfloat16 [2048, 25600], P(('groups', 'dp'), 'tensor'), parts along dimension 0, may hold values from -6 to 6
- up_activation_stored: bfloat16 [2048, 25600], P(('groups', 'dp'), 'tensor'), parts along dimension 0, may hold values from -6 to 6
- gate_matrix: bfloat16 [5120, 25600], P('dp', 'tensor'), may hold values from -0.078125 to 0.078125
- up_matrix: bfloat16 [5120, 25600], P('dp', 'tensor'), may hold values from -0.078125 to 0.078125
- down_matrix: bfloat16 [5120, 25600], P('dp', 'tensor'), may hold values from -0.0390625 to 0.0390625
- adapter_input_factor: bfloat16 [6, 25600, 64], P(None, 'tensor'), may hold values from -0.0390625 to 0.0390625
- adapter_output_factor: bfloat16 [6, 64, 5120], P(None, None, 'tensor'), may hold values from -0.078125 to 0.078125
- padded_block_segment: int32 [16], P('groups'), parts along dimension 0, may hold values from 0 to 5, never falling along the last dimension, each value on 1 to 2 neighbouring positions
- segment_adapter_index: int32 [12, 1], P('groups'), parts along dimension 0, may hold values from 0 to 5
- adapter_grad_slot: int32 [6], replicated, may hold values from 0 to 5, each once
Outputs:
- input_grad: bfloat16 [2048, 5120], P(('groups', 'dp', 'tensor')), parts along dimension 0
- grad_a: bfloat16 [12, 25600, 64], P(('groups', 'dp'), 'tensor'), parts along dimension 0
- grad_b: bfloat16 [12, 64, 5120], P(('groups', 'dp'), None, 'tensor'), parts along dimension 0
There are 2 independent parts, one for each index of `groups`. A program takes and returns all parts, laid end to end along the dimension named above; an argument that names none is the same for every part. Nothing has to cross between parts.
Inputs may be any that keep to these rules, and one draw needn't show every extreme that they name: padded_block_segment never falls; each segment holds 1 to 2 blocks. `segment_adapter_index`: every adapter is named by some segment. `adapter_grad_slot`: each slot is named once.
All inputs are finite; a program needn't handle non-finite values.
Results may differ from a plain program's by a relative error of at most 0.007.
Values may be sent and summed in bfloat16 or wider, within the bound.
No kernel may reach another device: no remote copies, remote signals or barrier semaphores. Data moves between devices by JAX's collectives and lax.ppermute only.
A program may use at most 384 MiB of HBM per device.

v0:
```python
import jax
import jax.numpy as jnp
from jax import lax
from jax.sharding import PartitionSpec as P

BLOCK = 128


ADAPTER_SCALE = 2.0


def body(
    cotangent,
    gate_activation_stored,
    up_activation_stored,
    gate_matrix,
    up_matrix,
    down_matrix,
    adapter_input_factor,
    adapter_output_factor,
    padded_block_segment,
    segment_adapter_index,
    adapter_grad_slot,
):
    local_token_rows = gate_activation_stored.shape[0]
    local_hidden_units = gate_activation_stored.shape[1]
    adapter_list = adapter_input_factor.shape[0]
    local_columns = adapter_output_factor.shape[2]
    seg_count = segment_adapter_index.shape[0]
    block_count = local_token_rows // BLOCK
    dp_index = lax.axis_index("dp")
    tensor_index = lax.axis_index("tensor")
    grad_all = lax.all_gather(cotangent, "tensor", axis=0, tiled=True)
    segments_here = lax.dynamic_slice_in_dim(
        padded_block_segment, dp_index * block_count, block_count
    )
    seg_onehot = (segments_here[:, None] == jnp.arange(seg_count, dtype=jnp.int32)[None, :]).astype(
        jnp.float32
    )
    adapter_onehot = (
        segment_adapter_index[:, 0][:, None] == jnp.arange(adapter_list, dtype=jnp.int32)[None, :]
    ).astype(jnp.float32)
    block_onehot = jnp.dot(seg_onehot, adapter_onehot)
    block_selector = block_onehot.astype(jnp.bfloat16)
    gate = gate_activation_stored.astype(jnp.float32)
    upper = up_activation_stored.astype(jnp.float32)
    sigmoid_gate = jax.nn.sigmoid(gate)
    silu_gate = gate * sigmoid_gate
    hidden_state = (silu_gate * upper).astype(jnp.bfloat16)
    hidden_blocks = hidden_state.reshape(block_count, BLOCK, local_hidden_units)
    cols_mine = lax.dynamic_slice_in_dim(grad_all, tensor_index * local_columns, local_columns, 1)
    cols_blocks = cols_mine.reshape(block_count, BLOCK, local_columns)
    a_blocks = jnp.einsum(
        "yz,zuo->yuo", block_selector, adapter_input_factor, preferred_element_type=jnp.float32
    ).astype(jnp.bfloat16)
    b_blocks = jnp.einsum(
        "vl,lyt->vyt", block_selector, adapter_output_factor, preferred_element_type=jnp.float32
    ).astype(jnp.bfloat16)
    part_in = jnp.einsum(
        "btf,bfr->btr", hidden_blocks, a_blocks, preferred_element_type=jnp.float32
    )
    part_out = jnp.einsum("btc,brc->btr", cols_blocks, b_blocks, preferred_element_type=jnp.float32)
    lowrank_input, lowrank_output = lax.psum((part_in, part_out), "tensor")
    lowrank_input = lowrank_input.astype(jnp.bfloat16)
    lowrank_output = lowrank_output.astype(jnp.bfloat16)
    gate_full, up_full, down_full = (
        lax.all_gather(gate_matrix, "dp", axis=0, tiled=True),
        lax.all_gather(up_matrix, "dp", axis=0, tiled=True),
        lax.all_gather(down_matrix, "dp", axis=0, tiled=True),
    )
    hidden_gradient = jnp.dot(grad_all, down_full, preferred_element_type=jnp.float32)
    additional_term = jnp.einsum(
        "btr,bfr->btf", lowrank_output, a_blocks, preferred_element_type=jnp.float32
    )
    hidden_gradient = hidden_gradient + ADAPTER_SCALE * additional_term.reshape(
        local_token_rows, local_hidden_units
    )
    gate_grad = (
        hidden_gradient * upper * sigmoid_gate * (1.0 + gate * (1.0 - sigmoid_gate))
    ).astype(jnp.bfloat16)
    up_grad = (hidden_gradient * silu_gate).astype(jnp.bfloat16)
    outer_product_input = jnp.einsum(
        "btf,btr->bfr", hidden_blocks, lowrank_output, preferred_element_type=jnp.float32
    )
    outer_product_output = jnp.einsum(
        "btr,btc->brc", lowrank_input, cols_blocks, preferred_element_type=jnp.float32
    )
    slot_onehot = (
        jnp.arange(adapter_list, dtype=jnp.int32)[:, None] == adapter_grad_slot[None, :]
    ).astype(jnp.float32)
    slot_block_mask = jnp.dot(slot_onehot, block_onehot.T)
    input_factor_terms = ADAPTER_SCALE * jnp.einsum(
        "pc,cdw->pdw", slot_block_mask, outer_product_input
    )
    output_factor_terms = ADAPTER_SCALE * jnp.einsum(
        "fn,nlv->flv", slot_block_mask, outer_product_output
    )
    owned_a, owned_b = (
        lax.psum_scatter(input_factor_terms, "dp", scatter_dimension=0, tiled=True),
        lax.psum_scatter(output_factor_terms, "dp", scatter_dimension=0, tiled=True),
    )
    grad_a = owned_a.astype(jnp.bfloat16)
    grad_b = owned_b.astype(jnp.bfloat16)
    first = lax.dot_general(
        gate_grad, gate_full, (((1,), (1,)), ((), ())), preferred_element_type=jnp.float32
    )
    second = lax.dot_general(
        up_grad, up_full, (((1,), (1,)), ((), ())), preferred_element_type=jnp.float32
    )
    summed = lax.psum_scatter(first + second, "tensor", scatter_dimension=0, tiled=True)
    input_grad = summed.astype(jnp.bfloat16)
    return (input_grad, grad_a, grad_b)


def solution(mesh):
    return jax.shard_map(
        body,
        mesh=mesh,
        in_specs=(
            P(("groups", "dp", "tensor"), None),
            P(("groups", "dp"), "tensor"),
            P(("groups", "dp"), "tensor"),
            P("dp", "tensor"),
            P("dp", "tensor"),
            P("dp", "tensor"),
            P(None, "tensor", None),
            P(None, None, "tensor"),
            P("groups"),
            P("groups", None),
            P(),
        ),
        out_specs=(
            P(("groups", "dp", "tensor"), None),
            P(("groups", "dp"), "tensor", None),
            P(("groups", "dp"), None, "tensor"),
        ),
        check_vma=False,
    )
```

profile of v0, /device:TPU:1, one launch (start us, length us, event | category | flops | bytes accessed | tf_op | source)
XLA Modules:
  0.0 475.7 jit_solution(2622364409772813443)
XLA Ops:
  7.2 0.7 all-gather.5.cloned.1.call-update
  8.0 0.7 all-gather.7.cloned.1.call-update
  10.3 2.0 convolution_convert_fusion
  12.4 4.0 fusion.3
  16.5 1.7 copy-done.2
  18.1 1.0 fusion.13
  19.7 78.1 %all-gather.5.cloned.1.call-done = bf16[512,5120]{1,0:T(8,128)(2,1)} async-done(((bf16[64,5120]{1,0:T(8,128)(2,1)}), bf16[512,5120]{1,0:T(8,128)(2,1)}) %all-gather.5.cloned.1.call-update) | async-done | bytes 5242896 | tf_op jit(solution)/shard_map/all_gather | solution.py:33
  97.8 1.1 constant_dynamic-slice_fusion
  99.3 34.0 %all-reduce.2 = (bf16[4,128,64]{1,2,0:T(8,128)(2,1)S(1)}, bf16[4,128,64]{2,1,0:T(8,128)(2,1)S(1)}) all-reduce(f32[4,128,64]{1,2,0:T(8,128)S(1)} %fusion.19, f32[4,128,64]{2,1,0:T(8,128)S(1)} %fusion.13), channel_id=1, replica_groups=mesh['groups'=2,'tensor'=8,'dp'=2] {'tensor'}, use_global_device_ids=true, to_apply=%region_0.0 | all-reduce | flops 65536 | bytes 393216 | tf_op jit(solution)/shard_map/psum | solution.py:63
  134.0 1.1 copy.21
  135.2 2.5 fusion.36
  137.8 1.7 convolution_multiply_fusion.1
  139.4 3.1 copy.20
  142.5 3.8 convolution_multiply_fusion
  146.5 2.5 all-gather.7.cloned.1.call-done
  149.0 33.1 %bitcast_add_fusion = f32[512,3200]{1,0:T(8,128)} fusion(f32[4,128,3200]{2,1,0:T(8,128)} %convolution_multiply_fusion, bf16[512,5120]{1,0:T(8,128)(2,1)} %all-gather.5.cloned.1.call-done, bf16[5120,3200]{1,0:T(8,128)(2,1)} %all-gather.7.cloned.1.call-done), kind=kOutput, calls=%fused_computation.16 | convolution fusion | flops 16778854400 | bytes 51118080 | tf_op jit(solution)/shard_map/dot_general | solution.py:71
  182.1 19.9 %all-gather.9.cloned.1.call-done = bf16[5120,3200]{1,0:T(8,128)(2,1)} async-done(((bf16[2560,3200]{1,0:T(8,128)(2,1)}), bf16[5120,3200]{1,0:T(8,128)(2,1)}) %all-gather.9.cloned.1.call-update) | async-done | bytes 32768016 | tf_op jit(solution)/shard_map/all_gather | solution.py:67
  202.0 35.6 %fusion.8 = f32[512,5120]{1,0:T(8,128)} fusion(bf16[5120,3200]{1,0:T(8,128)(2,1)} %all-gather.9.cloned.1.call-done, f32[512,3200]{1,0:T(8,128)} %bitcast_add_fusion, bf16[512,3200]{1,0:T(8,128)(2,1)} %param.13, bf16[512,3200]{1,0:T(8,128)(2,1)} %param.12), kind=kOutput, calls=%fused_computation.19 | convolution fusion | flops 16796876800 | bytes 56360960 | tf_op jit(solution)/shard_map/dot_general | solution.py:104
  237.6 17.3 %all-gather.11.cloned.1.call-done = bf16[5120,3200]{1,0:T(8,128)(2,1)} async-done(((bf16[2560,3200]{1,0:T(8,128)(2,1)}), bf16[5120,3200]{1,0:T(8,128)(2,1)}) %all-gather.11.cloned.1.call-update) | async-done | bytes 32768016 | tf_op jit(solution)/shard_map/all_gather | solution.py:68
  254.9 31.0 %convolution_add_fusion = f32[512,5120]{1,0:T(8,128)} fusion(f32[512,5120]{1,0:T(8,128)} %fusion.8, bf16[5120,3200]{1,0:T(8,128)(2,1)} %all-gather.11.cloned.1.call-done, f32[512,3200]{1,0:T(8,128)} %bitcast_add_fusion, bf16[512,3200]{1,0:T(8,128)(2,1)} %param.12), kind=kOutput, calls=%fused_computation.5 | convolution fusion | flops 16791306240 | bytes 63569920 | tf_op jit(solution)/shard_map/dot_general | solution.py:107
  285.9 1.9 convert_element_type.54
  287.8 2.9 convert_element_type.52
  290.6 176.0 %reduce-scatter.4.cloned.1.call-done = f32[64,5120]{1,0:T(8,128)} async-done(((f32[512,5120]{1,0:T(8,128)}), f32[64,5120]{1,0:T(8,128)}) %reduce-scatter.4.cloned.1.call-update) | async-done | bytes 1310736 | tf_op jit(solution)/shard_map/reduce_scatter | solution.py:110
  466.6 2.2 convert_element_type.50
  (40 shorter events, 3.7 us)
Async XLA Ops:
  7.2 3.2 copy-start
  7.2 90.6 %all-gather.5.cloned.1.call-start = ((), (), s32[]{:S(2)}) async-start(), calls=%async_computation.3 | async-start | bytes 5898240 | tf_op jit(solution)/shard_map/all_gather | solution.py:33
  7.9 141.1 %all-gather.7.cloned.1.call-start = ((), (), s32[]{:S(2)}) async-start(), calls=%async_computation.4 | async-start | bytes 49152000 | tf_op jit(solution)/shard_map/all_gather | solution.py:69
  8.7 193.3 %all-gather.9.cloned.1.call-start = ((), (), s32[]{:S(2)}) async-start(), calls=%async_computation.5 | async-start | bytes 49152000 | tf_op jit(solution)/shard_map/all_gather | solution.py:67
  9.4 0.7 copy-start.7
  9.4 0.7 copy-start.8
  9.4 245.4 %all-gather.11.cloned.1.call-start = ((), (), s32[]{:S(2)}) async-start(), calls=%async_computation.6 | async-start | bytes 49152000 | tf_op jit(solution)/shard_map/all_gather | solution.py:68
  10.0 275.9 %reduce-scatter.8.cloned.1.call-start = ((), (), s32[]{:S(2)}) async-start(), calls=%async_computation.9 | async-start | bytes 1474560 | tf_op jit(solution)/shard_map/reduce_scatter | solution.py:100
  10.1 2.3 copy-start.5
  12.4 4.1 copy-start.3
  12.4 6.8 %copy-start.9 = (s32[6]{0:T(128)S(1)}, s32[6]{0:T(128)}, u32[]{:S(2)}) copy-start(s32[6]{0:T(128)} %param.21) | copy-start | bytes 76
  12.4 6.9 %copy-start.6 = (bf16[6,64,640]{2,1,0:T(8,128)(2,1)S(1)}, bf16[6,64,640]{2,1,0:T(8,128)(2,1)}, u32[]{:S(2)}) copy-start(bf16[6,64,640]{2,1,0:T(8,128)(2,1)} %param.18) | copy-start | bytes 1474564
  16.4 1.7 copy-start.2
  135.2 152.6 %reduce-scatter.6.cloned.1.call-start = ((), (), s32[]{:S(2)}) async-start(), calls=%async_computation.8 | async-start | bytes 7372800 | tf_op jit(solution)/shard_map/reduce_scatter | solution.py:99
  139.4 3.1 copy-start.4
  146.3 320.3 %reduce-scatter.4.cloned.1.call-start = ((), (), s32[]{:S(2)}) async-start(), calls=%async_computation.7 | async-start | bytes 11796480 | tf_op jit(solution)/shard_map/reduce_scatter | solution.py:110
  285.8 183.0 %copy-start.1 = (bf16[6,3200,64]{1,2,0:T(8,128)(2,1)S(1)}, bf16[6,3200,64]{1,2,0:T(8,128)(2,1)}, u32[]{:S(2)}) copy-start(bf16[6,3200,64]{1,2,0:T(8,128)(2,1)} %param.17) | copy-start | bytes 7372804
Sparse Core Ops, SparseCore 0:
  10.2 87.5 all-gather.4
  99.3 49.6 all-gather.6
  150.6 51.3 all-gather.8
  203.4 51.3 all-gather.10
  257.5 9.6 reduce-scatter.7
  269.5 14.0 reduce-scatter.5
  287.6 178.9 reduce-scatter.3
where the time goes:
time: 477 us; the launch traced here: 476 us
  waiting for transfers between devices  296 us (62%)
  matrix products  112 us (23%)
  blocking collectives  34 us (7%)
  between operations  14.3 us (3%)
  other arithmetic  11 us (2%)
  local copies, waits for them, and re-layouts  7.13 us (1%)
    reduce_scatter x1, waiting for transfers between devices, body(): lax.psum_scatter(first + second, 'tensor', scatter_dimension=0, tiled=True)  176 us
    all_gather x1, waiting for transfers between devices, body(): grad_all = lax.all_gather(cotangent, 'tensor', axis=0, tiled=True)  78.1 us
    dot_general x1, matrix products, body(): lax.dot_general(gate_grad, gate_full, (((1,), (1,)), ((), ())), preferred...  35.6 us
    psum x1, blocking collectives, body(): lowrank_input, lowrank_output = lax.psum((part_in, part_out), 'tensor')  34 us
    dot_general x1, matrix products, body(): jnp.dot(grad_all, down_full, preferred_element_type=jnp.float32)  33.1 us
    dot_general x1, matrix products, body(): lax.dot_general(up_grad, up_full, (((1,), (1,)), ((), ())), preferred_ele...  31 us
    all_gather x1, waiting for transfers between devices, body(): lax.all_gather(gate_matrix, 'dp', axis=0, tiled=True)  19.9 us
    all_gather x1, waiting for transfers between devices, body(): lax.all_gather(up_matrix, 'dp', axis=0, tiled=True)  17.3 us
  transfers between devices with their start and end apart: 7, of which 5 were waited for; matrix products, arithmetic and copies ran while one was open for 27% of the time, Pallas kernels for 0%

commit v1 on v0

--- a/solution.py
+++ b/solution.py
@@ -1,12 +1,455 @@
+import functools
+
 import jax
 import jax.numpy as jnp
 from jax import lax
+from jax.experimental import pallas as pl
+from jax.experimental.pallas import tpu as pltpu
 from jax.sharding import PartitionSpec as P
 
 BLOCK = 128
 
 
 ADAPTER_SCALE = 2.0
+
+F32 = jnp.float32
+BF16 = jnp.bfloat16
+MIB = 1024 * 1024
+
+Y_SWAP = [(t, t ^ 1) for t in range(8)]
+PAIR = [(t, t ^ 2) for t in range(8)]
+FAR = [(t, t ^ 4) for t in range(8)]
+MID = [(2, 4), (3, 5), (4, 2), (5, 3)]
+OUTWARD = [(2, 0), (3, 1), (4, 6), (5, 7)]
+INWARD = [(0, 2), (1, 3), (6, 4), (7, 5)]
+CORES = [(0, 1), (1, 0)]
+
+M_T, M_Y, M_D, M_Z, M_SLOT_ADAPTER, M_ADAPTER, M_GRAD_SLOT = 0, 1, 2, 3, 7, 11, 15
+
+
+def nt_dot(a, b):
+    return lax.dot_general(a, b, (((1,), (1,)), ((), ())), preferred_element_type=F32)
+
+
+def tn_dot(a, b):
+    return lax.dot_general(a, b, (((0,), (0,)), ((), ())), preferred_element_type=F32)
+
+
+def call(
+    kernel, meta, args, grid, in_specs, out_specs, out_shape, scratch=(), flops=0, nbytes=0, vmem=48, after=()
+):
+    first, extra = len(args), len(after)
+
+    def run(m, *refs):
+        kernel(m, *refs[:first], *refs[first + extra :])
+
+    return pl.pallas_call(
+        run,
+        grid_spec=pltpu.PrefetchScalarGridSpec(
+            num_scalar_prefetch=1,
+            grid=grid,
+            in_specs=list(in_specs) + [pl.BlockSpec(memory_space=pl.ANY)] * extra,
+            out_specs=out_specs,
+            scratch_shapes=list(scratch),
+        ),
+        out_shape=out_shape,
+        compiler_params=pltpu.CompilerParams(vmem_limit_bytes=vmem * MIB),
+        cost_estimate=pl.CostEstimate(flops=flops, bytes_accessed=nbytes, transcendentals=0),
+    )(meta, *args, *after)
+
+
+def pack_halves(p):
+    h = p.shape[0] // 2
+    return jnp.concatenate([p[:h], p[h:]], axis=1)
+
+
+def unpack_halves(p):
+    h = p.shape[1] // 2
+    return jnp.concatenate([p[:, :h], p[:, h:]], axis=0)
+
+
+def hidden_kernel(m, gate_ref, up_ref, a_ref, hidden_ref, low_ref):
+    g = gate_ref[...].astype(F32)
+    hidden = (g * jax.nn.sigmoid(g) * up_ref[...].astype(F32)).astype(BF16)
+    hidden_ref[...] = hidden
+    low_ref[...] = pack_halves(nt_dot(hidden, a_ref[0]))
+
+
+def hidden_and_low_in(meta, gate_act, up_act, a_t):
+    rows, width = gate_act.shape
+    rank = a_t.shape[1]
+    blocks = rows // BLOCK
+    return call(
+        hidden_kernel,
+        meta,
+        (gate_act, up_act, a_t),
+        (blocks,),
+        [
+            pl.BlockSpec((BLOCK, width), lambda b, m: (b, 0)),
+            pl.BlockSpec((BLOCK, width), lambda b, m: (b, 0)),
+            pl.BlockSpec((1, rank, width), lambda b, m: (m[M_ADAPTER + b], 0, 0)),
+        ],
+        [
+            pl.BlockSpec((BLOCK, width), lambda b, m: (b, 0)),
+            pl.BlockSpec((BLOCK // 2, 2 * rank), lambda b, m: (b, 0)),
+        ],
+        [
+            jax.ShapeDtypeStruct((rows, width), BF16),
+            jax.ShapeDtypeStruct((rows // 2, 2 * rank), F32),
+        ],
+        flops=2 * rows * width * rank * 2,
+        nbytes=8 * rows * width,
+    )
+
+
+def low_out_kernel(m, *refs):
+    shards, b_ref, cols_ref, low_ref = refs[:8], refs[8], refs[9], refs[10]
+    rows = shards[0].shape[0]
+    y = m[M_Y]
+    for s in range(4):
+        z = m[M_Z + s]
+        own, other = shards[2 * s][...], shards[2 * s + 1][...]
+        first = jnp.where(y == 0, own, other)
+        second = jnp.where(y == 0, other, own)
+        tokens = jnp.concatenate([first, second], axis=0)
+        cols_ref[pl.ds(pl.multiple_of(z * 2 * rows, 2 * rows), 2 * rows), :] = tokens
+        part = nt_dot(tokens, b_ref[m[M_SLOT_ADAPTER + s]])
+        low_ref[pl.ds(pl.multiple_of(z * rows, rows), rows), :] = pack_halves(part)
+
+
+def low_out_parts(meta, shards, b, after):
+    rows = shards[0].shape[0]
+    adapters, rank, columns = b.shape
+    return call(
+        low_out_kernel,
+        meta,
+        (*shards, b),
+        (1,),
+        [pl.BlockSpec((rows, columns), lambda i, m: (0, m[M_T]))] * 8
+        + [pl.BlockSpec((adapters, rank, columns), lambda i, m: (0, 0, 0))],
+        [
+            pl.BlockSpec((8 * rows, columns), lambda i, m: (0, 0)),
+            pl.BlockSpec((4 * rows, 2 * rank), lambda i, m: (0, 0)),
+        ],
+        [
+            jax.ShapeDtypeStruct((8 * rows, columns), BF16),
+            jax.ShapeDtypeStruct((4 * rows, 2 * rank), F32),
+        ],
+        flops=2 * 8 * rows * columns * rank,
+        nbytes=4 * 8 * rows * columns,
+        after=after,
+    )
+
+
+def hidden_grad_kernel(count, m, *refs):
+    mine, other = refs[:count], refs[count : 2 * count]
+    down_mine, down_other, out_ref, lhs = refs[2 * count :]
+    rows = mine[0].shape[0]
+
+    @pl.when(pl.program_id(0) == 0)
+    def _():
+        for s in range(count):
+            lhs[0, s * rows : (s + 1) * rows] = mine[s][...]
+            lhs[1, s * rows : (s + 1) * rows] = other[s][...]
+
+    total = jnp.dot(lhs[0], down_mine[...], preferred_element_type=F32)
+    out_ref[...] = total + jnp.dot(lhs[1], down_other[...], preferred_element_type=F32)
+
+
+def hidden_grad(meta, shards, mine, other, span, after=()):
+    rows = shards[0].shape[0]
+    half = mine.shape[0]
+    start, width, step = span
+    count = len(shards)
+    total = rows * count
+    return call(
+        functools.partial(hidden_grad_kernel, count),
+        meta,
+        (*shards, *shards, mine, other),
+        (width // step,),
+        [pl.BlockSpec((rows, half), lambda n, m: (0, m[M_D]))] * count
+        + [pl.BlockSpec((rows, half), lambda n, m: (0, 1 - m[M_D]))] * count
+        + [pl.BlockSpec((half, step), lambda n, m: (0, n + start // step))] * 2,
+        pl.BlockSpec((total, step), lambda n, m: (0, n)),
+        jax.ShapeDtypeStruct((total, width), F32),
+        scratch=[pltpu.VMEM((2, total, half), BF16)],
+        flops=2 * total * 2 * half * width,
+        nbytes=2 * 2 * half * width,
+        after=after,
+    )
+
+
+def act_grad_kernel(spans, m, *refs):
+    hg_refs, (gate_ref, up_ref, low_ref, a_ref, out_ref) = refs[: len(spans)], refs[len(spans) :]
+    j = pl.program_id(0)
+    y = m[M_Y]
+    rank = low_ref.shape[1] // 2
+    second = jnp.where(j == 0, y, 1 - y) == 1
+    low = jnp.where(second, low_ref[:, rank:], low_ref[:, :rank])
+    for hg_ref, (start, width, _) in zip(hg_refs, spans):
+        at = slice(start, start + width)
+        hg = hg_ref[...] + ADAPTER_SCALE * jnp.dot(low, a_ref[0, :, at], preferred_element_type=F32)
+        g = gate_ref[:, at].astype(F32)
+        u = up_ref[:, at].astype(F32)
+        sig = jax.nn.sigmoid(g)
+        out_ref[0, :, at] = (hg * u * sig * (1.0 + g * (1.0 - sig))).astype(BF16)
+        out_ref[1, :, at] = (hg * (g * sig)).astype(BF16)
+
+
+def act_grad(meta, slot, spans, hgs, gate_act, up_act, low, a_t, after=()):
+    rank, width = a_t.shape[1:]
+    rows = BLOCK // 2
+
+    def shard_of(j, m):
+        y = m[M_Y]
+        return (m[M_Z + slot] * 2 + y + j * (1 - 2 * y), 0)
+
+    return call(
+        functools.partial(act_grad_kernel, spans),
+        meta,
+        (*hgs, gate_act, up_act, low, a_t),
+        (2,),
+        [pl.BlockSpec((rows, w), lambda j, m: ((slot % 2) * 2 + j, 0)) for _, w, _ in spans]
+        + [
+            pl.BlockSpec((rows, width), shard_of),
+            pl.BlockSpec((rows, width), shard_of),
+            pl.BlockSpec((rows, 2 * rank), lambda j, m: (m[M_Z + slot], 0)),
+            pl.BlockSpec((1, rank, width), lambda j, m: (m[M_SLOT_ADAPTER + slot], 0, 0)),
+        ],
+        pl.BlockSpec((2, rows, width), lambda j, m: (0, j, 0)),
+        jax.ShapeDtypeStruct((2, 2 * rows, width), BF16),
+        flops=2 * 2 * rows * width * rank,
+        nbytes=2 * rows * width * 12,
+        after=after,
+    )
+
+
+def input_grad_kernel(m, mine_ref, other_ref, gate_ref, up_ref, keep_ref, send_ref, lhs):
+    rows = mine_ref.shape[1] // 2
+
+    @pl.when(pl.program_id(0) == 0)
+    def _():
+        for i in range(2):
+            for y in range(2):
+                lhs[i, (2 * y) * rows : (2 * y + 1) * rows] = mine_ref[i, y * rows : (y + 1) * rows]
+                lhs[i, (2 * y + 1) * rows : (2 * y + 2) * rows] = other_ref[i, y * rows : (y + 1) * rows]
+
+    total = nt_dot(lhs[0], gate_ref[...]) + nt_dot(lhs[1], up_ref[...])
+    keep_ref[...] = total[: 2 * rows].astype(BF16)
+    send_ref[...] = total[2 * rows :].astype(BF16)
+
+
+def input_grad_parts(meta, mine, other, gate, up, after=()):
+    rows, width = mine.shape[1:]
+    half = gate.shape[0]
+    step = 512
+    out = jax.ShapeDtypeStruct((rows, half), BF16)
+    return call(
+        input_grad_kernel,
+        meta,
+        (mine, other, gate, up),
+        (half // step,),
+        [pl.BlockSpec((2, rows, width), lambda n, m: (0, 0, 0))] * 2
+        + [pl.BlockSpec((step, width), lambda n, m: (n, 0))] * 2,
+        [pl.BlockSpec((rows, step), lambda n, m: (0, n))] * 2,
+        [out, out],
+        scratch=[pltpu.VMEM((2, 2 * rows, width), BF16)],
+        flops=2 * 2 * rows * 2 * width * half,
+        nbytes=2 * 2 * width * half,
+        after=after,
+    )
+
+
+def owner_kernel(blocks, m, low_ref, features_ref, keep_ref, send_ref):
+    i = pl.program_id(0)
+    d = m[M_D]
+    owned = keep_ref.shape[0] * pl.num_programs(0)
+    rows = low_ref.shape[0] // blocks
+    for ref, owner in ((keep_ref, d), (send_ref, 1 - d)):
+        slot = owner * owned + i
+        total = jnp.zeros(ref.shape[1:], F32)
+        for b in range(blocks):
+            hit = jnp.where(m[M_GRAD_SLOT + b] == slot, ADAPTER_SCALE, 0.0)
+            low = unpack_halves(low_ref[b * rows : (b + 1) * rows, :])
+            total += hit * tn_dot(low, features_ref[b * BLOCK : (b + 1) * BLOCK, :])
+        ref[0] = total.astype(BF16)
+
+
+def owner_grads(meta, low, features, owned, after=()):
+    tokens, width = features.shape
+    half_rows, double = low.shape
+    rank = double // 2
+    out = jax.ShapeDtypeStruct((owned, rank, width), BF16)
+    return call(
+        functools.partial(owner_kernel, tokens // BLOCK),
+        meta,
+        (low, features),
+        (owned,),
+        [
+            pl.BlockSpec((half_rows, double), lambda i, m: (0, 0)),
+            pl.BlockSpec((tokens, width), lambda i, m: (0, 0)),
+        ],
+        [pl.BlockSpec((1, rank, width), lambda i, m: (i, 0, 0))] * 2,
+        [out, out],
+        flops=2 * tokens * rank * width * 2 * owned,
+        nbytes=2 * tokens * width,
+        after=after,
+    )
+
+
+def add_kernel(count, m, *refs):
+    total = refs[0][...].astype(F32)
+    for r in refs[1:count]:
+        total += r[...].astype(F32)
+    for r in refs[count:]:
+        r[...] = total.astype(r.dtype)
+
+
+def add_after(meta, xs, after, kinds=(BF16,), steps=1):
+    rows, width = xs[0].shape
+    spec = pl.BlockSpec((rows // steps, width), lambda i, m: (i, 0))
+    out = call(
+        functools.partial(add_kernel, len(xs)),
+        meta,
+        xs,
+        (steps,),
+        [spec] * len(xs),
+        [spec] * len(kinds),
+        [jax.ShapeDtypeStruct((rows, width), k) for k in kinds],
+        nbytes=2 * rows * width * (len(xs) + 1),
+        vmem=16,
+        after=after,
+    )
+    return out if len(kinds) > 1 else out[0]
+
+
+def add(*xs):
+    return functools.reduce(jnp.add, [x.astype(F32) for x in xs]).astype(BF16)
+
+
+def tied(x, *others):
+    return lax.optimization_barrier((x, *others))[0]
+
+
+def grid_body(
+    cotangent,
+    gate_act,
+    up_act,
+    gate_matrix,
+    up_matrix,
+    down_matrix,
+    adapter_input_factor,
+    adapter_output_factor,
+    padded_block_segment,
+    segment_adapter_index,
+    adapter_grad_slot,
+):
+    adapters = adapter_input_factor.shape[0]
+    blocks = gate_act.shape[0] // BLOCK
+    d = lax.axis_index("dp")
+    t = lax.axis_index("tensor")
+    z, y = t // 2, t % 2
+    low_side = z < 2
+    slots_z = jnp.stack([z, z ^ 1, jnp.where(low_side, 2, 1), jnp.where(low_side, 3, 0)])
+    segments_here = lax.dynamic_slice_in_dim(padded_block_segment, d * blocks, blocks)
+
+    def pick(table, index):
+        hit = index[:, None] == jnp.arange(table.shape[0], dtype=jnp.int32)[None, :]
+        return jnp.sum(jnp.where(hit, table[None, :], 0), axis=1)
+
+    block_adapter = pick(segment_adapter_index[:, 0], segments_here)
+    meta = jnp.concatenate(
+        [
+            jnp.stack([t, y, d]),
+            slots_z,
+            pick(block_adapter, slots_z),
+            block_adapter,
+            pick(adapter_grad_slot, block_adapter),
+        ]
+    ).astype(jnp.int32)
+    a_t = jnp.swapaxes(adapter_input_factor, 1, 2)
+    send = functools.partial(lax.ppermute, axis_name="tensor")
+    swap_cores = functools.partial(lax.ppermute, axis_name="dp", perm=CORES)
+    at_end = (z == 0) | (z == 3)
+
+    width = gate_act.shape[1]
+    step = width * 2 // 5
+    spans = ((0, step, step // 5), (step, step, step // 5), (2 * step, width - 2 * step, width - 2 * step))
+
+    down_other = swap_cores(down_matrix)
+    pair = send(cotangent, perm=PAIR)
+    mid = send(cotangent, perm=MID)
+    y0 = send(cotangent, perm=Y_SWAP)
+    hidden, low_in = hidden_and_low_in(meta, gate_act, up_act, a_t)
+    y1 = send(tied(pair, y0, low_in), perm=Y_SWAP)
+    pair_mid = send(tied(pair, low_in), perm=MID)
+    mid_out = send(tied(mid, low_in), perm=OUTWARD)
+    slot2 = jnp.where(at_end, mid_out, mid)
+    y2 = send(tied(slot2, y1), perm=Y_SWAP)
+    far_out = send(pair_mid, perm=OUTWARD)
+    hg_near, last = [], (low_in,)
+    for span in spans:
+        hg_near.append(hidden_grad(meta, (cotangent, y0, pair, y1), down_matrix, down_other, span, last))
+        last = (hg_near[-1],)
+    slot3 = jnp.where(at_end, tied(far_out, hg_near[0]), pair_mid)
+    y3 = send(tied(slot3, y2), perm=Y_SWAP)
+
+    far = (slot2, y2, slot3, y3)
+    columns, low_part = low_out_parts(meta, (cotangent, y0, pair, y1, *far), adapter_output_factor, last)
+    hg_far = []
+    low_sum, low_out = low_part, low_part.astype(BF16)
+    for perm, span in zip((Y_SWAP, PAIR, FAR), spans):
+        got = send(low_out, perm=perm)
+        hg_far.append(hidden_grad(meta, far, down_matrix, down_other, span, (low_out,)))
+        low_sum, low_out = add_after(meta, (low_sum, got), (hg_far[-1],), (F32, BF16))
+
+    def grads(slot, after):
+        hgs = hg_far if slot >= 2 else hg_near
+        return act_grad(meta, slot, spans, hgs, gate_act, up_act, low_out, a_t, after)
+
+    def parts(mine, other, after):
+        keep, give = input_grad_parts(meta, mine, other, gate_matrix, up_matrix, after)
+        return keep, send(give, perm=Y_SWAP), give
+
+    mine3 = grads(3, ())
+    low_in1 = low_in.astype(BF16)
+    got_in = send(low_in1, perm=Y_SWAP)
+    other3 = swap_cores(mine3)
+    mine2 = grads(2, (mine3,))
+    other2 = swap_cores(mine2)
+    low_in2, low_in2b = add_after(meta, (low_in, got_in), (mine2,), (F32, BF16))
+    got_in = send(low_in2b, perm=PAIR)
+    keep3, got3, give3 = parts(mine3, other3, (low_in2b,))
+    mine1 = grads(1, (give3,))
+    other1 = swap_cores(mine1)
+    low_in3, low_in3b = add_after(meta, (low_in2, got_in), (mine1,), (F32, BF16))
+    got_in = send(low_in3b, perm=FAR)
+    keep2, got2, give2 = parts(mine2, other2, (low_in3b,))
+    mine0 = grads(0, (give2,))
+    other0 = swap_cores(mine0)
+    sum3 = add_after(meta, (keep3, got3), (mine0,))
+    far_in = send(sum3, perm=INWARD)
+    keep1, got1, give1 = parts(mine1, other1, (sum3,))
+    sum2 = add_after(meta, (keep2, got2), (give1,))
+    mid_in = send(sum2, perm=INWARD)
+    far_mid = send(add_after(meta, (sum3, far_in), (sum2,)), perm=MID)
+    low_in4 = add_after(meta, (low_in3, got_in), (sum2,))
+    keep0, got0, give0 = parts(mine0, other0, (low_in4, sum2))
+    from_mid = send(add_after(meta, (sum2, mid_in), (give0,)), perm=MID)
+    from_pair = send(add_after(meta, (keep1, got1, far_mid), (give0,)), perm=PAIR)
+    owned = adapters // 2
+    keep_a, give_a = owner_grads(meta, low_out, hidden, owned, (give0,))
+    keep_b, give_b = owner_grads(meta, low_in4, columns, owned, (keep_a,))
+    grad_a = jnp.swapaxes(add(keep_a, swap_cores(give_a)), 1, 2)
+    grad_b = add(keep_b, swap_cores(give_b))
+    final = add_after(meta, (keep0, got0, from_pair, from_mid), (keep_b,))
+    own_rows = cotangent.shape[0]
+    got = swap_cores(final[own_rows:])
+    own = final[:own_rows]
+    input_grad = jnp.where(
+        d == 0, jnp.concatenate([own, got], axis=1), jnp.concatenate([got, own], axis=1)
+    )
+    return (input_grad, grad_a, grad_b)
 
 
 def body(
@@ -114,7 +557,7 @@
 
 def solution(mesh):
     return jax.shard_map(
-        body,
+        grid_body if mesh.shape["tensor"] == 8 and mesh.shape["dp"] == 2 else body,
         mesh=mesh,
         in_specs=(
             P(("groups", "dp", "tensor"), None),

time: 477 us -> 250 us (0.52)
  waiting for transfers between devices: 296 us -> 38.6 us
  Pallas kernels: 0 us -> 149 us
  matrix products: 112 us -> 0 us
  starting transfers between devices: 0.45 us -> 41.6 us
  blocking collectives: 34 us -> 0 us
  between operations: 14.3 us -> 1.16 us
    reduce_scatter x3 -> x0, waiting for transfers between devices: 176 us -> none  [the longest x1 176 us: body(): lax.psum_scatter(first + second, 'tensor', scatter_dimension=0, tiled=True)]
    pallas_call x0 -> x30, Pallas kernels: none -> 149 us  [call(): pl.pallas_call(run, grid_spec=pltpu.PrefetchScalarGridSpec(num_scalar_pre...]
    all_gather x4 -> x0, waiting for transfers between devices: 118 us -> none  [the longest x1 78.1 us: body(): grad_all = lax.all_gather(cotangent, 'tensor', axis=0, tiled=True)]
    dot_general x14 -> x0, matrix products: 112 us -> none  [the longest x1 35.6 us: body(): lax.dot_general(gate_grad, gate_full, (((1,), (1,)), ((), ())), preferred...]
    ppermute x0 -> x32, starting transfers between devices: none -> 41.6 us  [the longest x1 3.85 us: grid_body(): other3 = swap_cores(mine3)]
    ppermute x0 -> x32, waiting for transfers between devices: none -> 38.6 us  [the longest x1 14.4 us: grid_body(): mid_out = send(tied(mid, low_in), perm=OUTWARD)]
    psum x1 -> x0, blocking collectives: 34 us -> none  [body(): lowrank_input, lowrank_output = lax.psum((part_in, part_out), 'tensor')]
    convert_element_type x4 -> x3, other arithmetic: 11 us -> 0.77 us  [the longest x1 0.75 us: add(): return functools.reduce(jnp.add, [x.astype(F32) for x in xs]).astype(BF16)]
  transfers between devices with their start and end apart: 7 -> 32, of which waited for: 5 -> 7; matrix products, arithmetic and copies ran while one was open for 27% -> 3% of each run, Pallas kernels for 0% -> 57%
where the time goes in v1:
time: 250 us; the launch traced here: 249 us
  Pallas kernels  149 us (60%)
  starting transfers between devices  41.6 us (17%)
  waiting for transfers between devices  38.6 us (15%)
  local copies, waits for them, and re-layouts  10.7 us (4%)
  other arithmetic  7.55 us (3%)
    pallas_call x30, Pallas kernels, call(): pl.pallas_call(run, grid_spec=pltpu.PrefetchScalarGridSpec(num_scalar_pre...  149 us
    ppermute x1, waiting for transfers between devices, grid_body(): mid_out = send(tied(mid, low_in), perm=OUTWARD)  14.4 us
    ppermute x4, waiting for transfers between devices, parts(): return (keep, send(give, perm=Y_SWAP), give)  13.9 us
    unnamed x36, local copies, waits for them, and re-layouts  9.88 us
  transfers between devices with their start and end apart: 32, of which 7 were waited for; matrix products, arithmetic and copies ran while one was open for 3% of the time, Pallas kernels for 57%

profile of v1, /device:TPU:1, one launch (start us, length us, event | category | flops | bytes accessed | tf_op | source)
XLA Modules:
  0.0 248.8 jit_solution(6383204427201331994)
XLA Ops:
  0.8 2.8 %collective-permute-start.1 = (bf16[64,5120]{1,0:T(8,128)(2,1)}, bf16[64,5120]{1,0:T(8,128)(2,1)S(1)}, u32[]{:S(2)}, u32[]{:S(2)}) collective-permute-start(bf16[64,5120]{1,0:T(8,128)(2,1)} %refs_0_.9), channel_id=1, source_target_pairs={{0,4},{2,6},{4,0},{6,2},{8,12},{10,14},{12,8},{14,10},{1,5},{3,7},... | collective-permute-start | bytes 1966088 | tf_op jit(solution)/shard_map/ppermute | solution.py:380
  10.0 5.2 %shard_map.130 = (bf16[512,3200]{1,0:T(8,128)(2,1)S(1)}, f32[256,128]{1,0:T(8,128)S(1)}) custom-call(s32[19]{0:T(128)S(1)} %concatenate.10.m, bf16[512,3200]{1,0:T(8,128)(2,1)} %refs_3_.13, bf16[512,3200]{1,0:T(8,128)(2,1)} %refs_4_.13, bf16[6,64,3200]{2,1,0:T(8,128)(2,1)S(1)} %bitcast.15), custom_call_target="tpu_custom_call" | custom-call | flops 419430400 | bytes 13107200 | tf_op jit(solution)/shard_map/pallas_call | solution.py:46
  24.1 14.4 %collective-permute-done.5 = bf16[64,5120]{1,0:T(8,128)(2,1)} collective-permute-done((bf16[64,5120]{1,0:T(8,128)(2,1)S(1)}, bf16[64,5120]{1,0:T(8,128)(2,1)}, u32[]{:S(2)}, u32[]{:S(2)}) %collective-permute-start.5) | collective-permute-done | bytes 655392 | tf_op jit(solution)/shard_map/ppermute | solution.py:386
  41.0 8.7 %shard_map.131.refs_10_.refs_0_ = f32[256,1280]{1,0:T(8,128)S(1)} custom-call(s32[19]{0:T(128)S(1)} %concatenate.10.m, bf16[64,5120]{1,0:T(8,128)(2,1)S(1)} %copy-done.1, bf16[64,5120]{1,0:T(8,128)(2,1)S(1)} %collective-permute-done.refs_1_.refs_5_, bf16[64,5120]{1,0:T(8,128)(2,1)S(1)} %collective-permute-done.1.refs_2_.refs_6_, ...), custom_call_target="tpu_custom_call" | custom-call | flops 3355443200 | bytes 13107200 | tf_op jit(solution)/shard_map/pallas_call | solution.py:46
  49.7 3.1 %collective-permute-done.8 = bf16[64,5120]{1,0:T(8,128)(2,1)S(1)} collective-permute-done((bf16[64,5120]{1,0:T(8,128)(2,1)}, bf16[64,5120]{1,0:T(8,128)(2,1)S(1)}, u32[]{:S(2)}, u32[]{:S(2)}) %collective-permute-start.8) | collective-permute-done | bytes 655392 | tf_op jit(solution)/shard_map/ppermute | solution.py:389
  55.5 8.7 %shard_map.132.refs_10_.refs_1_ = f32[256,1280]{1,0:T(8,128)S(1)} custom-call(s32[19]{0:T(128)S(1)} %concatenate.10.m, bf16[64,5120]{1,0:T(8,128)(2,1)S(1)} %copy-done.1, bf16[64,5120]{1,0:T(8,128)(2,1)S(1)} %collective-permute-done.refs_1_.refs_5_, bf16[64,5120]{1,0:T(8,128)(2,1)S(1)} %collective-permute-done.1.refs_2_.refs_6_, ...), custom_call_target="tpu_custom_call" | custom-call | flops 3355443200 | bytes 13107200 | tf_op jit(solution)/shard_map/pallas_call | solution.py:46
  64.2 5.8 %shard_map.133.refs_9_.refs_2_ = f32[256,640]{1,0:T(8,128)S(1)} custom-call(s32[19]{0:T(128)S(1)} %concatenate.10.m, bf16[64,5120]{1,0:T(8,128)(2,1)S(1)} %copy-done.1, bf16[64,5120]{1,0:T(8,128)(2,1)S(1)} %collective-permute-done.refs_1_.refs_5_, bf16[64,5120]{1,0:T(8,128)(2,1)S(1)} %collective-permute-done.1.refs_2_.refs_6_, ...), custom_call_target="tpu_custom_call" | custom-call | flops 1677721600 | bytes 6553600 | tf_op jit(solution)/shard_map/pallas_call | solution.py:46
  75.0 8.7 %shard_map.135.refs_2_.refs_0_ = f32[256,1280]{1,0:T(8,128)S(1)} custom-call(s32[19]{0:T(128)S(1)} %concatenate.10.m, bf16[64,5120]{1,0:T(8,128)(2,1)S(1)} %broadcast_select_fusion.1.refs_4_.refs_0_, bf16[64,5120]{1,0:T(8,128)(2,1)S(1)} %collective-permute-done.6.refs_5_.refs_1_, bf16[64,5120]{1,0:T(8,128)(2,1)S(1)} %broadcast_select_fusion.refs_6_.refs_2_, ...), custom_call_target="tpu_custom_call" | custom-call | flops 3355443200 | bytes 13107200 | tf_op jit(solution)/shard_map/pallas_call | solution.py:46
  84.8 8.7 %shard_map.137.refs_2_.refs_1_ = f32[256,1280]{1,0:T(8,128)S(1)} custom-call(s32[19]{0:T(128)S(1)} %concatenate.10.m, bf16[64,5120]{1,0:T(8,128)(2,1)S(1)} %broadcast_select_fusion.1.refs_4_.refs_0_, bf16[64,5120]{1,0:T(8,128)(2,1)S(1)} %collective-permute-done.6.refs_5_.refs_1_, bf16[64,5120]{1,0:T(8,128)(2,1)S(1)} %broadcast_select_fusion.refs_6_.refs_2_, ...), custom_call_target="tpu_custom_call" | custom-call | flops 3355443200 | bytes 13107200 | tf_op jit(solution)/shard_map/pallas_call | solution.py:46
  96.4 5.8 %shard_map.139.refs_2_ = f32[256,640]{1,0:T(8,128)S(1)} custom-call(s32[19]{0:T(128)S(1)} %concatenate.10.m, bf16[64,5120]{1,0:T(8,128)(2,1)S(1)} %broadcast_select_fusion.1.refs_4_.refs_0_, bf16[64,5120]{1,0:T(8,128)(2,1)S(1)} %collective-permute-done.6.refs_5_.refs_1_, bf16[64,5120]{1,0:T(8,128)(2,1)S(1)} %broadcast_select_fusion.refs_6_.refs_2_, ...), custom_call_target="tpu_custom_call" | custom-call | flops 1677721600 | bytes 6553600 | tf_op jit(solution)/shard_map/pallas_call | solution.py:46
  103.5 3.3 %shard_map.141.refs_7_.refs_0_ = bf16[2,128,3200]{2,1,0:T(8,128)(2,1)S(1)} custom-call(s32[19]{0:T(128)S(1)} %concatenate.10.m, f32[256,1280]{1,0:T(8,128)S(1)} %shard_map.135.refs_2_.refs_0_, f32[256,1280]{1,0:T(8,128)S(1)} %shard_map.137.refs_2_.refs_1_, f32[256,640]{1,0:T(8,128)S(1)} %shard_map.139.refs_2_, bf16[512,3200]{1,0:T(8,128)(2,1)} %refs_3_.13, ...), custom_call_target="tpu_custom_call" | custom-call | flops 52428800 | bytes 4915200 | tf_op jit(solution)/shard_map/pallas_call | solution.py:46
  106.8 3.9 %collective-permute-start.16 = (bf16[2,128,3200]{2,1,0:T(8,128)(2,1)S(1)}, bf16[2,128,3200]{2,1,0:T(8,128)(2,1)S(1)}, u32[]{:S(2)}, u32[]{:S(2)}) collective-permute-start(bf16[2,128,3200]{2,1,0:T(8,128)(2,1)S(1)} %shard_map.141.refs_7_.refs_0_), channel_id=1, source_target_pairs={{0,1},{1,0},{2,3},{3,2},{4,5},{5,4},{6,7},{7,6},{8,9},{9,8},{10,11... | collective-permute-start | bytes 4915208 | tf_op jit(solution)/shard_map/ppermute | solution.py:417
  110.7 3.3 %shard_map.142.refs_2_.refs_0_ = bf16[2,128,3200]{2,1,0:T(8,128)(2,1)S(1)} custom-call(s32[19]{0:T(128)S(1)} %concatenate.10.m, f32[256,1280]{1,0:T(8,128)S(1)} %shard_map.135.refs_2_.refs_0_, f32[256,1280]{1,0:T(8,128)S(1)} %shard_map.137.refs_2_.refs_1_, f32[256,640]{1,0:T(8,128)S(1)} %shard_map.139.refs_2_, bf16[512,3200]{1,0:T(8,128)(2,1)} %refs_3_.13, ...), custom_call_target="tpu_custom_call" | custom-call | flops 52428800 | bytes 4915200 | tf_op jit(solution)/shard_map/pallas_call | solution.py:46
  122.9 15.5 %shard_map.144 = (bf16[128,2560]{1,0:T(8,128)(2,1)S(1)}, bf16[128,2560]{1,0:T(8,128)(2,1)S(1)}) custom-call(s32[19]{0:T(128)S(1)} %concatenate.10.m, bf16[2,128,3200]{2,1,0:T(8,128)(2,1)S(1)} %copy-done.5, bf16[2,128,3200]{2,1,0:T(8,128)(2,1)S(1)} %copy-done.9, bf16[2560,3200]{1,0:T(8,128)(2,1)} %refs_2_.7, bf16[2560,3200]{1,0:T(8,128)(2,1)} %refs_3_.15, ...), custom_call_target="tpu_custom_call" | custom-call | flops 8388608000 | bytes 32768000 | tf_op jit(solution)/shard_map/pallas_call | solution.py:46
  138.4 3.5 %shard_map.145.refs_2_.refs_0_ = bf16[2,128,3200]{2,1,0:T(8,128)(2,1)S(1)} custom-call(s32[19]{0:T(128)S(1)} %concatenate.10.m, f32[256,1280]{1,0:T(8,128)S(1)} %shard_map.131.refs_10_.refs_0_, f32[256,1280]{1,0:T(8,128)S(1)} %shard_map.132.refs_10_.refs_1_, f32[256,640]{1,0:T(8,128)S(1)} %copy-done.7, bf16[512,3200]{1,0:T(8,128)(2,1)} %refs_3_.13, ...), custom_call_target="tpu_custom_call" | custom-call | flops 52428800 | bytes 4915200 | tf_op jit(solution)/shard_map/pallas_call | solution.py:46
  143.6 15.5 %shard_map.147 = (bf16[128,2560]{1,0:T(8,128)(2,1)S(1)}, bf16[128,2560]{1,0:T(8,128)(2,1)S(1)}) custom-call(s32[19]{0:T(128)S(1)} %concatenate.10.m, bf16[2,128,3200]{2,1,0:T(8,128)(2,1)S(1)} %shard_map.142.refs_2_.refs_0_, bf16[2,128,3200]{2,1,0:T(8,128)(2,1)S(1)} %collective-permute-done.13.refs_1_, bf16[2560,3200]{1,0:T(8,128)(2,1)} %refs_2_.7, ...), custom_call_target="tpu_custom_call" | custom-call | flops 8388608000 | bytes 32768000 | tf_op jit(solution)/shard_map/pallas_call | solution.py:46
  159.1 3.3 %shard_map.148.refs_2_.refs_0_ = bf16[2,128,3200]{2,1,0:T(8,128)(2,1)S(1)} custom-call(s32[19]{0:T(128)S(1)} %concatenate.10.m, f32[256,1280]{1,0:T(8,128)S(1)} %shard_map.131.refs_10_.refs_0_, f32[256,1280]{1,0:T(8,128)S(1)} %shard_map.132.refs_10_.refs_1_, f32[256,640]{1,0:T(8,128)S(1)} %copy-done.7, bf16[512,3200]{1,0:T(8,128)(2,1)} %refs_3_.13, ...), custom_call_target="tpu_custom_call" | custom-call | flops 52428800 | bytes 4915200 | tf_op jit(solution)/shard_map/pallas_call | solution.py:46
  164.6 13.9 %collective-permute-done.21.refs_1_ = bf16[128,2560]{1,0:T(8,128)(2,1)S(1)} collective-permute-done((bf16[128,2560]{1,0:T(8,128)(2,1)S(1)}, bf16[128,2560]{1,0:T(8,128)(2,1)S(1)}, u32[]{:S(2)}, u32[]{:S(2)}) %collective-permute-start.21) | collective-permute-done | bytes 655392 | tf_op jit(solution)/shard_map/ppermute | solution.py:412
  179.2 2.9 %collective-permute-start.24 = (bf16[128,2560]{1,0:T(8,128)(2,1)S(1)}, bf16[128,2560]{1,0:T(8,128)(2,1)S(1)}, u32[]{:S(2)}, u32[]{:S(2)}) collective-permute-start(bf16[128,2560]{1,0:T(8,128)(2,1)S(1)} %shard_map.149.refs_4_.refs_0_), channel_id=1, source_target_pairs={{0,4},{2,6},{12,8},{14,10},{1,5},{3,7},{13,9},{15,11},{16,20},{18,... | collective-permute-start | bytes 1966088 | tf_op jit(solution)/shard_map/ppermute | solution.py:431
  182.1 15.5 %shard_map.150 = (bf16[128,2560]{1,0:T(8,128)(2,1)S(1)}, bf16[128,2560]{1,0:T(8,128)(2,1)S(1)}) custom-call(s32[19]{0:T(128)S(1)} %concatenate.10.m, bf16[2,128,3200]{2,1,0:T(8,128)(2,1)S(1)} %shard_map.145.refs_2_.refs_0_, bf16[2,128,3200]{2,1,0:T(8,128)(2,1)S(1)} %collective-permute-done.20.refs_1_, bf16[2560,3200]{1,0:T(8,128)(2,1)} %refs_2_.7, ...), custom_call_target="tpu_custom_call" | custom-call | flops 8388608000 | bytes 32768000 | tf_op jit(solution)/shard_map/pallas_call | solution.py:46
  202.9 15.5 %shard_map.153 = (bf16[128,2560]{1,0:T(8,128)(2,1)S(1)}, bf16[128,2560]{1,0:T(8,128)(2,1)S(1)}) custom-call(s32[19]{0:T(128)S(1)} %concatenate.10.m, bf16[2,128,3200]{2,1,0:T(8,128)(2,1)S(1)} %shard_map.148.refs_2_.refs_0_, bf16[2,128,3200]{2,1,0:T(8,128)(2,1)S(1)} %collective-permute-done.17.refs_1_, bf16[2560,3200]{1,0:T(8,128)(2,1)} %refs_2_.7, ...), custom_call_target="tpu_custom_call" | custom-call | flops 8388608000 | bytes 32768000 | tf_op jit(solution)/shard_map/pallas_call | solution.py:46
  225.7 6.7 %shard_map.157 = (bf16[3,64,3200]{2,1,0:T(8,128)(2,1)S(1)}, bf16[3,64,3200]{2,1,0:T(8,128)(2,1)}) custom-call(s32[19]{0:T(128)S(1)} %concatenate.10.m, bf16[256,128]{1,0:T(8,128)(2,1)S(1)} %get-tuple-element.46.refs_5_.refs_0_, bf16[512,3200]{1,0:T(8,128)(2,1)} %copy-done.17, bf16[128,2560]{1,0:T(8,128)(2,1)S(1)} %get-tuple-element.57.refs_3_.refs_2_), custom_call_target="tpu_custom_call" | custom-call | flops 1258291200 | bytes 3276800 | tf_op jit(solution)/shard_map/pallas_call | solution.py:46
  232.4 3.5 %collective-permute-start.30 = (bf16[3,64,3200]{2,1,0:T(8,128)(2,1)}, bf16[3,64,3200]{2,1,0:T(8,128)(2,1)}, u32[]{:S(2)}, u32[]{:S(2)}) collective-permute-start(bf16[3,64,3200]{2,1,0:T(8,128)(2,1)} %get-tuple-element.63), channel_id=1, source_target_pairs={{0,1},{1,0},{2,3},{3,2},{4,5},{5,4},{6,7},{7,6},{8,9},{9,8},{10,11... | collective-permute-start | bytes 3686408 | tf_op jit(solution)/shard_map/ppermute | solution.py:443
  245.3 2.6 %fusion = bf16[3,3200,64]{1,2,0:T(8,128)(2,1)} fusion(bf16[3,64,3200]{2,1,0:T(8,128)(2,1)} %collective-permute-done.30, bf16[3,64,3200]{2,1,0:T(8,128)(2,1)S(1)} %get-tuple-element.61.refs_2_), kind=kLoop, calls=%fused_computation.1 | loop fusion | flops 2457600 | bytes 3686400 | tf_op jit(solution)/shard_map/transpose | solution.py:443
  (120 shorter events, 66.9 us)
Async XLA Ops:
  0.6 40.4 %collective-permute-start.3 = (bf16[2560,3200]{1,0:T(8,128)(2,1)}, bf16[2560,3200]{1,0:T(8,128)(2,1)}, u32[]{:S(2)}, u32[]{:S(2)}) collective-permute-start(bf16[2560,3200]{1,0:T(8,128)(2,1)} %refs_8_.13), channel_id=1, source_target_pairs={{0,1},{1,0},{2,3},{3,2},{4,5},{5,4},{6,7},{7,6},{8,9},{9,8},{10,11... | collective-permute-start | bytes 49152008 | tf_op jit(solution)/shard_map/ppermute | solution.py:379
  0.8 18.0 %collective-permute-start.1 = (bf16[64,5120]{1,0:T(8,128)(2,1)}, bf16[64,5120]{1,0:T(8,128)(2,1)S(1)}, u32[]{:S(2)}, u32[]{:S(2)}) collective-permute-start(bf16[64,5120]{1,0:T(8,128)(2,1)} %refs_0_.9), channel_id=1, source_target_pairs={{0,4},{2,6},{4,0},{6,2},{8,12},{10,14},{12,8},{14,10},{1,5},{3,7},... | collective-permute-start | bytes 1966088 | tf_op jit(solution)/shard_map/ppermute | solution.py:380
  3.5 16.7 %collective-permute-start.4 = (bf16[64,5120]{1,0:T(8,128)(2,1)}, bf16[64,5120]{1,0:T(8,128)(2,1)S(1)}, u32[]{:S(2)}, u32[]{:S(2)}) collective-permute-start(bf16[64,5120]{1,0:T(8,128)(2,1)} %refs_0_.9), channel_id=1, source_target_pairs={{4,8},{6,10},{8,4},{10,6},{5,9},{7,11},{9,5},{11,7},{20,24},{22,26... | collective-permute-start | bytes 1966088 | tf_op jit(solution)/shard_map/ppermute | solution.py:381
  4.2 17.3 %collective-permute-start = (bf16[64,5120]{1,0:T(8,128)(2,1)}, bf16[64,5120]{1,0:T(8,128)(2,1)S(1)}, u32[]{:S(2)}, u32[]{:S(2)}) collective-permute-start(bf16[64,5120]{1,0:T(8,128)(2,1)} %refs_0_.9), channel_id=1, source_target_pairs={{0,2},{2,0},{4,6},{6,4},{8,10},{10,8},{12,14},{14,12},{1,3},{3,1},... | collective-permute-start | bytes 1966088 | tf_op jit(solution)/shard_map/ppermute | solution.py:382
  20.2 18.3 %collective-permute-start.5 = (bf16[64,5120]{1,0:T(8,128)(2,1)S(1)}, bf16[64,5120]{1,0:T(8,128)(2,1)}, u32[]{:S(2)}, u32[]{:S(2)}) collective-permute-start(bf16[64,5120]{1,0:T(8,128)(2,1)S(1)} %collective-permute-done.4), channel_id=1, source_target_pairs={{4,0},{6,2},{8,12},{10,14},{5,1},{7,3},{9,13},{11,15},{20,16},{22,... | collective-permute-start | bytes 1966088 | tf_op jit(solution)/shard_map/ppermute | solution.py:386
  21.5 18.2 %collective-permute-start.2 = (bf16[64,5120]{1,0:T(8,128)(2,1)S(1)}, bf16[64,5120]{1,0:T(8,128)(2,1)S(1)}, u32[]{:S(2)}, u32[]{:S(2)}) collective-permute-start(bf16[64,5120]{1,0:T(8,128)(2,1)S(1)} %collective-permute-done.1.refs_2_.refs_6_), channel_id=1, source_target_pairs={{0,2},{2,0},{4,6},{6,4},{8,10},{10,8},{12,14},{14,12},{1,3},{3,1},... | collective-permute-start | bytes 1966088 | tf_op jit(solution)/shard_map/ppermute | solution.py:384
  22.8 30.0 %collective-permute-start.8 = (bf16[64,5120]{1,0:T(8,128)(2,1)}, bf16[64,5120]{1,0:T(8,128)(2,1)S(1)}, u32[]{:S(2)}, u32[]{:S(2)}) collective-permute-start(bf16[64,5120]{1,0:T(8,128)(2,1)} %collective-permute-done.7), channel_id=1, source_target_pairs={{4,0},{6,2},{8,12},{10,14},{5,1},{7,3},{9,13},{11,15},{20,16},{22,... | collective-permute-start | bytes 1966088 | tf_op jit(solution)/shard_map/ppermute | solution.py:389
  39.7 14.5 %collective-permute-start.6 = (bf16[64,5120]{1,0:T(8,128)(2,1)S(1)}, bf16[64,5120]{1,0:T(8,128)(2,1)S(1)}, u32[]{:S(2)}, u32[]{:S(2)}) collective-permute-start(bf16[64,5120]{1,0:T(8,128)(2,1)S(1)} %broadcast_select_fusion.1.refs_4_.refs_0_), channel_id=1, source_target_pairs={{0,2},{2,0},{4,6},{6,4},{8,10},{10,8},{12,14},{14,12},{1,3},{3,1},... | collective-permute-start | bytes 1966088 | tf_op jit(solution)/shard_map/ppermute | solution.py:388
  54.3 16.7 %collective-permute-start.9 = (bf16[64,5120]{1,0:T(8,128)(2,1)S(1)}, bf16[64,5120]{1,0:T(8,128)(2,1)S(1)}, u32[]{:S(2)}, u32[]{:S(2)}) collective-permute-start(bf16[64,5120]{1,0:T(8,128)(2,1)S(1)} %broadcast_select_fusion.refs_6_.refs_2_), channel_id=1, source_target_pairs={{0,2},{2,0},{4,6},{6,4},{8,10},{10,8},{12,14},{14,12},{1,3},{3,1},... | collective-permute-start | bytes 1966088 | tf_op jit(solution)/shard_map/ppermute | solution.py:395
  106.8 13.5 %collective-permute-start.16 = (bf16[2,128,3200]{2,1,0:T(8,128)(2,1)S(1)}, bf16[2,128,3200]{2,1,0:T(8,128)(2,1)S(1)}, u32[]{:S(2)}, u32[]{:S(2)}) collective-permute-start(bf16[2,128,3200]{2,1,0:T(8,128)(2,1)S(1)} %shard_map.141.refs_7_.refs_0_), channel_id=1, source_target_pairs={{0,1},{1,0},{2,3},{3,2},{4,5},{5,4},{6,7},{7,6},{8,9},{9,8},{10,11... | collective-permute-start | bytes 4915208 | tf_op jit(solution)/shard_map/ppermute | solution.py:417
  114.0 29.6 %collective-permute-start.13 = (bf16[2,128,3200]{2,1,0:T(8,128)(2,1)S(1)}, bf16[2,128,3200]{2,1,0:T(8,128)(2,1)S(1)}, u32[]{:S(2)}, u32[]{:S(2)}) collective-permute-start(bf16[2,128,3200]{2,1,0:T(8,128)(2,1)S(1)} %shard_map.142.refs_2_.refs_0_), channel_id=1, source_target_pairs={{0,1},{1,0},{2,3},{3,2},{4,5},{5,4},{6,7},{7,6},{8,9},{9,8},{10,11... | collective-permute-start | bytes 4915208 | tf_op jit(solution)/shard_map/ppermute | solution.py:419
  119.6 23.5 %collective-permute-start.15 = (bf16[256,128]{1,0:T(8,128)(2,1)S(1)}, bf16[256,128]{1,0:T(8,128)(2,1)S(1)}, u32[]{:S(2)}, u32[]{:S(2)}) collective-permute-start(bf16[256,128]{1,0:T(8,128)(2,1)S(1)} %get-tuple-element.48.refs_4_), channel_id=1, source_target_pairs={{0,4},{2,6},{4,0},{6,2},{8,12},{10,14},{12,8},{14,10},{1,5},{3,7},... | collective-permute-start | bytes 196616 | tf_op jit(solution)/shard_map/ppermute | solution.py:421
  141.9 40.2 %collective-permute-start.20 = (bf16[2,128,3200]{2,1,0:T(8,128)(2,1)S(1)}, bf16[2,128,3200]{2,1,0:T(8,128)(2,1)S(1)}, u32[]{:S(2)}, u32[]{:S(2)}) collective-permute-start(bf16[2,128,3200]{2,1,0:T(8,128)(2,1)S(1)} %shard_map.145.refs_2_.refs_0_), channel_id=1, source_target_pairs={{0,1},{1,0},{2,3},{3,2},{4,5},{5,4},{6,7},{7,6},{8,9},{9,8},{10,11... | collective-permute-start | bytes 4915208 | tf_op jit(solution)/shard_map/ppermute | solution.py:424
  162.4 40.4 %collective-permute-start.17 = (bf16[2,128,3200]{2,1,0:T(8,128)(2,1)S(1)}, bf16[2,128,3200]{2,1,0:T(8,128)(2,1)S(1)}, u32[]{:S(2)}, u32[]{:S(2)}) collective-permute-start(bf16[2,128,3200]{2,1,0:T(8,128)(2,1)S(1)} %shard_map.148.refs_2_.refs_0_), channel_id=1, source_target_pairs={{0,1},{1,0},{2,3},{3,2},{4,5},{5,4},{6,7},{7,6},{8,9},{9,8},{10,11... | collective-permute-start | bytes 4915208 | tf_op jit(solution)/shard_map/ppermute | solution.py:429
  162.5 15.9 %collective-permute-start.21 = (bf16[128,2560]{1,0:T(8,128)(2,1)S(1)}, bf16[128,2560]{1,0:T(8,128)(2,1)S(1)}, u32[]{:S(2)}, u32[]{:S(2)}) collective-permute-start(bf16[128,2560]{1,0:T(8,128)(2,1)S(1)} %get-tuple-element.49.refs_7_), channel_id=1, source_target_pairs={{0,2},{2,0},{4,6},{6,4},{8,10},{10,8},{12,14},{14,12},{1,3},{3,1},... | collective-permute-start | bytes 1966088 | tf_op jit(solution)/shard_map/ppermute | solution.py:412
  163.8 35.0 %collective-permute-start.19 = (bf16[128,2560]{1,0:T(8,128)(2,1)S(1)}, bf16[128,2560]{1,0:T(8,128)(2,1)S(1)}, u32[]{:S(2)}, u32[]{:S(2)}) collective-permute-start(bf16[128,2560]{1,0:T(8,128)(2,1)S(1)} %get-tuple-element.51.refs_7_), channel_id=1, source_target_pairs={{0,2},{2,0},{4,6},{6,4},{8,10},{10,8},{12,14},{14,12},{1,3},{3,1},... | collective-permute-start | bytes 1966088 | tf_op jit(solution)/shard_map/ppermute | solution.py:412
  164.1 38.2 %collective-permute-start.18 = (bf16[256,128]{1,0:T(8,128)(2,1)S(1)}, bf16[256,128]{1,0:T(8,128)(2,1)S(1)}, u32[]{:S(2)}, u32[]{:S(2)}) collective-permute-start(bf16[256,128]{1,0:T(8,128)(2,1)S(1)} %get-tuple-element.50.refs_4_), channel_id=1, source_target_pairs={{0,8},{2,10},{4,12},{6,14},{8,0},{10,2},{12,4},{14,6},{1,9},{3,11}... | collective-permute-start | bytes 196616 | tf_op jit(solution)/shard_map/ppermute | solution.py:426
  179.2 21.7 %collective-permute-start.24 = (bf16[128,2560]{1,0:T(8,128)(2,1)S(1)}, bf16[128,2560]{1,0:T(8,128)(2,1)S(1)}, u32[]{:S(2)}, u32[]{:S(2)}) collective-permute-start(bf16[128,2560]{1,0:T(8,128)(2,1)S(1)} %shard_map.149.refs_4_.refs_0_), channel_id=1, source_target_pairs={{0,4},{2,6},{12,8},{14,10},{1,5},{3,7},{13,9},{15,11},{16,20},{18,... | collective-permute-start | bytes 1966088 | tf_op jit(solution)/shard_map/ppermute | solution.py:431
  197.5 24.1 %collective-permute-start.23 = (bf16[128,2560]{1,0:T(8,128)(2,1)S(1)}, bf16[128,2560]{1,0:T(8,128)(2,1)S(1)}, u32[]{:S(2)}, u32[]{:S(2)}) collective-permute-start(bf16[128,2560]{1,0:T(8,128)(2,1)S(1)} %get-tuple-element.55.refs_2_), channel_id=1, source_target_pairs={{0,2},{2,0},{4,6},{6,4},{8,10},{10,8},{12,14},{14,12},{1,3},{3,1},... | collective-permute-start | bytes 1966088 | tf_op jit(solution)/shard_map/ppermute | solution.py:412
  199.5 19.1 %collective-permute-start.27 = (bf16[128,2560]{1,0:T(8,128)(2,1)S(1)}, bf16[128,2560]{1,0:T(8,128)(2,1)S(1)}, u32[]{:S(2)}, u32[]{:S(2)}) collective-permute-start(bf16[128,2560]{1,0:T(8,128)(2,1)S(1)} %shard_map.151.refs_2_.refs_5_.refs_0_), channel_id=1, source_target_pairs={{0,4},{2,6},{12,8},{14,10},{1,5},{3,7},{13,9},{15,11},{16,20},{18,... | collective-permute-start | bytes 1966088 | tf_op jit(solution)/shard_map/ppermute | solution.py:434
  201.6 20.1 %collective-permute-start.25 = (bf16[128,2560]{1,0:T(8,128)(2,1)S(1)}, bf16[128,2560]{1,0:T(8,128)(2,1)S(1)}, u32[]{:S(2)}, u32[]{:S(2)}) collective-permute-start(bf16[128,2560]{1,0:T(8,128)(2,1)S(1)} %shard_map.154), channel_id=1, source_target_pairs={{4,8},{6,10},{8,4},{10,6},{5,9},{7,11},{9,5},{11,7},{20,24},{22,26... | collective-permute-start | bytes 1966088 | tf_op jit(solution)/shard_map/ppermute | solution.py:435
  218.4 22.0 %collective-permute-start.22 = (bf16[128,2560]{1,0:T(8,128)(2,1)S(1)}, bf16[128,2560]{1,0:T(8,128)(2,1)}, u32[]{:S(2)}, u32[]{:S(2)}) collective-permute-start(bf16[128,2560]{1,0:T(8,128)(2,1)S(1)} %get-tuple-element.57.refs_3_.refs_2_), channel_id=1, source_target_pairs={{0,2},{2,0},{4,6},{6,4},{8,10},{10,8},{12,14},{14,12},{1,3},{3,1},... | collective-permute-start | bytes 1966088 | tf_op jit(solution)/shard_map/ppermute | solution.py:412
  220.2 20.2 %collective-permute-start.28 = (bf16[128,2560]{1,0:T(8,128)(2,1)}, bf16[128,2560]{1,0:T(8,128)(2,1)}, u32[]{:S(2)}, u32[]{:S(2)}) collective-permute-start(bf16[128,2560]{1,0:T(8,128)(2,1)} %shard_map.156), channel_id=1, source_target_pairs={{4,8},{6,10},{8,4},{10,6},{5,9},{7,11},{9,5},{11,7},{20,24},{22,26... | collective-permute-start | bytes 1966088 | tf_op jit(solution)/shard_map/ppermute | solution.py:438
  223.3 17.0 %collective-permute-start.26 = (bf16[128,2560]{1,0:T(8,128)(2,1)}, bf16[128,2560]{1,0:T(8,128)(2,1)}, u32[]{:S(2)}, u32[]{:S(2)}) collective-permute-start(bf16[128,2560]{1,0:T(8,128)(2,1)} %shard_map.155), channel_id=1, source_target_pairs={{0,4},{2,6},{4,0},{6,2},{8,12},{10,14},{12,8},{14,10},{1,5},{3,7},... | collective-permute-start | bytes 1966088 | tf_op jit(solution)/shard_map/ppermute | solution.py:439
  (26 other events, 176.3 us)

commit v2 on v1

--- a/solution.py
+++ b/solution.py
@@ -19,12 +19,13 @@
 Y_SWAP = [(t, t ^ 1) for t in range(8)]
 PAIR = [(t, t ^ 2) for t in range(8)]
 FAR = [(t, t ^ 4) for t in range(8)]
+ACROSS = [(t, t ^ 6) for t in range(8)]
 MID = [(2, 4), (3, 5), (4, 2), (5, 3)]
 OUTWARD = [(2, 0), (3, 1), (4, 6), (5, 7)]
 INWARD = [(0, 2), (1, 3), (6, 4), (7, 5)]
 CORES = [(0, 1), (1, 0)]
 
-M_T, M_Y, M_D, M_Z, M_SLOT_ADAPTER, M_ADAPTER, M_GRAD_SLOT = 0, 1, 2, 3, 7, 11, 15
+M_T, M_Y, M_D, M_Z, M_SLOT_ADAPTER, M_ADAPTER, M_GRAD_SLOT, M_SLAB = 0, 1, 2, 3, 7, 11, 15, 19
 
 
 def nt_dot(a, b):
@@ -36,7 +37,7 @@
 
 
 def call(
-    kernel, meta, args, grid, in_specs, out_specs, out_shape, scratch=(), flops=0, nbytes=0, vmem=48, after=()
+    kernel, meta, args, grid, in_specs, out_specs, out_shape, scratch=(), vmem=48, after=(), cost=(1000, 1000)
 ):
     first, extra = len(args), len(after)
 
@@ -54,7 +55,7 @@
         ),
         out_shape=out_shape,
         compiler_params=pltpu.CompilerParams(vmem_limit_bytes=vmem * MIB),
-        cost_estimate=pl.CostEstimate(flops=flops, bytes_accessed=nbytes, transcendentals=0),
+        cost_estimate=pl.CostEstimate(flops=cost[0], bytes_accessed=cost[1], transcendentals=0),
     )(meta, *args, *after)
 
 
@@ -75,7 +76,7 @@
     low_ref[...] = pack_halves(nt_dot(hidden, a_ref[0]))
 
 
-def hidden_and_low_in(meta, gate_act, up_act, a_t):
+def hidden_and_low_in(meta, gate_act, up_act, a_t, after):
     rows, width = gate_act.shape
     rank = a_t.shape[1]
     blocks = rows // BLOCK
@@ -97,129 +98,168 @@
             jax.ShapeDtypeStruct((rows, width), BF16),
             jax.ShapeDtypeStruct((rows // 2, 2 * rank), F32),
         ],
-        flops=2 * rows * width * rank * 2,
-        nbytes=8 * rows * width,
-    )
-
-
-def low_out_kernel(m, *refs):
-    shards, b_ref, cols_ref, low_ref = refs[:8], refs[8], refs[9], refs[10]
-    rows = shards[0].shape[0]
+        after=after,
+    )
+
+
+def slabs_kernel(m, *refs):
+    for i in range(4):
+        refs[4 + i][...] = refs[i][0]
+
+
+def slabs(meta, b):
+    rank, columns = b.shape[1:]
+
+    def spec(k):
+        return pl.BlockSpec((1, rank, columns), lambda i, m: (m[M_SLAB + k], 0, 0))
+
+    return call(
+        slabs_kernel,
+        meta,
+        (b,) * 4,
+        (1,),
+        [spec(k) for k in range(4)],
+        [pl.BlockSpec((rank, columns), lambda i, m: (0, 0))] * 4,
+        [jax.ShapeDtypeStruct((rank, columns), BF16)] * 4,
+    )
+
+
+def low_out_kernel(m, own_ref, other_ref, s0, s1, s2, s3, low_in_ref, full_ref, short_ref):
+    rows = own_ref.shape[0]
+    rank, columns = s0.shape
+    y, z = m[M_Y], m[M_Z]
+    total = jnp.zeros((2 * rows, rank), F32)
+    for k, slab in enumerate((s0, s1, s2, s3)):
+        at = pl.ds(pl.multiple_of((jnp.bitwise_xor(z, k) * 2 + y) * columns, 128), columns)
+        tokens = jnp.concatenate([own_ref[:, at], other_ref[:, at]], axis=0)
+        total += nt_dot(tokens, slab[...])
+    own, other = total[:rows], total[rows:]
+    packed = jnp.concatenate(
+        [jnp.where(y == 0, own, other), jnp.where(y == 0, other, own)], axis=1
+    )
+    at = pl.ds(pl.multiple_of(z * rows, rows), rows)
+    for ref in (full_ref, short_ref):
+        ref[: 4 * rows] = jnp.zeros((4 * rows, 2 * rank), ref.dtype)
+        ref[4 * rows :] = low_in_ref[...].astype(ref.dtype)
+        ref[at, :] = packed.astype(ref.dtype)
+
+
+def low_parts(meta, own, other, pieces, low_in, after):
+    rows, full = own.shape
+    rank, columns = pieces[0].shape
+    out = (8 * rows, 2 * rank)
+    return call(
+        low_out_kernel,
+        meta,
+        (own, other, *pieces, low_in),
+        (1,),
+        [pl.BlockSpec((rows, full), lambda i, m: (0, 0))] * 2
+        + [pl.BlockSpec((rank, columns), lambda i, m: (0, 0))] * 4
+        + [pl.BlockSpec((4 * rows, 2 * rank), lambda i, m: (0, 0))],
+        [pl.BlockSpec(out, lambda i, m: (0, 0))] * 2,
+        [jax.ShapeDtypeStruct(out, F32), jax.ShapeDtypeStruct(out, BF16)],
+        after=after,
+    )
+
+
+def columns_kernel(m, *refs):
+    cols_ref = refs[8]
+    rows = refs[0].shape[0]
     y = m[M_Y]
     for s in range(4):
         z = m[M_Z + s]
-        own, other = shards[2 * s][...], shards[2 * s + 1][...]
+        own, other = refs[2 * s][...], refs[2 * s + 1][...]
         first = jnp.where(y == 0, own, other)
         second = jnp.where(y == 0, other, own)
         tokens = jnp.concatenate([first, second], axis=0)
         cols_ref[pl.ds(pl.multiple_of(z * 2 * rows, 2 * rows), 2 * rows), :] = tokens
-        part = nt_dot(tokens, b_ref[m[M_SLOT_ADAPTER + s]])
-        low_ref[pl.ds(pl.multiple_of(z * rows, rows), rows), :] = pack_halves(part)
-
-
-def low_out_parts(meta, shards, b, after):
+
+
+def own_columns(meta, shards, columns, after):
     rows = shards[0].shape[0]
-    adapters, rank, columns = b.shape
-    return call(
-        low_out_kernel,
-        meta,
-        (*shards, b),
+    return call(
+        columns_kernel,
+        meta,
+        shards,
         (1,),
-        [pl.BlockSpec((rows, columns), lambda i, m: (0, m[M_T]))] * 8
-        + [pl.BlockSpec((adapters, rank, columns), lambda i, m: (0, 0, 0))],
-        [
-            pl.BlockSpec((8 * rows, columns), lambda i, m: (0, 0)),
-            pl.BlockSpec((4 * rows, 2 * rank), lambda i, m: (0, 0)),
-        ],
-        [
-            jax.ShapeDtypeStruct((8 * rows, columns), BF16),
-            jax.ShapeDtypeStruct((4 * rows, 2 * rank), F32),
-        ],
-        flops=2 * 8 * rows * columns * rank,
-        nbytes=4 * 8 * rows * columns,
-        after=after,
-    )
-
-
-def hidden_grad_kernel(count, m, *refs):
-    mine, other = refs[:count], refs[count : 2 * count]
-    down_mine, down_other, out_ref, lhs = refs[2 * count :]
+        [pl.BlockSpec((rows, columns), lambda i, m: (0, m[M_T]))] * 8,
+        pl.BlockSpec((8 * rows, columns), lambda i, m: (0, 0)),
+        jax.ShapeDtypeStruct((8 * rows, columns), BF16),
+        after=after,
+    )
+
+
+def act_grad_kernel(m, *refs):
+    mine, other, gates, ups = refs[:4], refs[4:8], refs[8:12], refs[12:16]
+    lows, factors = refs[16:18], refs[18:20]
+    down_mine, down_other = refs[20:22]
+    outs, lhs = refs[22:24], refs[24]
     rows = mine[0].shape[0]
+    rank = factors[0].shape[1]
+    y = m[M_Y]
 
     @pl.when(pl.program_id(0) == 0)
     def _():
-        for s in range(count):
+        for s in range(4):
             lhs[0, s * rows : (s + 1) * rows] = mine[s][...]
             lhs[1, s * rows : (s + 1) * rows] = other[s][...]
 
     total = jnp.dot(lhs[0], down_mine[...], preferred_element_type=F32)
-    out_ref[...] = total + jnp.dot(lhs[1], down_other[...], preferred_element_type=F32)
-
-
-def hidden_grad(meta, shards, mine, other, span, after=()):
+    total += jnp.dot(lhs[1], down_other[...], preferred_element_type=F32)
+    for i in range(2):
+        first, second = lows[i][:, :rank], lows[i][:, rank:]
+        low = jnp.concatenate(
+            [jnp.where(y == 0, first, second), jnp.where(y == 0, second, first)], axis=0
+        )
+        term = jnp.dot(low, factors[i][0], preferred_element_type=F32)
+        for j in range(2):
+            at = slice(j * rows, (j + 1) * rows)
+            hg = total[(2 * i + j) * rows : (2 * i + j + 1) * rows] + ADAPTER_SCALE * term[at]
+            g = gates[2 * i + j][...].astype(F32)
+            u = ups[2 * i + j][...].astype(F32)
+            sig = jax.nn.sigmoid(g)
+            outs[i][0, at] = (hg * u * sig * (1.0 + g * (1.0 - sig))).astype(BF16)
+            outs[i][1, at] = (hg * (g * sig)).astype(BF16)
+
+
+def act_grads(meta, slots, shards, gate_act, up_act, low, a_t, down, after=()):
     rows = shards[0].shape[0]
-    half = mine.shape[0]
-    start, width, step = span
-    count = len(shards)
-    total = rows * count
-    return call(
-        functools.partial(hidden_grad_kernel, count),
-        meta,
-        (*shards, *shards, mine, other),
+    rank = a_t.shape[1]
+    half, width = down.shape[0] // 2, down.shape[1]
+    step = width // 5
+
+    def act_spec(slot, j):
+        def index(n, m):
+            y = m[M_Y]
+            return (m[M_Z + slot] * 2 + (1 - y if j else y), n)
+
+        return pl.BlockSpec((rows, step), index)
+
+    def low_spec(slot):
+        return pl.BlockSpec((rows, 2 * rank), lambda n, m: (m[M_Z + slot], 0))
+
+    def factor_spec(slot):
+        return pl.BlockSpec((1, rank, step), lambda n, m: (m[M_SLOT_ADAPTER + slot], 0, n))
+
+    acts = [act_spec(slot, j) for slot in slots for j in range(2)]
+    return call(
+        act_grad_kernel,
+        meta,
+        (*shards, *shards, *[gate_act] * 4, *[up_act] * 4, low, low, a_t, a_t, down, down),
         (width // step,),
-        [pl.BlockSpec((rows, half), lambda n, m: (0, m[M_D]))] * count
-        + [pl.BlockSpec((rows, half), lambda n, m: (0, 1 - m[M_D]))] * count
-        + [pl.BlockSpec((half, step), lambda n, m: (0, n + start // step))] * 2,
-        pl.BlockSpec((total, step), lambda n, m: (0, n)),
-        jax.ShapeDtypeStruct((total, width), F32),
-        scratch=[pltpu.VMEM((2, total, half), BF16)],
-        flops=2 * total * 2 * half * width,
-        nbytes=2 * 2 * half * width,
-        after=after,
-    )
-
-
-def act_grad_kernel(spans, m, *refs):
-    hg_refs, (gate_ref, up_ref, low_ref, a_ref, out_ref) = refs[: len(spans)], refs[len(spans) :]
-    j = pl.program_id(0)
-    y = m[M_Y]
-    rank = low_ref.shape[1] // 2
-    second = jnp.where(j == 0, y, 1 - y) == 1
-    low = jnp.where(second, low_ref[:, rank:], low_ref[:, :rank])
-    for hg_ref, (start, width, _) in zip(hg_refs, spans):
-        at = slice(start, start + width)
-        hg = hg_ref[...] + ADAPTER_SCALE * jnp.dot(low, a_ref[0, :, at], preferred_element_type=F32)
-        g = gate_ref[:, at].astype(F32)
-        u = up_ref[:, at].astype(F32)
-        sig = jax.nn.sigmoid(g)
-        out_ref[0, :, at] = (hg * u * sig * (1.0 + g * (1.0 - sig))).astype(BF16)
-        out_ref[1, :, at] = (hg * (g * sig)).astype(BF16)
-
-
-def act_grad(meta, slot, spans, hgs, gate_act, up_act, low, a_t, after=()):
-    rank, width = a_t.shape[1:]
-    rows = BLOCK // 2
-
-    def shard_of(j, m):
-        y = m[M_Y]
-        return (m[M_Z + slot] * 2 + y + j * (1 - 2 * y), 0)
-
-    return call(
-        functools.partial(act_grad_kernel, spans),
-        meta,
-        (*hgs, gate_act, up_act, low, a_t),
-        (2,),
-        [pl.BlockSpec((rows, w), lambda j, m: ((slot % 2) * 2 + j, 0)) for _, w, _ in spans]
+        [pl.BlockSpec((rows, half), lambda n, m: (0, m[M_D]))] * 4
+        + [pl.BlockSpec((rows, half), lambda n, m: (0, 1 - m[M_D]))] * 4
+        + acts
+        + acts
+        + [low_spec(slot) for slot in slots]
+        + [factor_spec(slot) for slot in slots]
         + [
-            pl.BlockSpec((rows, width), shard_of),
-            pl.BlockSpec((rows, width), shard_of),
-            pl.BlockSpec((rows, 2 * rank), lambda j, m: (m[M_Z + slot], 0)),
-            pl.BlockSpec((1, rank, width), lambda j, m: (m[M_SLOT_ADAPTER + slot], 0, 0)),
+            pl.BlockSpec((half, step), lambda n, m: (m[M_D], n)),
+            pl.BlockSpec((half, step), lambda n, m: (1 - m[M_D], n)),
         ],
-        pl.BlockSpec((2, rows, width), lambda j, m: (0, j, 0)),
-        jax.ShapeDtypeStruct((2, 2 * rows, width), BF16),
-        flops=2 * 2 * rows * width * rank,
-        nbytes=2 * rows * width * 12,
+        [pl.BlockSpec((2, 2 * rows, step), lambda n, m: (0, 0, n))] * 2,
+        [jax.ShapeDtypeStruct((2, 2 * rows, width), BF16)] * 2,
+        scratch=[pltpu.VMEM((2, 4 * rows, half), BF16)],
         after=after,
     )
 
@@ -254,8 +294,6 @@
         [pl.BlockSpec((rows, step), lambda n, m: (0, n))] * 2,
         [out, out],
         scratch=[pltpu.VMEM((2, 2 * rows, width), BF16)],
-        flops=2 * 2 * rows * 2 * width * half,
-        nbytes=2 * 2 * width * half,
         after=after,
     )
 
@@ -275,9 +313,9 @@
         ref[0] = total.astype(BF16)
 
 
-def owner_grads(meta, low, features, owned, after=()):
+def owner_grads(meta, low, which, features, owned, after=()):
     tokens, width = features.shape
-    half_rows, double = low.shape
+    half_rows, double = low.shape[0] // 2, low.shape[1]
     rank = double // 2
     out = jax.ShapeDtypeStruct((owned, rank, width), BF16)
     return call(
@@ -286,13 +324,11 @@
         (low, features),
         (owned,),
         [
-            pl.BlockSpec((half_rows, double), lambda i, m: (0, 0)),
+            pl.BlockSpec((half_rows, double), lambda i, m: (which, 0)),
             pl.BlockSpec((tokens, width), lambda i, m: (0, 0)),
         ],
         [pl.BlockSpec((1, rank, width), lambda i, m: (i, 0, 0))] * 2,
         [out, out],
-        flops=2 * tokens * rank * width * 2 * owned,
-        nbytes=2 * tokens * width,
         after=after,
     )
 
@@ -316,11 +352,34 @@
         [spec] * len(xs),
         [spec] * len(kinds),
         [jax.ShapeDtypeStruct((rows, width), k) for k in kinds],
-        nbytes=2 * rows * width * (len(xs) + 1),
         vmem=16,
         after=after,
     )
     return out if len(kinds) > 1 else out[0]
+
+
+def final_kernel(m, *refs):
+    total = refs[0][...].astype(F32)
+    for r in refs[1:-2]:
+        total += r[...].astype(F32)
+    rows = refs[-1].shape[0]
+    refs[-2][...] = total[:rows].astype(BF16)
+    refs[-1][...] = total[rows:].astype(BF16)
+
+
+def final_sum(meta, xs, after):
+    rows, width = xs[0].shape
+    return call(
+        final_kernel,
+        meta,
+        xs,
+        (1,),
+        [pl.BlockSpec((rows, width), lambda i, m: (0, 0))] * len(xs),
+        [pl.BlockSpec((rows // 2, width), lambda i, m: (0, 0))] * 2,
+        [jax.ShapeDtypeStruct((rows // 2, width), BF16)] * 2,
+        vmem=16,
+        after=after,
+    )
 
 
 def add(*xs):
@@ -365,6 +424,7 @@
             pick(block_adapter, slots_z),
             block_adapter,
             pick(adapter_grad_slot, block_adapter),
+            pick(block_adapter, jnp.stack([z, z ^ 1, z ^ 2, z ^ 3])),
         ]
     ).astype(jnp.int32)
     a_t = jnp.swapaxes(adapter_input_factor, 1, 2)
@@ -372,83 +432,70 @@
     swap_cores = functools.partial(lax.ppermute, axis_name="dp", perm=CORES)
     at_end = (z == 0) | (z == 3)
 
-    width = gate_act.shape[1]
-    step = width * 2 // 5
-    spans = ((0, step, step // 5), (step, step, step // 5), (2 * step, width - 2 * step, width - 2 * step))
-
-    down_other = swap_cores(down_matrix)
+    down = lax.all_gather(down_matrix, "dp", axis=0, tiled=True)
     pair = send(cotangent, perm=PAIR)
     mid = send(cotangent, perm=MID)
     y0 = send(cotangent, perm=Y_SWAP)
-    hidden, low_in = hidden_and_low_in(meta, gate_act, up_act, a_t)
-    y1 = send(tied(pair, y0, low_in), perm=Y_SWAP)
+    slab, *others = slabs(meta, adapter_output_factor)
+    pieces = [send(s, perm=p) for s, p in zip(others, (PAIR, FAR, ACROSS))]
+    hidden, low_in = hidden_and_low_in(meta, gate_act, up_act, a_t, tuple(others))
+    y1 = send(tied(pair, y0, low_in, *pieces), perm=Y_SWAP)
     pair_mid = send(tied(pair, low_in), perm=MID)
     mid_out = send(tied(mid, low_in), perm=OUTWARD)
+    low_sum, low = low_parts(meta, cotangent, y0, [slab] + pieces, low_in, ())
+    low_sum, low = add_after(meta, (low_sum, send(low, perm=Y_SWAP)), (), (F32, BF16))
     slot2 = jnp.where(at_end, mid_out, mid)
-    y2 = send(tied(slot2, y1), perm=Y_SWAP)
+    y2 = send(tied(slot2, y1, low), perm=Y_SWAP)
+    low = tied(low, y1)
+    low_sum, low = add_after(meta, (low_sum, send(low, perm=PAIR)), (), (F32, BF16))
     far_out = send(pair_mid, perm=OUTWARD)
-    hg_near, last = [], (low_in,)
-    for span in spans:
-        hg_near.append(hidden_grad(meta, (cotangent, y0, pair, y1), down_matrix, down_other, span, last))
-        last = (hg_near[-1],)
-    slot3 = jnp.where(at_end, tied(far_out, hg_near[0]), pair_mid)
-    y3 = send(tied(slot3, y2), perm=Y_SWAP)
-
-    far = (slot2, y2, slot3, y3)
-    columns, low_part = low_out_parts(meta, (cotangent, y0, pair, y1, *far), adapter_output_factor, last)
-    hg_far = []
-    low_sum, low_out = low_part, low_part.astype(BF16)
-    for perm, span in zip((Y_SWAP, PAIR, FAR), spans):
-        got = send(low_out, perm=perm)
-        hg_far.append(hidden_grad(meta, far, down_matrix, down_other, span, (low_out,)))
-        low_sum, low_out = add_after(meta, (low_sum, got), (hg_far[-1],), (F32, BF16))
-
-    def grads(slot, after):
-        hgs = hg_far if slot >= 2 else hg_near
-        return act_grad(meta, slot, spans, hgs, gate_act, up_act, low_out, a_t, after)
+    slot3 = tied(jnp.where(at_end, tied(far_out, low), pair_mid), y2)
+    y3 = send(slot3, perm=Y_SWAP)
+    low = tied(low, y2)
+    low_sum, low = add_after(meta, (low_sum, send(low, perm=FAR)), (), (F32, BF16))
+    near, far = (cotangent, y0, pair, y1), (slot2, y2, slot3, y3)
+    rest = (gate_act, up_act, low, a_t, down)
+    mine0, mine1 = act_grads(meta, (0, 1), near, *rest, (slot3,))
+    mine2, mine3 = act_grads(meta, (2, 3), far, *rest, (mine0,))
+    other3 = swap_cores(mine3)
+    other2 = swap_cores(tied(mine2, other3))
+    other1 = swap_cores(tied(mine1, other2))
+    other0 = swap_cores(tied(mine0, other1))
 
     def parts(mine, other, after):
         keep, give = input_grad_parts(meta, mine, other, gate_matrix, up_matrix, after)
         return keep, send(give, perm=Y_SWAP), give
 
-    mine3 = grads(3, ())
-    low_in1 = low_in.astype(BF16)
-    got_in = send(low_in1, perm=Y_SWAP)
-    other3 = swap_cores(mine3)
-    mine2 = grads(2, (mine3,))
-    other2 = swap_cores(mine2)
-    low_in2, low_in2b = add_after(meta, (low_in, got_in), (mine2,), (F32, BF16))
-    got_in = send(low_in2b, perm=PAIR)
-    keep3, got3, give3 = parts(mine3, other3, (low_in2b,))
-    mine1 = grads(1, (give3,))
-    other1 = swap_cores(mine1)
-    low_in3, low_in3b = add_after(meta, (low_in2, got_in), (mine1,), (F32, BF16))
-    got_in = send(low_in3b, perm=FAR)
-    keep2, got2, give2 = parts(mine2, other2, (low_in3b,))
-    mine0 = grads(0, (give2,))
-    other0 = swap_cores(mine0)
-    sum3 = add_after(meta, (keep3, got3), (mine0,))
+    keep3, got3, give3 = parts(mine3, other3, (mine2,))
+    keep2, got2, give2 = parts(mine2, other2, (give3,))
+    sum3 = add_after(meta, (keep3, got3), (give2,))
     far_in = send(sum3, perm=INWARD)
     keep1, got1, give1 = parts(mine1, other1, (sum3,))
     sum2 = add_after(meta, (keep2, got2), (give1,))
     mid_in = send(sum2, perm=INWARD)
-    far_mid = send(add_after(meta, (sum3, far_in), (sum2,)), perm=MID)
-    low_in4 = add_after(meta, (low_in3, got_in), (sum2,))
-    keep0, got0, give0 = parts(mine0, other0, (low_in4, sum2))
-    from_mid = send(add_after(meta, (sum2, mid_in), (give0,)), perm=MID)
-    from_pair = send(add_after(meta, (keep1, got1, far_mid), (give0,)), perm=PAIR)
+    sum3 = add_after(meta, (sum3, far_in), (sum2,))
+    far_mid = send(sum3, perm=MID)
+    keep0, got0, give0 = parts(mine0, other0, (sum3,))
+    sum1 = add_after(meta, (keep1, got1, far_mid), (give0,))
+    from_pair = send(sum1, perm=PAIR)
+    sum2 = add_after(meta, (sum2, mid_in), (sum1,))
+    from_mid = send(sum2, perm=MID)
     owned = adapters // 2
-    keep_a, give_a = owner_grads(meta, low_out, hidden, owned, (give0,))
-    keep_b, give_b = owner_grads(meta, low_in4, columns, owned, (keep_a,))
-    grad_a = jnp.swapaxes(add(keep_a, swap_cores(give_a)), 1, 2)
+    keep_a, give_a = owner_grads(meta, low, 0, hidden, owned, (sum2,))
+    columns = own_columns(meta, near + far, adapter_output_factor.shape[2], (keep_a,))
+    keep_b, give_b = owner_grads(meta, low, 1, columns, owned)
+    own, give = final_sum(meta, (keep0, got0, from_pair, from_mid), (keep_b,))
     grad_b = add(keep_b, swap_cores(give_b))
-    final = add_after(meta, (keep0, got0, from_pair, from_mid), (keep_b,))
-    own_rows = cotangent.shape[0]
-    got = swap_cores(final[own_rows:])
-    own = final[:own_rows]
+    shape = keep_a.shape
+    flat = (shape[0] * shape[1], shape[2])
+    grad_a = add_after(
+        meta, (keep_a.reshape(flat), swap_cores(give_a).reshape(flat)), (give,), steps=2
+    )
+    got = swap_cores(give)
     input_grad = jnp.where(
         d == 0, jnp.concatenate([own, got], axis=1), jnp.concatenate([got, own], axis=1)
     )
+    grad_a = jnp.swapaxes(grad_a.reshape(shape), 1, 2)
     return (input_grad, grad_a, grad_b)
 
 

time: 250 us -> 251 us (level)
  Pallas kernels: 149 us -> 130 us
  between operations: 1.16 us -> 14.5 us
  waiting for transfers between devices: 38.6 us -> 45.3 us
  other arithmetic: 7.55 us -> 3.64 us
  local copies, waits for them, and re-layouts: 10.7 us -> 14.4 us
    ppermute x18 -> x17, waiting for transfers between devices: 3.83 us -> 28.6 us  [the longest x1 11 us: grid_body(): send(low, perm=Y_SWAP)]
    pallas_call x30 -> x22, Pallas kernels: 149 us -> 130 us  [call(): pl.pallas_call(run, grid_spec=pltpu.PrefetchScalarGridSpec(num_scalar_pre...]
    ppermute x1, waiting for transfers between devices: 14.4 us -> 0.01 us  [grid_body(): mid_out = send(tied(mid, low_in), perm=OUTWARD)]
    ppermute x4, waiting for transfers between devices: 13.9 us -> 0.01 us  [parts(): return (keep, send(give, perm=Y_SWAP), give)]
    ppermute x1, waiting for transfers between devices: 3.12 us -> 12.9 us  [grid_body(): far_out = send(pair_mid, perm=OUTWARD)]
    unnamed x36 -> x44, local copies, waits for them, and re-layouts: 9.88 us -> 14.2 us
    ppermute x1, waiting for transfers between devices: 0.01 us -> 3.13 us  [grid_body(): other3 = swap_cores(mine3)]
    transpose x1 -> x0, other arithmetic: 2.6 us -> none  [grid_body(): grad_a = jnp.swapaxes(add(keep_a, swap_cores(give_a)), 1, 2)]
  transfers between devices with their start and end apart: 32 -> 32, of which waited for: 7 -> 8; matrix products, arithmetic and copies ran while one was open for 3% -> 2% of each run, Pallas kernels for 57% -> 43%
where the time goes in v2:
time: 251 us; the launch traced here: 250 us
  Pallas kernels  130 us (52%)
  waiting for transfers between devices  45.3 us (18%)
  starting transfers between devices  41.8 us (17%)
  between operations  14.5 us (6%)
  local copies, waits for them, and re-layouts  14.4 us (6%)
  other arithmetic  3.64 us (1%)
    pallas_call x22, Pallas kernels, call(): pl.pallas_call(run, grid_spec=pltpu.PrefetchScalarGridSpec(num_scalar_pre...  130 us
    unnamed x44, local copies, waits for them, and re-layouts  14.2 us
    ppermute x1, waiting for transfers between devices, grid_body(): far_out = send(pair_mid, perm=OUTWARD)  12.9 us
    ppermute x1, waiting for transfers between devices, grid_body(): send(low, perm=Y_SWAP)  11 us
    ppermute x3, waiting for transfers between devices, grid_body(): pieces = [send(s, perm=p) for s, p in zip(others, (PAIR, FAR, ACROSS))]  8.02 us
    ppermute x3, starting transfers between devices, grid_body(): pieces = [send(s, perm=p) for s, p in zip(others, (PAIR, FAR, ACROSS))]  6.24 us
    ppermute x1, waiting for transfers between devices, grid_body(): send(low, perm=FAR)  5.35 us
  transfers between devices with their start and end apart: 32, of which 8 were waited for; matrix products, arithmetic and copies ran while one was open for 2% of the time, Pallas kernels for 43%

profile of v2, /device:TPU:1, one launch (start us, length us, event | category | flops | bytes accessed | tf_op | source)
XLA Modules:
  0.0 250.1 jit_solution(18236480102062607202)
XLA Ops:
  8.3 2.1 collective-permute-start.1
  15.6 3.1 %collective-permute-start.2 = (bf16[64,640]{1,0:T(8,128)(2,1)S(1)}, bf16[64,640]{1,0:T(8,128)(2,1)S(1)}, u32[]{:S(2)}, u32[]{:S(2)}) collective-permute-start(bf16[64,640]{1,0:T(8,128)(2,1)S(1)} %get-tuple-element.45.refs_3_), channel_id=1, source_target_pairs={{0,4},{2,6},{4,0},{6,2},{8,12},{10,14},{12,8},{14,10},{1,5},{3,7},... | collective-permute-start | bytes 245768 | tf_op jit(solution)/shard_map/ppermute | solution.py:440
  18.7 8.0 %collective-permute-done.2.refs_3_ = bf16[64,640]{1,0:T(8,128)(2,1)S(1)} collective-permute-done((bf16[64,640]{1,0:T(8,128)(2,1)S(1)}, bf16[64,640]{1,0:T(8,128)(2,1)S(1)}, u32[]{:S(2)}, u32[]{:S(2)}) %collective-permute-start.2) | collective-permute-done | bytes 81952 | tf_op jit(solution)/shard_map/ppermute | solution.py:440
  26.7 3.2 %collective-permute-start.4 = (bf16[64,640]{1,0:T(8,128)(2,1)S(1)}, bf16[64,640]{1,0:T(8,128)(2,1)S(1)}, u32[]{:S(2)}, u32[]{:S(2)}) collective-permute-start(bf16[64,640]{1,0:T(8,128)(2,1)S(1)} %get-tuple-element.47.refs_5_), channel_id=1, source_target_pairs={{0,12},{2,14},{4,8},{6,10},{8,4},{10,6},{12,0},{14,2},{1,13},{3,15... | collective-permute-start | bytes 245768 | tf_op jit(solution)/shard_map/ppermute | solution.py:440
  29.9 6.7 %shard_map.131 = (bf16[512,3200]{1,0:T(8,128)(2,1)S(1)}, f32[256,128]{1,0:T(8,128)S(1)}) custom-call(s32[23]{0:T(128)S(1)} %concatenate.10.m, bf16[512,3200]{1,0:T(8,128)(2,1)} %refs_11_.3, bf16[512,3200]{1,0:T(8,128)(2,1)} %refs_15_.3, bf16[6,64,3200]{2,1,0:T(8,128)(2,1)S(1)} %bitcast.20, bf16[64,640]{1,0:T(8,128)(2,1)S(1)} %get-tuple-element.45.refs_3_, ...), custom_call_target="tpu_custom_call" | custom-call | flops 1000 | bytes 1000 | tf_op jit(solution)/shard_map/pallas_call | solution.py:47
  42.4 2.2 shard_map.132
  45.0 11.0 %collective-permute-done.6.refs_1_ = bf16[512,128]{1,0:T(8,128)(2,1)S(1)} collective-permute-done((bf16[512,128]{1,0:T(8,128)(2,1)S(1)}, bf16[512,128]{1,0:T(8,128)(2,1)S(1)}, u32[]{:S(2)}, u32[]{:S(2)}) %collective-permute-start.6) | collective-permute-done | bytes 131104 | tf_op jit(solution)/shard_map/ppermute | solution.py:446
  61.7 12.9 %collective-permute-done.13 = bf16[64,5120]{1,0:T(8,128)(2,1)S(1)} collective-permute-done((bf16[64,5120]{1,0:T(8,128)(2,1)}, bf16[64,5120]{1,0:T(8,128)(2,1)S(1)}, u32[]{:S(2)}, u32[]{:S(2)}) %collective-permute-start.13) | collective-permute-done | bytes 655392 | tf_op jit(solution)/shard_map/ppermute | solution.py:451
  77.4 5.3 %collective-permute-done.11.refs_1_ = bf16[512,128]{1,0:T(8,128)(2,1)S(1)} collective-permute-done((bf16[512,128]{1,0:T(8,128)(2,1)S(1)}, bf16[512,128]{1,0:T(8,128)(2,1)S(1)}, u32[]{:S(2)}, u32[]{:S(2)}) %collective-permute-start.11) | collective-permute-done | bytes 131104 | tf_op jit(solution)/shard_map/ppermute | solution.py:455
  84.1 19.6 %shard_map.136 = (bf16[2,128,3200]{2,1,0:T(8,128)(2,1)S(1)}, bf16[2,128,3200]{2,1,0:T(8,128)(2,1)}) custom-call(s32[23]{0:T(128)S(1)} %concatenate.10.m, bf16[64,5120]{1,0:T(8,128)(2,1)S(1)} %copy-done.1, bf16[64,5120]{1,0:T(8,128)(2,1)} %collective-permute-done.refs_1_.refs_5_, bf16[64,5120]{1,0:T(8,128)(2,1)} %collective-permute-done.1.refs_2_.refs_6_, ...), custom_call_target="tpu_custom_call" | custom-call | flops 1000 | bytes 1000 | tf_op jit(solution)/shard_map/pallas_call | solution.py:47
  104.9 19.0 %shard_map.137 = (bf16[2,128,3200]{2,1,0:T(8,128)(2,1)S(1)}, bf16[2,128,3200]{2,1,0:T(8,128)(2,1)S(1)}) custom-call(s32[23]{0:T(128)S(1)} %concatenate.10.m, bf16[64,5120]{1,0:T(8,128)(2,1)S(1)} %broadcast_select_fusion.1.refs_0_.refs_4_, bf16[64,5120]{1,0:T(8,128)(2,1)S(1)} %copy-done.8, bf16[64,5120]{1,0:T(8,128)(2,1)S(1)} %broadcast_select_fusion.refs_22_.refs_2_.refs_6_, ...), custom_call_target="tpu_custom_call" | custom-call | flops 1000 | bytes 1000 | tf_op jit(solution)/shard_map/pallas_call | solution.py:47
  123.9 4.3 %collective-permute-start.15 = (bf16[2,128,3200]{2,1,0:T(8,128)(2,1)S(1)}, bf16[2,128,3200]{2,1,0:T(8,128)(2,1)S(1)}, u32[]{:S(2)}, u32[]{:S(2)}) collective-permute-start(bf16[2,128,3200]{2,1,0:T(8,128)(2,1)S(1)} %get-tuple-element.68.refs_0_), channel_id=1, source_target_pairs={{0,1},{1,0},{2,3},{3,2},{4,5},{5,4},{6,7},{7,6},{8,9},{9,8},{10,11... | collective-permute-start | bytes 4915208 | tf_op jit(solution)/shard_map/ppermute | solution.py:460
  128.2 3.1 %collective-permute-done.15.refs_1_ = bf16[2,128,3200]{2,1,0:T(8,128)(2,1)S(1)} collective-permute-done((bf16[2,128,3200]{2,1,0:T(8,128)(2,1)S(1)}, bf16[2,128,3200]{2,1,0:T(8,128)(2,1)S(1)}, u32[]{:S(2)}, u32[]{:S(2)}) %collective-permute-start.15) | collective-permute-done | bytes 1638432 | tf_op jit(solution)/shard_map/ppermute | solution.py:460
  132.9 3.1 %collective-permute-done.16.refs_1_ = bf16[2,128,3200]{2,1,0:T(8,128)(2,1)S(1)} collective-permute-done((bf16[2,128,3200]{2,1,0:T(8,128)(2,1)S(1)}, bf16[2,128,3200]{2,1,0:T(8,128)(2,1)S(1)}, u32[]{:S(2)}, u32[]{:S(2)}) %collective-permute-start.16) | collective-permute-done | bytes 1638432 | tf_op jit(solution)/shard_map/ppermute | solution.py:461
  139.1 16.2 %shard_map.138 = (bf16[128,2560]{1,0:T(8,128)(2,1)S(1)}, bf16[128,2560]{1,0:T(8,128)(2,1)}) custom-call(s32[23]{0:T(128)S(1)} %concatenate.10.m, bf16[2,128,3200]{2,1,0:T(8,128)(2,1)S(1)} %get-tuple-element.68.refs_0_, bf16[2,128,3200]{2,1,0:T(8,128)(2,1)S(1)} %copy-done.18, bf16[2560,3200]{1,0:T(8,128)(2,1)} %refs_2_.9, bf16[2560,3200]{1,0:T(8,128)(2,1)} %refs_3_.9, ...), custom_call_target="tpu_custom_call" | custom-call | flops 1000 | bytes 1000 | tf_op jit(solution)/shard_map/pallas_call | solution.py:47
  160.0 15.5 %shard_map.139 = (bf16[128,2560]{1,0:T(8,128)(2,1)S(1)}, bf16[128,2560]{1,0:T(8,128)(2,1)S(1)}) custom-call(s32[23]{0:T(128)S(1)} %concatenate.10.m, bf16[2,128,3200]{2,1,0:T(8,128)(2,1)S(1)} %copy-done.6, bf16[2,128,3200]{2,1,0:T(8,128)(2,1)S(1)} %copy-done.16, bf16[2560,3200]{1,0:T(8,128)(2,1)} %refs_2_.9, bf16[2560,3200]{1,0:T(8,128)(2,1)} %refs_3_.9, ...), custom_call_target="tpu_custom_call" | custom-call | flops 1000 | bytes 1000 | tf_op jit(solution)/shard_map/pallas_call | solution.py:47
  179.3 15.5 %shard_map.141 = (bf16[128,2560]{1,0:T(8,128)(2,1)S(1)}, bf16[128,2560]{1,0:T(8,128)(2,1)S(1)}) custom-call(s32[23]{0:T(128)S(1)} %concatenate.10.m, bf16[2,128,3200]{2,1,0:T(8,128)(2,1)S(1)} %copy-done.12, bf16[2,128,3200]{2,1,0:T(8,128)(2,1)S(1)} %copy-done.14, bf16[2560,3200]{1,0:T(8,128)(2,1)} %refs_2_.9, bf16[2560,3200]{1,0:T(8,128)(2,1)} %refs_3_.9, ...), custom_call_target="tpu_custom_call" | custom-call | flops 1000 | bytes 1000 | tf_op jit(solution)/shard_map/pallas_call | solution.py:47
  197.3 3.2 %collective-permute-start.26 = (bf16[128,2560]{1,0:T(8,128)(2,1)S(1)}, bf16[128,2560]{1,0:T(8,128)(2,1)S(1)}, u32[]{:S(2)}, u32[]{:S(2)}) collective-permute-start(bf16[128,2560]{1,0:T(8,128)(2,1)S(1)} %shard_map.142.refs_2_.refs_0_), channel_id=1, source_target_pairs={{0,4},{2,6},{12,8},{14,10},{1,5},{3,7},{13,9},{15,11},{16,20},{18,... | collective-permute-start | bytes 1966088 | tf_op jit(solution)/shard_map/ppermute | solution.py:475
  200.5 15.5 %shard_map.144 = (bf16[128,2560]{1,0:T(8,128)(2,1)S(1)}, bf16[128,2560]{1,0:T(8,128)(2,1)S(1)}) custom-call(s32[23]{0:T(128)S(1)} %concatenate.10.m, bf16[2,128,3200]{2,1,0:T(8,128)(2,1)S(1)} %copy-done.4, bf16[2,128,3200]{2,1,0:T(8,128)(2,1)S(1)} %collective-permute-done.18.refs_1_, bf16[2560,3200]{1,0:T(8,128)(2,1)} %refs_2_.9, ...), custom_call_target="tpu_custom_call" | custom-call | flops 1000 | bytes 1000 | tf_op jit(solution)/shard_map/pallas_call | solution.py:47
  218.2 2.0 collective-permute-start.25
  221.3 6.7 %shard_map.147 = (bf16[3,64,3200]{2,1,0:T(8,128)(2,1)S(1)}, bf16[3,64,3200]{2,1,0:T(8,128)(2,1)}) custom-call(s32[23]{0:T(128)S(1)} %concatenate.10.m, bf16[512,128]{1,0:T(8,128)(2,1)S(1)} %get-tuple-element.61.refs_16_.refs_17_.refs_0_, bf16[512,3200]{1,0:T(8,128)(2,1)} %copy-done.11, bf16[128,2560]{1,0:T(8,128)(2,1)S(1)} %shard_map.146.refs_2_), custom_call_target="tpu_custom_call" | custom-call | flops 1000 | bytes 1000 | tf_op jit(solution)/shard_map/pallas_call | solution.py:47
  229.1 2.6 %collective-permute-start.29 = (bf16[3,64,3200]{2,1,0:T(8,128)(2,1)}, bf16[3,64,3200]{2,1,0:T(8,128)(2,1)}, u32[]{:S(2)}, u32[]{:S(2)}) collective-permute-start(bf16[3,64,3200]{2,1,0:T(8,128)(2,1)} %get-tuple-element.85), channel_id=1, source_target_pairs={{0,1},{1,0},{2,3},{3,2},{4,5},{5,4},{6,7},{7,6},{8,9},{9,8},{10,11... | collective-permute-start | bytes 3686408 | tf_op jit(solution)/shard_map/ppermute | solution.py:492
  233.3 2.0 shard_map.149
  240.5 2.8 %shard_map.151 = bf16[192,3200]{1,0:T(8,128)(2,1)} custom-call(s32[23]{0:T(128)S(1)} %concatenate.10.m, bf16[192,3200]{1,0:T(8,128)(2,1)S(1)} %bitcast.21, bf16[192,3200]{1,0:T(8,128)(2,1)} %bitcast.12.refs_1_, bf16[64,2560]{1,0:T(8,128)(2,1)S(1)} %get-tuple-element.84.refs_2_), custom_call_target="tpu_custom_call" | custom-call | flops 1000 | bytes 1000 | tf_op jit(solution)/shard_map/pallas_call | solution.py:47
  (117 shorter events, 50.2 us)
Async XLA Ops:
  7.2 76.9 %all-gather.2.cloned.1.call-start = ((), (), s32[]{:S(2)}) async-start(), calls=%async_computation | async-start | bytes 49152000 | tf_op jit(solution)/shard_map/all_gather | solution.py:435
  8.3 30.1 %collective-permute-start.1 = (bf16[64,5120]{1,0:T(8,128)(2,1)S(1)}, bf16[64,5120]{1,0:T(8,128)(2,1)}, u32[]{:S(2)}, u32[]{:S(2)}) collective-permute-start(bf16[64,5120]{1,0:T(8,128)(2,1)S(1)} %copy-done.1), channel_id=1, source_target_pairs={{0,4},{2,6},{4,0},{6,2},{8,12},{10,14},{12,8},{14,10},{1,5},{3,7},... | collective-permute-start | bytes 1966088 | tf_op jit(solution)/shard_map/ppermute | solution.py:436
  10.4 27.9 %collective-permute-start = (bf16[64,5120]{1,0:T(8,128)(2,1)S(1)}, bf16[64,5120]{1,0:T(8,128)(2,1)}, u32[]{:S(2)}, u32[]{:S(2)}) collective-permute-start(bf16[64,5120]{1,0:T(8,128)(2,1)S(1)} %copy-done.1), channel_id=1, source_target_pairs={{0,2},{2,0},{4,6},{6,4},{8,10},{10,8},{12,14},{14,12},{1,3},{3,1},... | collective-permute-start | bytes 1966088 | tf_op jit(solution)/shard_map/ppermute | solution.py:438
  11.6 28.0 %collective-permute-start.8 = (bf16[64,5120]{1,0:T(8,128)(2,1)S(1)}, bf16[64,5120]{1,0:T(8,128)(2,1)}, u32[]{:S(2)}, u32[]{:S(2)}) collective-permute-start(bf16[64,5120]{1,0:T(8,128)(2,1)S(1)} %copy-done.1), channel_id=1, source_target_pairs={{4,8},{6,10},{8,4},{10,6},{5,9},{7,11},{9,5},{11,7},{20,24},{22,26... | collective-permute-start | bytes 1966088 | tf_op jit(solution)/shard_map/ppermute | solution.py:437
  18.7 19.6 %collective-permute-start.3 = (bf16[64,640]{1,0:T(8,128)(2,1)S(1)}, bf16[64,640]{1,0:T(8,128)(2,1)S(1)}, u32[]{:S(2)}, u32[]{:S(2)}) collective-permute-start(bf16[64,640]{1,0:T(8,128)(2,1)S(1)} %get-tuple-element.46.refs_4_), channel_id=1, source_target_pairs={{0,8},{2,10},{4,12},{6,14},{8,0},{10,2},{12,4},{14,6},{1,9},{3,11}... | collective-permute-start | bytes 245768 | tf_op jit(solution)/shard_map/ppermute | solution.py:440
  26.7 11.6 %collective-permute-start.4 = (bf16[64,640]{1,0:T(8,128)(2,1)S(1)}, bf16[64,640]{1,0:T(8,128)(2,1)S(1)}, u32[]{:S(2)}, u32[]{:S(2)}) collective-permute-start(bf16[64,640]{1,0:T(8,128)(2,1)S(1)} %get-tuple-element.47.refs_5_), channel_id=1, source_target_pairs={{0,12},{2,14},{4,8},{6,10},{8,4},{10,6},{12,0},{14,2},{1,13},{3,15... | collective-permute-start | bytes 245768 | tf_op jit(solution)/shard_map/ppermute | solution.py:440
  38.3 18.2 %collective-permute-start.5 = (bf16[64,5120]{1,0:T(8,128)(2,1)}, bf16[64,5120]{1,0:T(8,128)(2,1)S(1)}, u32[]{:S(2)}, u32[]{:S(2)}) collective-permute-start(bf16[64,5120]{1,0:T(8,128)(2,1)} %collective-permute-done.1.refs_2_.refs_6_), channel_id=1, source_target_pairs={{0,2},{2,0},{4,6},{6,4},{8,10},{10,8},{12,14},{14,12},{1,3},{3,1},... | collective-permute-start | bytes 1966088 | tf_op jit(solution)/shard_map/ppermute | solution.py:442
  39.6 17.0 %collective-permute-start.12 = (bf16[64,5120]{1,0:T(8,128)(2,1)}, bf16[64,5120]{1,0:T(8,128)(2,1)}, u32[]{:S(2)}, u32[]{:S(2)}) collective-permute-start(bf16[64,5120]{1,0:T(8,128)(2,1)} %collective-permute-done.1.refs_2_.refs_6_), channel_id=1, source_target_pairs={{4,8},{6,10},{8,4},{10,6},{5,9},{7,11},{9,5},{11,7},{20,24},{22,26... | collective-permute-start | bytes 1966088 | tf_op jit(solution)/shard_map/ppermute | solution.py:443
  41.1 17.0 %collective-permute-start.9 = (bf16[64,5120]{1,0:T(8,128)(2,1)}, bf16[64,5120]{1,0:T(8,128)(2,1)}, u32[]{:S(2)}, u32[]{:S(2)}) collective-permute-start(bf16[64,5120]{1,0:T(8,128)(2,1)} %collective-permute-done.8), channel_id=1, source_target_pairs={{4,0},{6,2},{8,12},{10,14},{5,1},{7,3},{9,13},{11,15},{20,16},{22,... | collective-permute-start | bytes 1966088 | tf_op jit(solution)/shard_map/ppermute | solution.py:444
  56.7 18.0 %collective-permute-start.13 = (bf16[64,5120]{1,0:T(8,128)(2,1)}, bf16[64,5120]{1,0:T(8,128)(2,1)S(1)}, u32[]{:S(2)}, u32[]{:S(2)}) collective-permute-start(bf16[64,5120]{1,0:T(8,128)(2,1)} %collective-permute-done.12), channel_id=1, source_target_pairs={{4,0},{6,2},{8,12},{10,14},{5,1},{7,3},{9,13},{11,15},{20,16},{22,... | collective-permute-start | bytes 1966088 | tf_op jit(solution)/shard_map/ppermute | solution.py:451
  59.3 15.4 %collective-permute-start.10 = (bf16[64,5120]{1,0:T(8,128)(2,1)S(1)}, bf16[64,5120]{1,0:T(8,128)(2,1)S(1)}, u32[]{:S(2)}, u32[]{:S(2)}) collective-permute-start(bf16[64,5120]{1,0:T(8,128)(2,1)S(1)} %broadcast_select_fusion.1.refs_0_.refs_4_), channel_id=1, source_target_pairs={{0,2},{2,0},{4,6},{6,4},{8,10},{10,8},{12,14},{14,12},{1,3},{3,1},... | collective-permute-start | bytes 1966088 | tf_op jit(solution)/shard_map/ppermute | solution.py:448
  75.6 29.4 %collective-permute-start.14 = (bf16[64,5120]{1,0:T(8,128)(2,1)S(1)}, bf16[64,5120]{1,0:T(8,128)(2,1)}, u32[]{:S(2)}, u32[]{:S(2)}) collective-permute-start(bf16[64,5120]{1,0:T(8,128)(2,1)S(1)} %broadcast_select_fusion.refs_22_.refs_2_.refs_6_), channel_id=1, source_target_pairs={{0,2},{2,0},{4,6},{6,4},{8,10},{10,8},{12,14},{14,12},{1,3},{3,1},... | collective-permute-start | bytes 1966088 | tf_op jit(solution)/shard_map/ppermute | solution.py:453
  137.2 18.4 %collective-permute-start.17 = (bf16[2,128,3200]{2,1,0:T(8,128)(2,1)S(1)}, bf16[2,128,3200]{2,1,0:T(8,128)(2,1)S(1)}, u32[]{:S(2)}, u32[]{:S(2)}) collective-permute-start(bf16[2,128,3200]{2,1,0:T(8,128)(2,1)S(1)} %copy-done.12), channel_id=1, source_target_pairs={{0,1},{1,0},{2,3},{3,2},{4,5},{5,4},{6,7},{7,6},{8,9},{9,8},{10,11... | collective-permute-start | bytes 4915208 | tf_op jit(solution)/shard_map/ppermute | solution.py:462
  155.2 21.5 %collective-permute-start.19 = (bf16[128,2560]{1,0:T(8,128)(2,1)}, bf16[128,2560]{1,0:T(8,128)(2,1)S(1)}, u32[]{:S(2)}, u32[]{:S(2)}) collective-permute-start(bf16[128,2560]{1,0:T(8,128)(2,1)} %get-tuple-element.73.refs_4_), channel_id=1, source_target_pairs={{0,2},{2,0},{4,6},{6,4},{8,10},{10,8},{12,14},{14,12},{1,3},{3,1},... | collective-permute-start | bytes 1966088 | tf_op jit(solution)/shard_map/ppermute | solution.py:467
  156.7 43.7 %collective-permute-start.18 = (bf16[2,128,3200]{2,1,0:T(8,128)(2,1)S(1)}, bf16[2,128,3200]{2,1,0:T(8,128)(2,1)S(1)}, u32[]{:S(2)}, u32[]{:S(2)}) collective-permute-start(bf16[2,128,3200]{2,1,0:T(8,128)(2,1)S(1)} %copy-done.4), channel_id=1, source_target_pairs={{0,1},{1,0},{2,3},{3,2},{4,5},{5,4},{6,7},{7,6},{8,9},{9,8},{10,11... | collective-permute-start | bytes 4915208 | tf_op jit(solution)/shard_map/ppermute | solution.py:463
  175.4 19.4 %collective-permute-start.21 = (bf16[128,2560]{1,0:T(8,128)(2,1)S(1)}, bf16[128,2560]{1,0:T(8,128)(2,1)S(1)}, u32[]{:S(2)}, u32[]{:S(2)}) collective-permute-start(bf16[128,2560]{1,0:T(8,128)(2,1)S(1)} %get-tuple-element.74.refs_2_), channel_id=1, source_target_pairs={{0,2},{2,0},{4,6},{6,4},{8,10},{10,8},{12,14},{14,12},{1,3},{3,1},... | collective-permute-start | bytes 1966088 | tf_op jit(solution)/shard_map/ppermute | solution.py:467
  177.4 18.1 %collective-permute-start.20 = (bf16[128,2560]{1,0:T(8,128)(2,1)S(1)}, bf16[128,2560]{1,0:T(8,128)(2,1)S(1)}, u32[]{:S(2)}, u32[]{:S(2)}) collective-permute-start(bf16[128,2560]{1,0:T(8,128)(2,1)S(1)} %shard_map.140.refs_4_.refs_0_), channel_id=1, source_target_pairs={{0,4},{2,6},{12,8},{14,10},{1,5},{3,7},{13,9},{15,11},{16,20},{18,... | collective-permute-start | bytes 1966088 | tf_op jit(solution)/shard_map/ppermute | solution.py:472
  196.2 19.7 %collective-permute-start.24 = (bf16[128,2560]{1,0:T(8,128)(2,1)S(1)}, bf16[128,2560]{1,0:T(8,128)(2,1)S(1)}, u32[]{:S(2)}, u32[]{:S(2)}) collective-permute-start(bf16[128,2560]{1,0:T(8,128)(2,1)S(1)} %shard_map.143.refs_4_), channel_id=1, source_target_pairs={{4,8},{6,10},{8,4},{10,6},{5,9},{7,11},{9,5},{11,7},{20,24},{22,26... | collective-permute-start | bytes 1966088 | tf_op jit(solution)/shard_map/ppermute | solution.py:477
  196.9 19.0 %collective-permute-start.23 = (bf16[128,2560]{1,0:T(8,128)(2,1)S(1)}, bf16[128,2560]{1,0:T(8,128)(2,1)S(1)}, u32[]{:S(2)}, u32[]{:S(2)}) collective-permute-start(bf16[128,2560]{1,0:T(8,128)(2,1)S(1)} %get-tuple-element.76.refs_2_), channel_id=1, source_target_pairs={{0,2},{2,0},{4,6},{6,4},{8,10},{10,8},{12,14},{14,12},{1,3},{3,1},... | collective-permute-start | bytes 1966088 | tf_op jit(solution)/shard_map/ppermute | solution.py:467
  197.3 19.5 %collective-permute-start.26 = (bf16[128,2560]{1,0:T(8,128)(2,1)S(1)}, bf16[128,2560]{1,0:T(8,128)(2,1)S(1)}, u32[]{:S(2)}, u32[]{:S(2)}) collective-permute-start(bf16[128,2560]{1,0:T(8,128)(2,1)S(1)} %shard_map.142.refs_2_.refs_0_), channel_id=1, source_target_pairs={{0,4},{2,6},{12,8},{14,10},{1,5},{3,7},{13,9},{15,11},{16,20},{18,... | collective-permute-start | bytes 1966088 | tf_op jit(solution)/shard_map/ppermute | solution.py:475
  217.5 17.9 %collective-permute-start.27 = (bf16[128,2560]{1,0:T(8,128)(2,1)S(1)}, bf16[128,2560]{1,0:T(8,128)(2,1)S(1)}, u32[]{:S(2)}, u32[]{:S(2)}) collective-permute-start(bf16[128,2560]{1,0:T(8,128)(2,1)S(1)} %shard_map.146.refs_2_), channel_id=1, source_target_pairs={{4,8},{6,10},{8,4},{10,6},{5,9},{7,11},{9,5},{11,7},{20,24},{22,26... | collective-permute-start | bytes 1966088 | tf_op jit(solution)/shard_map/ppermute | solution.py:482
  218.2 17.2 %collective-permute-start.25 = (bf16[128,2560]{1,0:T(8,128)(2,1)S(1)}, bf16[128,2560]{1,0:T(8,128)(2,1)S(1)}, u32[]{:S(2)}, u32[]{:S(2)}) collective-permute-start(bf16[128,2560]{1,0:T(8,128)(2,1)S(1)} %shard_map.145.refs_2_), channel_id=1, source_target_pairs={{0,4},{2,6},{4,0},{6,2},{8,12},{10,14},{12,8},{14,10},{1,5},{3,7},... | collective-permute-start | bytes 1966088 | tf_op jit(solution)/shard_map/ppermute | solution.py:480
  220.2 15.3 %collective-permute-start.22 = (bf16[128,2560]{1,0:T(8,128)(2,1)S(1)}, bf16[128,2560]{1,0:T(8,128)(2,1)S(1)}, u32[]{:S(2)}, u32[]{:S(2)}) collective-permute-start(bf16[128,2560]{1,0:T(8,128)(2,1)S(1)} %get-tuple-element.78.refs_3_), channel_id=1, source_target_pairs={{0,2},{2,0},{4,6},{6,4},{8,10},{10,8},{12,14},{14,12},{1,3},{3,1},... | collective-permute-start | bytes 1966088 | tf_op jit(solution)/shard_map/ppermute | solution.py:467
  229.1 11.3 %collective-permute-start.29 = (bf16[3,64,3200]{2,1,0:T(8,128)(2,1)}, bf16[3,64,3200]{2,1,0:T(8,128)(2,1)}, u32[]{:S(2)}, u32[]{:S(2)}) collective-permute-start(bf16[3,64,3200]{2,1,0:T(8,128)(2,1)} %get-tuple-element.85), channel_id=1, source_target_pairs={{0,1},{1,0},{2,3},{3,2},{4,5},{5,4},{6,7},{7,6},{8,9},{9,8},{10,11... | collective-permute-start | bytes 3686408 | tf_op jit(solution)/shard_map/ppermute | solution.py:492
  (30 other events, 200.5 us)
Sparse Core Ops, SparseCore 0:
  9.6 52.6 all-gather.1

commit v3 on v2

--- a/solution.py
+++ b/solution.py
@@ -37,7 +37,7 @@
 
 
 def call(
-    kernel, meta, args, grid, in_specs, out_specs, out_shape, scratch=(), vmem=48, after=(), cost=(1000, 1000)
+    kernel, meta, args, grid, in_specs, out_specs, out_shape, scratch=(), vmem=58, after=(), cost=(1000, 1000)
 ):
     first, extra = len(args), len(after)
 
@@ -124,7 +124,7 @@
     )
 
 
-def low_out_kernel(m, own_ref, other_ref, s0, s1, s2, s3, low_in_ref, full_ref, short_ref):
+def low_out_kernel(m, own_ref, other_ref, s0, s1, s2, s3, out_ref):
     rows = own_ref.shape[0]
     rank, columns = s0.shape
     y, z = m[M_Y], m[M_Z]
@@ -134,31 +134,47 @@
         tokens = jnp.concatenate([own_ref[:, at], other_ref[:, at]], axis=0)
         total += nt_dot(tokens, slab[...])
     own, other = total[:rows], total[rows:]
-    packed = jnp.concatenate(
+    out_ref[...] = jnp.concatenate(
         [jnp.where(y == 0, own, other), jnp.where(y == 0, other, own)], axis=1
     )
-    at = pl.ds(pl.multiple_of(z * rows, rows), rows)
-    for ref in (full_ref, short_ref):
-        ref[: 4 * rows] = jnp.zeros((4 * rows, 2 * rank), ref.dtype)
-        ref[4 * rows :] = low_in_ref[...].astype(ref.dtype)
-        ref[at, :] = packed.astype(ref.dtype)
-
-
-def low_parts(meta, own, other, pieces, low_in, after):
+
+
+def low_block(meta, own, other, pieces, after):
     rows, full = own.shape
     rank, columns = pieces[0].shape
-    out = (8 * rows, 2 * rank)
     return call(
         low_out_kernel,
         meta,
-        (own, other, *pieces, low_in),
+        (own, other, *pieces),
         (1,),
         [pl.BlockSpec((rows, full), lambda i, m: (0, 0))] * 2
-        + [pl.BlockSpec((rank, columns), lambda i, m: (0, 0))] * 4
-        + [pl.BlockSpec((4 * rows, 2 * rank), lambda i, m: (0, 0))],
+        + [pl.BlockSpec((rank, columns), lambda i, m: (0, 0))] * 4,
+        pl.BlockSpec((rows, 2 * rank), lambda i, m: (0, 0)),
+        jax.ShapeDtypeStruct((rows, 2 * rank), F32),
+        after=after,
+    )
+
+
+def place_kernel(m, *refs):
+    rows = refs[0].shape[0]
+    for k in range(4):
+        at = pl.ds(pl.multiple_of(jnp.bitwise_xor(m[M_Z], k) * rows, rows), rows)
+        part = refs[k][...]
+        refs[4][at, :] = part
+        refs[5][at, :] = part.astype(BF16)
+
+
+def place_blocks(meta, parts):
+    rows, width = parts[0].shape
+    out = (4 * rows, width)
+    return call(
+        place_kernel,
+        meta,
+        parts,
+        (1,),
+        [pl.BlockSpec((rows, width), lambda i, m: (0, 0))] * 4,
         [pl.BlockSpec(out, lambda i, m: (0, 0))] * 2,
         [jax.ShapeDtypeStruct(out, F32), jax.ShapeDtypeStruct(out, BF16)],
-        after=after,
     )
 
 
@@ -189,107 +205,109 @@
     )
 
 
-def act_grad_kernel(m, *refs):
-    mine, other, gates, ups = refs[:4], refs[4:8], refs[8:12], refs[12:16]
-    lows, factors = refs[16:18], refs[18:20]
-    down_mine, down_other = refs[20:22]
-    outs, lhs = refs[22:24], refs[24]
+def act_grad_kernel(joined, m, *refs):
+    mine, other = refs[:8], refs[8:16]
+    gate_ref, up_ref, low_ref = refs[16:19]
+    factors = refs[19:23]
+    down_mine, down_other = refs[23:25]
+    outs, lhs = refs[25:-1], refs[-1]
     rows = mine[0].shape[0]
     rank = factors[0].shape[1]
     y = m[M_Y]
 
     @pl.when(pl.program_id(0) == 0)
     def _():
-        for s in range(4):
+        for s in range(8):
             lhs[0, s * rows : (s + 1) * rows] = mine[s][...]
             lhs[1, s * rows : (s + 1) * rows] = other[s][...]
 
     total = jnp.dot(lhs[0], down_mine[...], preferred_element_type=F32)
     total += jnp.dot(lhs[1], down_other[...], preferred_element_type=F32)
-    for i in range(2):
-        first, second = lows[i][:, :rank], lows[i][:, rank:]
+    for i in range(4):
+        z = m[M_Z + i]
+        packed = low_ref[pl.ds(pl.multiple_of(z * rows, rows), rows), :]
+        first, second = packed[:, :rank], packed[:, rank:]
         low = jnp.concatenate(
             [jnp.where(y == 0, first, second), jnp.where(y == 0, second, first)], axis=0
         )
         term = jnp.dot(low, factors[i][0], preferred_element_type=F32)
+        out = outs[0].at[i] if joined else outs[i]
         for j in range(2):
             at = slice(j * rows, (j + 1) * rows)
             hg = total[(2 * i + j) * rows : (2 * i + j + 1) * rows] + ADAPTER_SCALE * term[at]
-            g = gates[2 * i + j][...].astype(F32)
-            u = ups[2 * i + j][...].astype(F32)
+            source = pl.ds(pl.multiple_of((z * 2 + (1 - y if j else y)) * rows, rows), rows)
+            g = gate_ref[source, :].astype(F32)
+            u = up_ref[source, :].astype(F32)
             sig = jax.nn.sigmoid(g)
-            outs[i][0, at] = (hg * u * sig * (1.0 + g * (1.0 - sig))).astype(BF16)
-            outs[i][1, at] = (hg * (g * sig)).astype(BF16)
-
-
-def act_grads(meta, slots, shards, gate_act, up_act, low, a_t, down, after=()):
+            out[0, at] = (hg * u * sig * (1.0 + g * (1.0 - sig))).astype(BF16)
+            out[1, at] = (hg * (g * sig)).astype(BF16)
+
+
+def act_grads(meta, shards, gate_act, up_act, low, a_t, down_mine, down_other, span, joined, after=()):
     rows = shards[0].shape[0]
     rank = a_t.shape[1]
-    half, width = down.shape[0] // 2, down.shape[1]
-    step = width // 5
-
-    def act_spec(slot, j):
-        def index(n, m):
-            y = m[M_Y]
-            return (m[M_Z + slot] * 2 + (1 - y if j else y), n)
-
-        return pl.BlockSpec((rows, step), index)
-
-    def low_spec(slot):
-        return pl.BlockSpec((rows, 2 * rank), lambda n, m: (m[M_Z + slot], 0))
+    half = down_mine.shape[0]
+    start, width, step = span
+    first = start // step
 
     def factor_spec(slot):
-        return pl.BlockSpec((1, rank, step), lambda n, m: (m[M_SLOT_ADAPTER + slot], 0, n))
-
-    acts = [act_spec(slot, j) for slot in slots for j in range(2)]
-    return call(
-        act_grad_kernel,
-        meta,
-        (*shards, *shards, *[gate_act] * 4, *[up_act] * 4, low, low, a_t, a_t, down, down),
+        return pl.BlockSpec((1, rank, step), lambda n, m: (m[M_SLOT_ADAPTER + slot], 0, n + first))
+
+    if joined:
+        out_specs = [pl.BlockSpec((4, 2, 2 * rows, step), lambda n, m: (0, 0, 0, n))]
+        out_shape = [jax.ShapeDtypeStruct((4, 2, 2 * rows, width), BF16)]
+    else:
+        out_specs = [pl.BlockSpec((2, 2 * rows, step), lambda n, m: (0, 0, n))] * 4
+        out_shape = [jax.ShapeDtypeStruct((2, 2 * rows, width), BF16)] * 4
+    return call(
+        functools.partial(act_grad_kernel, joined),
+        meta,
+        (*shards, *shards, gate_act, up_act, low, *[a_t] * 4, down_mine, down_other),
         (width // step,),
-        [pl.BlockSpec((rows, half), lambda n, m: (0, m[M_D]))] * 4
-        + [pl.BlockSpec((rows, half), lambda n, m: (0, 1 - m[M_D]))] * 4
-        + acts
-        + acts
-        + [low_spec(slot) for slot in slots]
-        + [factor_spec(slot) for slot in slots]
-        + [
-            pl.BlockSpec((half, step), lambda n, m: (m[M_D], n)),
-            pl.BlockSpec((half, step), lambda n, m: (1 - m[M_D], n)),
-        ],
-        [pl.BlockSpec((2, 2 * rows, step), lambda n, m: (0, 0, n))] * 2,
-        [jax.ShapeDtypeStruct((2, 2 * rows, width), BF16)] * 2,
-        scratch=[pltpu.VMEM((2, 4 * rows, half), BF16)],
-        after=after,
-    )
-
-
-def input_grad_kernel(m, mine_ref, other_ref, gate_ref, up_ref, keep_ref, send_ref, lhs):
+        [pl.BlockSpec((rows, half), lambda n, m: (0, m[M_D]))] * 8
+        + [pl.BlockSpec((rows, half), lambda n, m: (0, 1 - m[M_D]))] * 8
+        + [pl.BlockSpec((8 * rows, step), lambda n, m: (0, n + first))] * 2
+        + [pl.BlockSpec((4 * rows, 2 * rank), lambda n, m: (0, 0))]
+        + [factor_spec(slot) for slot in range(4)]
+        + [pl.BlockSpec((half, step), lambda n, m: (0, n + first))] * 2,
+        out_specs,
+        out_shape,
+        scratch=[pltpu.VMEM((2, 8 * rows, half), BF16)],
+        after=after,
+    )
+
+
+def input_grad_kernel(m, mine_ref, other_ref, tail_ref, other_tail_ref, gate_ref, up_ref, keep_ref, send_ref, lhs):
     rows = mine_ref.shape[1] // 2
+    main = mine_ref.shape[2]
 
     @pl.when(pl.program_id(0) == 0)
     def _():
         for i in range(2):
             for y in range(2):
-                lhs[i, (2 * y) * rows : (2 * y + 1) * rows] = mine_ref[i, y * rows : (y + 1) * rows]
-                lhs[i, (2 * y + 1) * rows : (2 * y + 2) * rows] = other_ref[i, y * rows : (y + 1) * rows]
+                at = slice(y * rows, (y + 1) * rows)
+                for k, (ref, tail) in enumerate(((mine_ref, tail_ref), (other_ref, other_tail_ref))):
+                    to = slice((2 * y + k) * rows, (2 * y + k + 1) * rows)
+                    lhs[i, to, :main] = ref[i, at]
+                    lhs[i, to, main:] = tail[0, i, at]
 
     total = nt_dot(lhs[0], gate_ref[...]) + nt_dot(lhs[1], up_ref[...])
     keep_ref[...] = total[: 2 * rows].astype(BF16)
     send_ref[...] = total[2 * rows :].astype(BF16)
 
 
-def input_grad_parts(meta, mine, other, gate, up, after=()):
-    rows, width = mine.shape[1:]
-    half = gate.shape[0]
+def input_grad_parts(meta, slot, mine, other, tail, other_tail, gate, up, after=()):
+    rows, main = mine.shape[1:]
+    half, width = gate.shape
     step = 512
     out = jax.ShapeDtypeStruct((rows, half), BF16)
     return call(
         input_grad_kernel,
         meta,
-        (mine, other, gate, up),
+        (mine, other, tail, other_tail, gate, up),
         (half // step,),
-        [pl.BlockSpec((2, rows, width), lambda n, m: (0, 0, 0))] * 2
+        [pl.BlockSpec((2, rows, main), lambda n, m: (0, 0, 0))] * 2
+        + [pl.BlockSpec((1, 2, rows, width - main), lambda n, m: (slot, 0, 0, 0))] * 2
         + [pl.BlockSpec((step, width), lambda n, m: (n, 0))] * 2,
         [pl.BlockSpec((rows, step), lambda n, m: (0, n))] * 2,
         [out, out],
@@ -313,9 +331,9 @@
         ref[0] = total.astype(BF16)
 
 
-def owner_grads(meta, low, which, features, owned, after=()):
+def owner_grads(meta, low, features, owned, after=()):
     tokens, width = features.shape
-    half_rows, double = low.shape[0] // 2, low.shape[1]
+    half_rows, double = low.shape
     rank = double // 2
     out = jax.ShapeDtypeStruct((owned, rank, width), BF16)
     return call(
@@ -324,7 +342,7 @@
         (low, features),
         (owned,),
         [
-            pl.BlockSpec((half_rows, double), lambda i, m: (which, 0)),
+            pl.BlockSpec((half_rows, double), lambda i, m: (0, 0)),
             pl.BlockSpec((tokens, width), lambda i, m: (0, 0)),
         ],
         [pl.BlockSpec((1, rank, width), lambda i, m: (i, 0, 0))] * 2,
@@ -352,7 +370,6 @@
         [spec] * len(xs),
         [spec] * len(kinds),
         [jax.ShapeDtypeStruct((rows, width), k) for k in kinds],
-        vmem=16,
         after=after,
     )
     return out if len(kinds) > 1 else out[0]
@@ -377,7 +394,6 @@
         [pl.BlockSpec((rows, width), lambda i, m: (0, 0))] * len(xs),
         [pl.BlockSpec((rows // 2, width), lambda i, m: (0, 0))] * 2,
         [jax.ShapeDtypeStruct((rows // 2, width), BF16)] * 2,
-        vmem=16,
         after=after,
     )
 
@@ -432,58 +448,69 @@
     swap_cores = functools.partial(lax.ppermute, axis_name="dp", perm=CORES)
     at_end = (z == 0) | (z == 3)
 
-    down = lax.all_gather(down_matrix, "dp", axis=0, tiled=True)
+    down_other = swap_cores(down_matrix)
     pair = send(cotangent, perm=PAIR)
     mid = send(cotangent, perm=MID)
     y0 = send(cotangent, perm=Y_SWAP)
     slab, *others = slabs(meta, adapter_output_factor)
-    pieces = [send(s, perm=p) for s, p in zip(others, (PAIR, FAR, ACROSS))]
     hidden, low_in = hidden_and_low_in(meta, gate_act, up_act, a_t, tuple(others))
-    y1 = send(tied(pair, y0, low_in, *pieces), perm=Y_SWAP)
-    pair_mid = send(tied(pair, low_in), perm=MID)
-    mid_out = send(tied(mid, low_in), perm=OUTWARD)
-    low_sum, low = low_parts(meta, cotangent, y0, [slab] + pieces, low_in, ())
-    low_sum, low = add_after(meta, (low_sum, send(low, perm=Y_SWAP)), (), (F32, BF16))
+    piece1 = send(others[0], perm=PAIR)
+    piece2 = send(tied(others[1], y0, low_in), perm=FAR)
+    piece3 = send(tied(others[2], y0, low_in), perm=ACROSS)
+    y1 = send(tied(pair, y0, low_in, piece1), perm=Y_SWAP)
+    pair_mid = send(tied(pair, y0, low_in), perm=MID)
+    mid_out = send(tied(mid, y0, low_in), perm=OUTWARD)
     slot2 = jnp.where(at_end, mid_out, mid)
-    y2 = send(tied(slot2, y1, low), perm=Y_SWAP)
-    low = tied(low, y1)
-    low_sum, low = add_after(meta, (low_sum, send(low, perm=PAIR)), (), (F32, BF16))
-    far_out = send(pair_mid, perm=OUTWARD)
-    slot3 = tied(jnp.where(at_end, tied(far_out, low), pair_mid), y2)
+    y2 = send(tied(slot2, y1, piece2, piece3), perm=Y_SWAP)
+    far_out = send(tied(pair_mid, y1), perm=OUTWARD)
+    block = low_block(meta, cotangent, y0, (slab, piece1, piece2, piece3), (y1, down_other))
+    blocks_z = [block] + [send(block, perm=p) for p in (PAIR, FAR, ACROSS)]
+    low_half, low_half_short = place_blocks(meta, blocks_z)
+    slot3 = tied(jnp.where(at_end, far_out, pair_mid), y2, low_half)
     y3 = send(slot3, perm=Y_SWAP)
-    low = tied(low, y2)
-    low_sum, low = add_after(meta, (low_sum, send(low, perm=FAR)), (), (F32, BF16))
-    near, far = (cotangent, y0, pair, y1), (slot2, y2, slot3, y3)
-    rest = (gate_act, up_act, low, a_t, down)
-    mine0, mine1 = act_grads(meta, (0, 1), near, *rest, (slot3,))
-    mine2, mine3 = act_grads(meta, (2, 3), far, *rest, (mine0,))
-    other3 = swap_cores(mine3)
-    other2 = swap_cores(tied(mine2, other3))
-    other1 = swap_cores(tied(mine1, other2))
-    other0 = swap_cores(tied(mine0, other1))
-
-    def parts(mine, other, after):
-        keep, give = input_grad_parts(meta, mine, other, gate_matrix, up_matrix, after)
+    low = add_after(meta, (low_half, send(tied(low_half_short, y2), perm=Y_SWAP)), ())
+    shards = (cotangent, y0, pair, y1, slot2, y2, slot3, y3)
+    width = gate_act.shape[1]
+    main = width // 256 * 256
+    rest = (shards, gate_act, up_act, low, a_t, down_matrix, down_other)
+    (tail,) = act_grads(meta, *rest, (main, width - main, width - main), True)
+    mine = act_grads(meta, *rest, (0, main, 256), False, (tail,))
+    other_tail = swap_cores(tail)
+    other3 = swap_cores(mine[3])
+    other2 = swap_cores(tied(mine[2], other3))
+
+    def parts(slot, other, after):
+        keep, give = input_grad_parts(
+            meta, slot, mine[slot], other, tail, other_tail, gate_matrix, up_matrix, after
+        )
         return keep, send(give, perm=Y_SWAP), give
 
-    keep3, got3, give3 = parts(mine3, other3, (mine2,))
-    keep2, got2, give2 = parts(mine2, other2, (give3,))
-    sum3 = add_after(meta, (keep3, got3), (give2,))
+    got_in = send(tied(low_in, mine[3]).astype(BF16), perm=Y_SWAP)
+    keep3, got3, give3 = parts(3, other3, ())
+    low_in, short = add_after(meta, (low_in, got_in), (give3,), (F32, BF16))
+    got_in = send(short, perm=PAIR)
+    keep2, got2, give2 = parts(2, other2, (short,))
+    low_in, short = add_after(meta, (low_in, got_in), (give2,), (F32, BF16))
+    got_in = send(short, perm=FAR)
+    sum3 = add_after(meta, (keep3, got3), (short,))
     far_in = send(sum3, perm=INWARD)
-    keep1, got1, give1 = parts(mine1, other1, (sum3,))
-    sum2 = add_after(meta, (keep2, got2), (give1,))
+    other1 = swap_cores(tied(mine[1], give3))
+    keep1, got1, give1 = parts(1, other1, (sum3,))
+    low_in = add_after(meta, (low_in, got_in), (give1,))
+    sum2 = add_after(meta, (keep2, got2), (low_in,))
     mid_in = send(sum2, perm=INWARD)
     sum3 = add_after(meta, (sum3, far_in), (sum2,))
     far_mid = send(sum3, perm=MID)
-    keep0, got0, give0 = parts(mine0, other0, (sum3,))
+    other0 = swap_cores(tied(mine[0], give2))
+    keep0, got0, give0 = parts(0, other0, (sum3,))
     sum1 = add_after(meta, (keep1, got1, far_mid), (give0,))
     from_pair = send(sum1, perm=PAIR)
     sum2 = add_after(meta, (sum2, mid_in), (sum1,))
     from_mid = send(sum2, perm=MID)
     owned = adapters // 2
-    keep_a, give_a = owner_grads(meta, low, 0, hidden, owned, (sum2,))
-    columns = own_columns(meta, near + far, adapter_output_factor.shape[2], (keep_a,))
-    keep_b, give_b = owner_grads(meta, low, 1, columns, owned)
+    keep_a, give_a = owner_grads(meta, low, hidden, owned, (sum2,))
+    columns = own_columns(meta, shards, adapter_output_factor.shape[2], (keep_a,))
+    keep_b, give_b = owner_grads(meta, low_in, columns, owned)
     own, give = final_sum(meta, (keep0, got0, from_pair, from_mid), (keep_b,))
     grad_b = add(keep_b, swap_cores(give_b))
     shape = keep_a.shape

time: 251 us -> 292 us (1.16)
  Pallas kernels: 130 us -> 164 us
  between operations: 14.5 us -> 1.07 us
  waiting for transfers between devices: 45.3 us -> 55.5 us
  starting transfers between devices: 41.8 us -> 50.5 us
    pallas_call x22 -> x24, Pallas kernels: 130 us -> 164 us  [call(): pl.pallas_call(run, grid_spec=pltpu.PrefetchScalarGridSpec(num_scalar_pre...]
    ppermute x15 -> x21, waiting for transfers between devices: 44.1 us -> 54.7 us  [the longest x1 16 us: grid_body(): got_in = send(tied(low_in, mine[3]).astype(BF16), perm=Y_SWAP)]
    ppermute x15 -> x21, starting transfers between devices: 19.6 us -> 29.6 us  [the longest x1 5.75 us: grid_body(): other3 = swap_cores(mine[3])]
    unnamed x44 -> x82, local copies, waits for them, and re-layouts: 14.2 us -> 12.9 us
  transfers between devices with their start and end apart: 32 -> 37, of which waited for: 8 -> 11; matrix products, arithmetic and copies ran while one was open for 2% -> 3% of each run, Pallas kernels for 43% -> 43%
where the time goes in v3:
time: 292 us; the launch traced here: 291 us
  Pallas kernels  164 us (56%)
  waiting for transfers between devices  55.5 us (19%)
  starting transfers between devices  50.5 us (17%)
  local copies, waits for them, and re-layouts  14.3 us (5%)
  other arithmetic  6.01 us (2%)
    pallas_call x24, Pallas kernels, call(): pl.pallas_call(run, grid_spec=pltpu.PrefetchScalarGridSpec(num_scalar_pre...  164 us
    ppermute x1, waiting for transfers between devices, grid_body(): got_in = send(tied(low_in, mine[3]).astype(BF16), perm=Y_SWAP)  16 us
    unnamed x82, local copies, waits for them, and re-layouts  12.9 us
    ppermute x1, waiting for transfers between devices, grid_body(): send(tied(low_half_short, y2), perm=Y_SWAP)  11.4 us
    ppermute x1, waiting for transfers between devices, grid_body(): y1 = send(tied(pair, y0, low_in, piece1), perm=Y_SWAP)  8.35 us
    ppermute x1, waiting for transfers between devices, grid_body(): far_out = send(tied(pair_mid, y1), perm=OUTWARD)  5.86 us
  transfers between devices with their start and end apart: 37, of which 11 were waited for; matrix products, arithmetic and copies ran while one was open for 3% of the time, Pallas kernels for 43%

profile of v3, /device:TPU:1, one launch (start us, length us, event | category | flops | bytes accessed | tf_op | source)
XLA Modules:
  0.0 290.9 jit_solution(10724857726184415896)
XLA Ops:
  11.3 3.8 %collective-permute-start.2 = (bf16[64,640]{1,0:T(8,128)(2,1)}, bf16[64,640]{1,0:T(8,128)(2,1)S(1)}, u32[]{:S(2)}, u32[]{:S(2)}) collective-permute-start(bf16[64,640]{1,0:T(8,128)(2,1)} %get-tuple-element.46.refs_3_), channel_id=1, source_target_pairs={{0,4},{2,6},{4,0},{6,2},{8,12},{10,14},{12,8},{14,10},{1,5},{3,7},... | collective-permute-start | bytes 245768 | tf_op jit(solution)/shard_map/ppermute | solution.py:457
  15.1 6.8 %shard_map.131 = (bf16[512,3200]{1,0:T(8,128)(2,1)}, f32[256,128]{1,0:T(8,128)}) custom-call(s32[23]{0:T(128)} %concatenate.10.m, bf16[512,3200]{1,0:T(8,128)(2,1)} %refs_16_.3, bf16[512,3200]{1,0:T(8,128)(2,1)} %refs_17_.3, bf16[6,64,3200]{2,1,0:T(8,128)(2,1)} %bitcast.16, bf16[64,640]{1,0:T(8,128)(2,1)} %get-tuple-element.46.refs_3_, ...), custom_call_target="tpu_custom_call" | custom-call | flops 1000 | bytes 1000 | tf_op jit(solution)/shard_map/pallas_call | solution.py:47
  24.3 4.6 %collective-permute-start.6 = (bf16[64,640]{1,0:T(8,128)(2,1)S(1)}, bf16[64,640]{1,0:T(8,128)(2,1)S(1)}, u32[]{:S(2)}, u32[]{:S(2)}) collective-permute-start(bf16[64,640]{1,0:T(8,128)(2,1)S(1)} %copy-done.28), channel_id=1, source_target_pairs={{0,8},{2,10},{4,12},{6,14},{8,0},{10,2},{12,4},{14,6},{1,9},{3,11}... | collective-permute-start | bytes 245768 | tf_op jit(solution)/shard_map/ppermute | solution.py:458
  28.9 8.4 %collective-permute-done.3.refs_6_.refs_3_.refs_11_ = bf16[64,5120]{1,0:T(8,128)(2,1)S(1)} collective-permute-done((bf16[64,5120]{1,0:T(8,128)(2,1)S(1)}, bf16[64,5120]{1,0:T(8,128)(2,1)S(1)}, u32[]{:S(2)}, u32[]{:S(2)}) %collective-permute-start.3) | collective-permute-done | bytes 655392 | tf_op jit(solution)/shard_map/ppermute | solution.py:460
  52.0 5.9 %collective-permute-done.10 = bf16[64,5120]{1,0:T(8,128)(2,1)S(1)} collective-permute-done((bf16[64,5120]{1,0:T(8,128)(2,1)S(1)}, bf16[64,5120]{1,0:T(8,128)(2,1)S(1)}, u32[]{:S(2)}, u32[]{:S(2)}) %collective-permute-start.10) | collective-permute-done | bytes 655392 | tf_op jit(solution)/shard_map/ppermute | solution.py:465
  62.9 11.4 %collective-permute-done.16.refs_1_ = bf16[256,128]{1,0:T(8,128)(2,1)S(1)} collective-permute-done((bf16[256,128]{1,0:T(8,128)(2,1)}, bf16[256,128]{1,0:T(8,128)(2,1)S(1)}, u32[]{:S(2)}, u32[]{:S(2)}) %collective-permute-start.16) | collective-permute-done | bytes 65568 | tf_op jit(solution)/shard_map/ppermute | solution.py:471
  78.0 6.0 %shard_map.135.refs_25_.refs_2_ = bf16[4,2,128,128]{3,2,1,0:T(8,128)(2,1)} custom-call(s32[23]{0:T(128)} %concatenate.10.m, bf16[64,5120]{1,0:T(8,128)(2,1)} %refs_0_.11, bf16[64,5120]{1,0:T(8,128)(2,1)} %copy-done, bf16[64,5120]{1,0:T(8,128)(2,1)} %copy-done.4, bf16[64,5120]{1,0:T(8,128)(2,1)} %copy-done.1, bf16[64,5120]{1,0:T(8,128)(2,1)} %copy-done.2, ...), custom_call_target="tpu_custom_call" | custom-call | flops 1000 | bytes 1000 | tf_op jit(solution)/shard_map/pallas_call | solution.py:47
  84.0 29.3 %shard_map.136 = (bf16[2,128,3072]{2,1,0:T(8,128)(2,1)}, bf16[2,128,3072]{2,1,0:T(8,128)(2,1)}, bf16[2,128,3072]{2,1,0:T(8,128)(2,1)}, bf16[2,128,3072]{2,1,0:T(8,128)(2,1)}) custom-call(s32[23]{0:T(128)} %concatenate.10.m, bf16[64,5120]{1,0:T(8,128)(2,1)} %refs_0_.11, bf16[64,5120]{1,0:T(8,128)(2,1)} %copy-done, bf16[64,5120]{1,0:T(8,128)(2,1)} %copy-done.4, ...), custom_call_target="tpu_custom_call" | custom-call | flops 1000 | bytes 1000 | tf_op jit(solution)/shard_map/pallas_call | solution.py:47
  113.3 5.8 %collective-permute-start.17 = (bf16[2,128,3072]{2,1,0:T(8,128)(2,1)}, bf16[2,128,3072]{2,1,0:T(8,128)(2,1)S(1)}, u32[]{:S(2)}, u32[]{:S(2)}) collective-permute-start(bf16[2,128,3072]{2,1,0:T(8,128)(2,1)} %get-tuple-element.64.refs_0_), channel_id=1, source_target_pairs={{0,1},{1,0},{2,3},{3,2},{4,5},{5,4},{6,7},{7,6},{8,9},{9,8},{10,11... | collective-permute-start | bytes 4718600 | tf_op jit(solution)/shard_map/ppermute | solution.py:479
  119.1 3.2 %collective-permute-done.17.refs_1_ = bf16[2,128,3072]{2,1,0:T(8,128)(2,1)S(1)} collective-permute-done((bf16[2,128,3072]{2,1,0:T(8,128)(2,1)}, bf16[2,128,3072]{2,1,0:T(8,128)(2,1)S(1)}, u32[]{:S(2)}, u32[]{:S(2)}) %collective-permute-start.17) | collective-permute-done | bytes 1572896 | tf_op jit(solution)/shard_map/ppermute | solution.py:479
  122.8 3.3 %collective-permute-done.19.refs_3_ = bf16[4,2,128,128]{3,2,1,0:T(8,128)(2,1)S(1)} collective-permute-done((bf16[4,2,128,128]{3,2,1,0:T(8,128)(2,1)S(1)}, bf16[4,2,128,128]{3,2,1,0:T(8,128)(2,1)S(1)}, u32[]{:S(2)}, u32[]{:S(2)}) %collective-permute-start.19) | collective-permute-done | bytes 262176 | tf_op jit(solution)/shard_map/ppermute | solution.py:478
  126.8 17.3 %shard_map.137 = (bf16[128,2560]{1,0:T(8,128)(2,1)}, bf16[128,2560]{1,0:T(8,128)(2,1)}) custom-call(s32[23]{0:T(128)} %concatenate.10.m, bf16[2,128,3072]{2,1,0:T(8,128)(2,1)} %get-tuple-element.64.refs_0_, bf16[2,128,3072]{2,1,0:T(8,128)(2,1)} %copy-done.15, bf16[4,2,128,128]{3,2,1,0:T(8,128)(2,1)} %shard_map.135.refs_25_.refs_2_, ...), custom_call_target="tpu_custom_call" | custom-call | flops 1000 | bytes 1000 | tf_op jit(solution)/shard_map/pallas_call | solution.py:47
  145.9 16.0 %collective-permute-done.20.refs_1_ = bf16[256,128]{1,0:T(8,128)(2,1)S(1)} collective-permute-done((bf16[256,128]{1,0:T(8,128)(2,1)S(1)}, bf16[256,128]{1,0:T(8,128)(2,1)S(1)}, u32[]{:S(2)}, u32[]{:S(2)}) %collective-permute-start.20) | collective-permute-done | bytes 65568 | tf_op jit(solution)/shard_map/ppermute | solution.py:488
  165.9 17.4 %shard_map.139 = (bf16[128,2560]{1,0:T(8,128)(2,1)}, bf16[128,2560]{1,0:T(8,128)(2,1)}) custom-call(s32[23]{0:T(128)} %concatenate.10.m, bf16[2,128,3072]{2,1,0:T(8,128)(2,1)} %get-tuple-element.65.refs_0_, bf16[2,128,3072]{2,1,0:T(8,128)(2,1)} %copy-done.14, bf16[4,2,128,128]{3,2,1,0:T(8,128)(2,1)} %shard_map.135.refs_25_.refs_2_, ...), custom_call_target="tpu_custom_call" | custom-call | flops 1000 | bytes 1000 | tf_op jit(solution)/shard_map/pallas_call | solution.py:47
  184.7 3.6 %collective-permute-done.23.refs_1_ = bf16[256,128]{1,0:T(8,128)(2,1)S(1)} collective-permute-done((bf16[256,128]{1,0:T(8,128)(2,1)S(1)}, bf16[256,128]{1,0:T(8,128)(2,1)S(1)}, u32[]{:S(2)}, u32[]{:S(2)}) %collective-permute-start.23) | collective-permute-done | bytes 65568 | tf_op jit(solution)/shard_map/ppermute | solution.py:491
  197.9 17.3 %shard_map.142 = (bf16[128,2560]{1,0:T(8,128)(2,1)}, bf16[128,2560]{1,0:T(8,128)(2,1)}) custom-call(s32[23]{0:T(128)} %concatenate.10.m, bf16[2,128,3072]{2,1,0:T(8,128)(2,1)} %get-tuple-element.77.refs_0_, bf16[2,128,3072]{2,1,0:T(8,128)(2,1)} %collective-permute-done.27.refs_1_, bf16[4,2,128,128]{3,2,1,0:T(8,128)(2,1)} %shard_map.135.refs_25_.refs_2_, ...), custom_call_target="tpu_custom_call" | custom-call | flops 1000 | bytes 1000 | tf_op jit(solution)/shard_map/pallas_call | solution.py:47
  221.8 3.1 %shard_map.145.refs_6_ = bf16[128,2560]{1,0:T(8,128)(2,1)} custom-call(s32[23]{0:T(128)} %concatenate.10.m, bf16[128,2560]{1,0:T(8,128)(2,1)} %shard_map.141.refs_6_.refs_0_, bf16[128,2560]{1,0:T(8,128)(2,1)} %collective-permute-done.24.refs_1_, bf16[128,2560]{1,0:T(8,128)(2,1)} %shard_map.144.refs_2_.refs_0_), custom_call_target="tpu_custom_call" | custom-call | flops 1000 | bytes 1000 | tf_op jit(solution)/shard_map/pallas_call | solution.py:47
  225.6 5.8 %collective-permute-start.32 = (bf16[128,2560]{1,0:T(8,128)(2,1)S(1)}, bf16[128,2560]{1,0:T(8,128)(2,1)S(1)}, u32[]{:S(2)}, u32[]{:S(2)}) collective-permute-start(bf16[128,2560]{1,0:T(8,128)(2,1)S(1)} %copy-done.8), channel_id=1, source_target_pairs={{0,4},{2,6},{12,8},{14,10},{1,5},{3,7},{13,9},{15,11},{16,20},{18,... | collective-permute-start | bytes 1966088 | tf_op jit(solution)/shard_map/ppermute | solution.py:501
  232.6 17.3 %shard_map.146 = (bf16[128,2560]{1,0:T(8,128)(2,1)}, bf16[128,2560]{1,0:T(8,128)(2,1)}) custom-call(s32[23]{0:T(128)} %concatenate.10.m, bf16[2,128,3072]{2,1,0:T(8,128)(2,1)} %get-tuple-element.70.refs_0_, bf16[2,128,3072]{2,1,0:T(8,128)(2,1)} %copy-done.13, bf16[4,2,128,128]{3,2,1,0:T(8,128)(2,1)} %shard_map.135.refs_25_.refs_2_, ...), custom_call_target="tpu_custom_call" | custom-call | flops 1000 | bytes 1000 | tf_op jit(solution)/shard_map/pallas_call | solution.py:47
  252.4 3.2 %shard_map.147.refs_2_ = bf16[128,2560]{1,0:T(8,128)(2,1)} custom-call(s32[23]{0:T(128)} %concatenate.10.m, bf16[128,2560]{1,0:T(8,128)(2,1)} %get-tuple-element.81.refs_0_, bf16[128,2560]{1,0:T(8,128)(2,1)} %copy-done.21, bf16[128,2560]{1,0:T(8,128)(2,1)} %copy-done.25, bf16[128,2560]{1,0:T(8,128)(2,1)} %get-tuple-element.80.refs_3_), custom_call_target="tpu_custom_call" | custom-call | flops 1000 | bytes 1000 | tf_op jit(solution)/shard_map/pallas_call | solution.py:47
  261.4 6.9 %shard_map.149 = (bf16[3,64,3200]{2,1,0:T(8,128)(2,1)}, bf16[3,64,3200]{2,1,0:T(8,128)(2,1)}) custom-call(s32[23]{0:T(128)} %concatenate.10.m, bf16[256,128]{1,0:T(8,128)(2,1)} %shard_map.134.refs_18_.refs_0_, bf16[512,3200]{1,0:T(8,128)(2,1)} %get-tuple-element.82.refs_1_, bf16[128,2560]{1,0:T(8,128)(2,1)} %shard_map.148.refs_2_), custom_call_target="tpu_custom_call" | custom-call | flops 1000 | bytes 1000 | tf_op jit(solution)/shard_map/pallas_call | solution.py:47
  273.8 4.0 %shard_map.151 = (bf16[3,64,640]{2,1,0:T(8,128)(2,1)}, bf16[3,64,640]{2,1,0:T(8,128)(2,1)}) custom-call(s32[23]{0:T(128)} %concatenate.10.m, bf16[256,128]{1,0:T(8,128)(2,1)} %shard_map.143.refs_2_.refs_0_, bf16[512,640]{1,0:T(8,128)(2,1)} %shard_map.150.refs_1_), custom_call_target="tpu_custom_call" | custom-call | flops 1000 | bytes 1000 | tf_op jit(solution)/shard_map/pallas_call | solution.py:47
  279.2 3.4 %shard_map.152 = (bf16[64,2560]{1,0:T(8,128)(2,1)}, bf16[64,2560]{1,0:T(8,128)(2,1)}) custom-call(s32[23]{0:T(128)} %concatenate.10.m, bf16[128,2560]{1,0:T(8,128)(2,1)} %get-tuple-element.79.refs_0_, bf16[128,2560]{1,0:T(8,128)(2,1)} %copy-done.20, bf16[128,2560]{1,0:T(8,128)(2,1)} %copy-done.23, bf16[128,2560]{1,0:T(8,128)(2,1)} %copy-done.22, ...), custom_call_target="tpu_custom_call" | custom-call | flops 1000 | bytes 1000 | tf_op jit(solution)/shard_map/pallas_call | solution.py:47
  287.6 3.3 %shard_map.153 = bf16[192,3200]{1,0:T(8,128)(2,1)} custom-call(s32[23]{0:T(128)} %concatenate.10.m, bf16[192,3200]{1,0:T(8,128)(2,1)} %bitcast.25, bf16[192,3200]{1,0:T(8,128)(2,1)} %bitcast.26, bf16[64,2560]{1,0:T(8,128)(2,1)} %get-tuple-element.86.refs_2_), custom_call_target="tpu_custom_call" | custom-call | flops 1000 | bytes 1000 | tf_op jit(solution)/shard_map/pallas_call | solution.py:47
  (167 shorter events, 82.7 us)
Async XLA Ops:
  0.6 44.7 %collective-permute-start.11 = (bf16[2560,3200]{1,0:T(8,128)(2,1)}, bf16[2560,3200]{1,0:T(8,128)(2,1)}, u32[]{:S(2)}, u32[]{:S(2)}) collective-permute-start(bf16[2560,3200]{1,0:T(8,128)(2,1)} %refs_23_.3), channel_id=1, source_target_pairs={{0,1},{1,0},{2,3},{3,2},{4,5},{5,4},{6,7},{7,6},{8,9},{9,8},{10,11... | collective-permute-start | bytes 49152008 | tf_op jit(solution)/shard_map/ppermute | solution.py:451
  0.8 21.2 %collective-permute-start.1 = (bf16[64,5120]{1,0:T(8,128)(2,1)}, bf16[64,5120]{1,0:T(8,128)(2,1)S(1)}, u32[]{:S(2)}, u32[]{:S(2)}) collective-permute-start(bf16[64,5120]{1,0:T(8,128)(2,1)} %refs_0_.11), channel_id=1, source_target_pairs={{0,4},{2,6},{4,0},{6,2},{8,12},{10,14},{12,8},{14,10},{1,5},{3,7},... | collective-permute-start | bytes 1966088 | tf_op jit(solution)/shard_map/ppermute | solution.py:452
  3.5 18.4 %collective-permute-start = (bf16[64,5120]{1,0:T(8,128)(2,1)}, bf16[64,5120]{1,0:T(8,128)(2,1)S(1)}, u32[]{:S(2)}, u32[]{:S(2)}) collective-permute-start(bf16[64,5120]{1,0:T(8,128)(2,1)} %refs_0_.11), channel_id=1, source_target_pairs={{0,2},{2,0},{4,6},{6,4},{8,10},{10,8},{12,14},{14,12},{1,3},{3,1},... | collective-permute-start | bytes 1966088 | tf_op jit(solution)/shard_map/ppermute | solution.py:454
  4.8 18.2 %collective-permute-start.4 = (bf16[64,5120]{1,0:T(8,128)(2,1)}, bf16[64,5120]{1,0:T(8,128)(2,1)S(1)}, u32[]{:S(2)}, u32[]{:S(2)}) collective-permute-start(bf16[64,5120]{1,0:T(8,128)(2,1)} %refs_0_.11), channel_id=1, source_target_pairs={{4,8},{6,10},{8,4},{10,6},{5,9},{7,11},{9,5},{11,7},{20,24},{22,26... | collective-permute-start | bytes 1966088 | tf_op jit(solution)/shard_map/ppermute | solution.py:453
  22.3 17.1 %collective-permute-start.9 = (bf16[64,5120]{1,0:T(8,128)(2,1)S(1)}, bf16[64,5120]{1,0:T(8,128)(2,1)S(1)}, u32[]{:S(2)}, u32[]{:S(2)}) collective-permute-start(bf16[64,5120]{1,0:T(8,128)(2,1)S(1)} %collective-permute-done.1.refs_2_.refs_10_), channel_id=1, source_target_pairs={{4,8},{6,10},{8,4},{10,6},{5,9},{7,11},{9,5},{11,7},{20,24},{22,26... | collective-permute-start | bytes 1966088 | tf_op jit(solution)/shard_map/ppermute | solution.py:461
  23.0 18.3 %collective-permute-start.5 = (bf16[64,5120]{1,0:T(8,128)(2,1)S(1)}, bf16[64,5120]{1,0:T(8,128)(2,1)}, u32[]{:S(2)}, u32[]{:S(2)}) collective-permute-start(bf16[64,5120]{1,0:T(8,128)(2,1)S(1)} %collective-permute-done.4), channel_id=1, source_target_pairs={{4,0},{6,2},{8,12},{10,14},{5,1},{7,3},{9,13},{11,15},{20,16},{22,... | collective-permute-start | bytes 1966088 | tf_op jit(solution)/shard_map/ppermute | solution.py:462
  24.3 19.9 %collective-permute-start.6 = (bf16[64,640]{1,0:T(8,128)(2,1)S(1)}, bf16[64,640]{1,0:T(8,128)(2,1)S(1)}, u32[]{:S(2)}, u32[]{:S(2)}) collective-permute-start(bf16[64,640]{1,0:T(8,128)(2,1)S(1)} %copy-done.28), channel_id=1, source_target_pairs={{0,8},{2,10},{4,12},{6,14},{8,0},{10,2},{12,4},{14,6},{1,9},{3,11}... | collective-permute-start | bytes 245768 | tf_op jit(solution)/shard_map/ppermute | solution.py:458
  39.4 18.4 %collective-permute-start.10 = (bf16[64,5120]{1,0:T(8,128)(2,1)S(1)}, bf16[64,5120]{1,0:T(8,128)(2,1)S(1)}, u32[]{:S(2)}, u32[]{:S(2)}) collective-permute-start(bf16[64,5120]{1,0:T(8,128)(2,1)S(1)} %collective-permute-done.9), channel_id=1, source_target_pairs={{4,0},{6,2},{8,12},{10,14},{5,1},{7,3},{9,13},{11,15},{20,16},{22,... | collective-permute-start | bytes 1966088 | tf_op jit(solution)/shard_map/ppermute | solution.py:465
  44.2 17.2 %collective-permute-start.8 = (bf16[64,5120]{1,0:T(8,128)(2,1)S(1)}, bf16[64,5120]{1,0:T(8,128)(2,1)S(1)}, u32[]{:S(2)}, u32[]{:S(2)}) collective-permute-start(bf16[64,5120]{1,0:T(8,128)(2,1)S(1)} %broadcast_select_fusion.1.refs_4_.refs_12_), channel_id=1, source_target_pairs={{0,2},{2,0},{4,6},{6,4},{8,10},{10,8},{12,14},{14,12},{1,3},{3,1},... | collective-permute-start | bytes 1966088 | tf_op jit(solution)/shard_map/ppermute | solution.py:464
  122.3 42.4 %collective-permute-start.18 = (bf16[2,128,3072]{2,1,0:T(8,128)(2,1)}, bf16[2,128,3072]{2,1,0:T(8,128)(2,1)S(1)}, u32[]{:S(2)}, u32[]{:S(2)}) collective-permute-start(bf16[2,128,3072]{2,1,0:T(8,128)(2,1)} %get-tuple-element.65.refs_0_), channel_id=1, source_target_pairs={{0,1},{1,0},{2,3},{3,2},{4,5},{5,4},{6,7},{7,6},{8,9},{9,8},{10,11... | collective-permute-start | bytes 4718600 | tf_op jit(solution)/shard_map/ppermute | solution.py:480
  144.1 53.8 %collective-permute-start.27 = (bf16[2,128,3072]{2,1,0:T(8,128)(2,1)S(1)}, bf16[2,128,3072]{2,1,0:T(8,128)(2,1)}, u32[]{:S(2)}, u32[]{:S(2)}) collective-permute-start(bf16[2,128,3072]{2,1,0:T(8,128)(2,1)S(1)} %copy-done.12), channel_id=1, source_target_pairs={{0,1},{1,0},{2,3},{3,2},{4,5},{5,4},{6,7},{7,6},{8,9},{9,8},{10,11... | collective-permute-start | bytes 4718600 | tf_op jit(solution)/shard_map/ppermute | solution.py:497
  144.3 46.8 %collective-permute-start.22 = (bf16[128,2560]{1,0:T(8,128)(2,1)}, bf16[128,2560]{1,0:T(8,128)(2,1)S(1)}, u32[]{:S(2)}, u32[]{:S(2)}) collective-permute-start(bf16[128,2560]{1,0:T(8,128)(2,1)} %get-tuple-element.67.refs_2_), channel_id=1, source_target_pairs={{0,2},{2,0},{4,6},{6,4},{8,10},{10,8},{12,14},{14,12},{1,3},{3,1},... | collective-permute-start | bytes 1966088 | tf_op jit(solution)/shard_map/ppermute | solution.py:486
  144.3 17.5 %collective-permute-start.20 = (bf16[256,128]{1,0:T(8,128)(2,1)S(1)}, bf16[256,128]{1,0:T(8,128)(2,1)S(1)}, u32[]{:S(2)}, u32[]{:S(2)}) collective-permute-start(bf16[256,128]{1,0:T(8,128)(2,1)S(1)} %convert_element_type.12), channel_id=1, source_target_pairs={{0,2},{2,0},{4,6},{6,4},{8,10},{10,8},{12,14},{14,12},{1,3},{3,1},... | collective-permute-start | bytes 196616 | tf_op jit(solution)/shard_map/ppermute | solution.py:488
  183.4 48.0 %collective-permute-start.21 = (bf16[2,128,3072]{2,1,0:T(8,128)(2,1)S(1)}, bf16[2,128,3072]{2,1,0:T(8,128)(2,1)S(1)}, u32[]{:S(2)}, u32[]{:S(2)}) collective-permute-start(bf16[2,128,3072]{2,1,0:T(8,128)(2,1)S(1)} %copy-done.11), channel_id=1, source_target_pairs={{0,1},{1,0},{2,3},{3,2},{4,5},{5,4},{6,7},{7,6},{8,9},{9,8},{10,11... | collective-permute-start | bytes 4718600 | tf_op jit(solution)/shard_map/ppermute | solution.py:504
  184.6 33.4 %collective-permute-start.25 = (bf16[128,2560]{1,0:T(8,128)(2,1)}, bf16[128,2560]{1,0:T(8,128)(2,1)S(1)}, u32[]{:S(2)}, u32[]{:S(2)}) collective-permute-start(bf16[128,2560]{1,0:T(8,128)(2,1)} %get-tuple-element.69.refs_2_), channel_id=1, source_target_pairs={{0,2},{2,0},{4,6},{6,4},{8,10},{10,8},{12,14},{14,12},{1,3},{3,1},... | collective-permute-start | bytes 1966088 | tf_op jit(solution)/shard_map/ppermute | solution.py:486
  194.9 26.9 %collective-permute-start.24 = (bf16[128,2560]{1,0:T(8,128)(2,1)}, bf16[128,2560]{1,0:T(8,128)(2,1)}, u32[]{:S(2)}, u32[]{:S(2)}) collective-permute-start(bf16[128,2560]{1,0:T(8,128)(2,1)} %shard_map.141.refs_6_.refs_0_), channel_id=1, source_target_pairs={{0,4},{2,6},{12,8},{14,10},{1,5},{3,7},{13,9},{15,11},{16,20},{18,... | collective-permute-start | bytes 1966088 | tf_op jit(solution)/shard_map/ppermute | solution.py:496
  197.9 17.3 %collective-permute-start.26 = (bf16[256,128]{1,0:T(8,128)(2,1)S(1)}, bf16[256,128]{1,0:T(8,128)(2,1)S(1)}, u32[]{:S(2)}, u32[]{:S(2)}) collective-permute-start(bf16[256,128]{1,0:T(8,128)(2,1)S(1)} %copy-done.33), channel_id=1, source_target_pairs={{0,8},{2,10},{4,12},{6,14},{8,0},{10,2},{12,4},{14,6},{1,9},{3,11}... | collective-permute-start | bytes 196616 | tf_op jit(solution)/shard_map/ppermute | solution.py:494
  215.2 36.1 %collective-permute-start.29 = (bf16[128,2560]{1,0:T(8,128)(2,1)}, bf16[128,2560]{1,0:T(8,128)(2,1)S(1)}, u32[]{:S(2)}, u32[]{:S(2)}) collective-permute-start(bf16[128,2560]{1,0:T(8,128)(2,1)} %get-tuple-element.78.refs_2_), channel_id=1, source_target_pairs={{0,2},{2,0},{4,6},{6,4},{8,10},{10,8},{12,14},{14,12},{1,3},{3,1},... | collective-permute-start | bytes 1966088 | tf_op jit(solution)/shard_map/ppermute | solution.py:486
  224.9 26.5 %collective-permute-start.30 = (bf16[128,2560]{1,0:T(8,128)(2,1)}, bf16[128,2560]{1,0:T(8,128)(2,1)S(1)}, u32[]{:S(2)}, u32[]{:S(2)}) collective-permute-start(bf16[128,2560]{1,0:T(8,128)(2,1)} %shard_map.145.refs_6_), channel_id=1, source_target_pairs={{4,8},{6,10},{8,4},{10,6},{5,9},{7,11},{9,5},{11,7},{20,24},{22,26... | collective-permute-start | bytes 1966088 | tf_op jit(solution)/shard_map/ppermute | solution.py:503
  225.6 30.0 %collective-permute-start.32 = (bf16[128,2560]{1,0:T(8,128)(2,1)S(1)}, bf16[128,2560]{1,0:T(8,128)(2,1)S(1)}, u32[]{:S(2)}, u32[]{:S(2)}) collective-permute-start(bf16[128,2560]{1,0:T(8,128)(2,1)S(1)} %copy-done.8), channel_id=1, source_target_pairs={{0,4},{2,6},{12,8},{14,10},{1,5},{3,7},{13,9},{15,11},{16,20},{18,... | collective-permute-start | bytes 1966088 | tf_op jit(solution)/shard_map/ppermute | solution.py:501
  249.9 28.0 %collective-permute-start.28 = (bf16[128,2560]{1,0:T(8,128)(2,1)}, bf16[128,2560]{1,0:T(8,128)(2,1)S(1)}, u32[]{:S(2)}, u32[]{:S(2)}) collective-permute-start(bf16[128,2560]{1,0:T(8,128)(2,1)} %get-tuple-element.80.refs_3_), channel_id=1, source_target_pairs={{0,2},{2,0},{4,6},{6,4},{8,10},{10,8},{12,14},{14,12},{1,3},{3,1},... | collective-permute-start | bytes 1966088 | tf_op jit(solution)/shard_map/ppermute | solution.py:486
  259.4 18.5 %collective-permute-start.33 = (bf16[128,2560]{1,0:T(8,128)(2,1)}, bf16[128,2560]{1,0:T(8,128)(2,1)S(1)}, u32[]{:S(2)}, u32[]{:S(2)}) collective-permute-start(bf16[128,2560]{1,0:T(8,128)(2,1)} %shard_map.148.refs_2_), channel_id=1, source_target_pairs={{4,8},{6,10},{8,4},{10,6},{5,9},{7,11},{9,5},{11,7},{20,24},{22,26... | collective-permute-start | bytes 1966088 | tf_op jit(solution)/shard_map/ppermute | solution.py:509
  260.1 17.8 %collective-permute-start.31 = (bf16[128,2560]{1,0:T(8,128)(2,1)S(1)}, bf16[128,2560]{1,0:T(8,128)(2,1)S(1)}, u32[]{:S(2)}, u32[]{:S(2)}) collective-permute-start(bf16[128,2560]{1,0:T(8,128)(2,1)S(1)} %copy-done.10), channel_id=1, source_target_pairs={{0,4},{2,6},{4,0},{6,2},{8,12},{10,14},{12,8},{14,10},{1,5},{3,7},... | collective-permute-start | bytes 1966088 | tf_op jit(solution)/shard_map/ppermute | solution.py:507
  268.3 18.3 %collective-permute-start.35 = (bf16[3,64,3200]{2,1,0:T(8,128)(2,1)}, bf16[3,64,3200]{2,1,0:T(8,128)(2,1)S(1)}, u32[]{:S(2)}, u32[]{:S(2)}) collective-permute-start(bf16[3,64,3200]{2,1,0:T(8,128)(2,1)} %get-tuple-element.87), channel_id=1, source_target_pairs={{0,1},{1,0},{2,3},{3,2},{4,5},{5,4},{6,7},{7,6},{8,9},{9,8},{10,11... | collective-permute-start | bytes 3686408 | tf_op jit(solution)/shard_map/ppermute | solution.py:519
  (54 other events, 423.8 us)

commit v4 on v1

--- a/solution.py
+++ b/solution.py
@@ -36,7 +36,7 @@
 
 
 def call(
-    kernel, meta, args, grid, in_specs, out_specs, out_shape, scratch=(), flops=0, nbytes=0, vmem=48, after=()
+    kernel, meta, args, grid, in_specs, out_specs, out_shape, scratch=(), vmem=48, after=(), cost=(1000, 1000)
 ):
     first, extra = len(args), len(after)
 
@@ -54,7 +54,7 @@
         ),
         out_shape=out_shape,
         compiler_params=pltpu.CompilerParams(vmem_limit_bytes=vmem * MIB),
-        cost_estimate=pl.CostEstimate(flops=flops, bytes_accessed=nbytes, transcendentals=0),
+        cost_estimate=pl.CostEstimate(flops=cost[0], bytes_accessed=cost[1], transcendentals=0),
     )(meta, *args, *after)
 
 
@@ -97,13 +97,12 @@
             jax.ShapeDtypeStruct((rows, width), BF16),
             jax.ShapeDtypeStruct((rows // 2, 2 * rank), F32),
         ],
-        flops=2 * rows * width * rank * 2,
-        nbytes=8 * rows * width,
     )
 
 
 def low_out_kernel(m, *refs):
-    shards, b_ref, cols_ref, low_ref = refs[:8], refs[8], refs[9], refs[10]
+    shards, b_ref, low_in_ref = refs[:8], refs[8], refs[9]
+    cols_ref, full_ref, short_ref = refs[10:]
     rows = shards[0].shape[0]
     y = m[M_Y]
     for s in range(4):
@@ -113,30 +112,33 @@
         second = jnp.where(y == 0, other, own)
         tokens = jnp.concatenate([first, second], axis=0)
         cols_ref[pl.ds(pl.multiple_of(z * 2 * rows, 2 * rows), 2 * rows), :] = tokens
-        part = nt_dot(tokens, b_ref[m[M_SLOT_ADAPTER + s]])
-        low_ref[pl.ds(pl.multiple_of(z * rows, rows), rows), :] = pack_halves(part)
-
-
-def low_out_parts(meta, shards, b, after):
+        part = pack_halves(nt_dot(tokens, b_ref[m[M_SLOT_ADAPTER + s]]))
+        at = pl.ds(pl.multiple_of(z * rows, rows), rows)
+        full_ref[at, :] = part
+        short_ref[at, :] = part.astype(BF16)
+    full_ref[4 * rows :] = low_in_ref[...]
+    short_ref[4 * rows :] = low_in_ref[...].astype(BF16)
+
+
+def low_parts(meta, shards, b, low_in, after):
     rows = shards[0].shape[0]
     adapters, rank, columns = b.shape
+    out = (8 * rows, 2 * rank)
     return call(
         low_out_kernel,
         meta,
-        (*shards, b),
+        (*shards, b, low_in),
         (1,),
         [pl.BlockSpec((rows, columns), lambda i, m: (0, m[M_T]))] * 8
-        + [pl.BlockSpec((adapters, rank, columns), lambda i, m: (0, 0, 0))],
-        [
-            pl.BlockSpec((8 * rows, columns), lambda i, m: (0, 0)),
-            pl.BlockSpec((4 * rows, 2 * rank), lambda i, m: (0, 0)),
-        ],
+        + [pl.BlockSpec((adapters, rank, columns), lambda i, m: (0, 0, 0))]
+        + [pl.BlockSpec((4 * rows, 2 * rank), lambda i, m: (0, 0))],
+        [pl.BlockSpec((8 * rows, columns), lambda i, m: (0, 0))]
+        + [pl.BlockSpec(out, lambda i, m: (0, 0))] * 2,
         [
             jax.ShapeDtypeStruct((8 * rows, columns), BF16),
-            jax.ShapeDtypeStruct((4 * rows, 2 * rank), F32),
+            jax.ShapeDtypeStruct(out, F32),
+            jax.ShapeDtypeStruct(out, BF16),
         ],
-        flops=2 * 8 * rows * columns * rank,
-        nbytes=4 * 8 * rows * columns,
         after=after,
     )
 
@@ -173,8 +175,6 @@
         pl.BlockSpec((total, step), lambda n, m: (0, n)),
         jax.ShapeDtypeStruct((total, width), F32),
         scratch=[pltpu.VMEM((2, total, half), BF16)],
-        flops=2 * total * 2 * half * width,
-        nbytes=2 * 2 * half * width,
         after=after,
     )
 
@@ -218,8 +218,6 @@
         ],
         pl.BlockSpec((2, rows, width), lambda j, m: (0, j, 0)),
         jax.ShapeDtypeStruct((2, 2 * rows, width), BF16),
-        flops=2 * 2 * rows * width * rank,
-        nbytes=2 * rows * width * 12,
         after=after,
     )
 
@@ -254,45 +252,51 @@
         [pl.BlockSpec((rows, step), lambda n, m: (0, n))] * 2,
         [out, out],
         scratch=[pltpu.VMEM((2, 2 * rows, width), BF16)],
-        flops=2 * 2 * rows * 2 * width * half,
-        nbytes=2 * 2 * width * half,
         after=after,
     )
 
 
-def owner_kernel(blocks, m, low_ref, features_ref, keep_ref, send_ref):
-    i = pl.program_id(0)
+def owner_kernel(m, low_ref, features_ref, keep_ref, send_ref, lhs):
+    owned, rank = keep_ref.shape[:2]
+    blocks = features_ref.shape[0] // BLOCK
+    rows = low_ref.shape[0] // blocks
     d = m[M_D]
-    owned = keep_ref.shape[0] * pl.num_programs(0)
-    rows = low_ref.shape[0] // blocks
-    for ref, owner in ((keep_ref, d), (send_ref, 1 - d)):
-        slot = owner * owned + i
-        total = jnp.zeros(ref.shape[1:], F32)
+
+    @pl.when(pl.program_id(0) == 0)
+    def _():
         for b in range(blocks):
-            hit = jnp.where(m[M_GRAD_SLOT + b] == slot, ADAPTER_SCALE, 0.0)
             low = unpack_halves(low_ref[b * rows : (b + 1) * rows, :])
-            total += hit * tn_dot(low, features_ref[b * BLOCK : (b + 1) * BLOCK, :])
-        ref[0] = total.astype(BF16)
-
-
-def owner_grads(meta, low, features, owned, after=()):
+            masked = []
+            for owner in (d, 1 - d):
+                for i in range(owned):
+                    hit = m[M_GRAD_SLOT + b] == owner * owned + i
+                    masked.append(jnp.where(hit, low, jnp.zeros_like(low)))
+            lhs[b * BLOCK : (b + 1) * BLOCK] = jnp.concatenate(masked, axis=1)
+
+    total = (ADAPTER_SCALE * tn_dot(lhs[...], features_ref[...])).astype(BF16)
+    for i in range(owned):
+        keep_ref[i] = total[i * rank : (i + 1) * rank]
+        send_ref[i] = total[(owned + i) * rank : (owned + i + 1) * rank]
+
+
+def owner_grads(meta, low, which, features, owned, after=()):
     tokens, width = features.shape
-    half_rows, double = low.shape
+    half_rows, double = low.shape[0] // 2, low.shape[1]
     rank = double // 2
+    step = 640
     out = jax.ShapeDtypeStruct((owned, rank, width), BF16)
     return call(
-        functools.partial(owner_kernel, tokens // BLOCK),
+        owner_kernel,
         meta,
         (low, features),
-        (owned,),
+        (width // step,),
         [
-            pl.BlockSpec((half_rows, double), lambda i, m: (0, 0)),
-            pl.BlockSpec((tokens, width), lambda i, m: (0, 0)),
+            pl.BlockSpec((half_rows, double), lambda n, m: (which, 0)),
+            pl.BlockSpec((tokens, step), lambda n, m: (0, n)),
         ],
-        [pl.BlockSpec((1, rank, width), lambda i, m: (i, 0, 0))] * 2,
+        [pl.BlockSpec((owned, rank, step), lambda n, m: (0, 0, n))] * 2,
         [out, out],
-        flops=2 * tokens * rank * width * 2 * owned,
-        nbytes=2 * tokens * width,
+        scratch=[pltpu.VMEM((tokens, 2 * owned * rank), BF16)],
         after=after,
     )
 
@@ -316,11 +320,34 @@
         [spec] * len(xs),
         [spec] * len(kinds),
         [jax.ShapeDtypeStruct((rows, width), k) for k in kinds],
-        nbytes=2 * rows * width * (len(xs) + 1),
         vmem=16,
         after=after,
     )
     return out if len(kinds) > 1 else out[0]
+
+
+def final_kernel(m, *refs):
+    total = refs[0][...].astype(F32)
+    for r in refs[1:-2]:
+        total += r[...].astype(F32)
+    rows = refs[-1].shape[0]
+    refs[-2][...] = total[:rows].astype(BF16)
+    refs[-1][...] = total[rows:].astype(BF16)
+
+
+def final_sum(meta, xs, after):
+    rows, width = xs[0].shape
+    return call(
+        final_kernel,
+        meta,
+        xs,
+        (1,),
+        [pl.BlockSpec((rows, width), lambda i, m: (0, 0))] * len(xs),
+        [pl.BlockSpec((rows // 2, width), lambda i, m: (0, 0))] * 2,
+        [jax.ShapeDtypeStruct((rows // 2, width), BF16)] * 2,
+        vmem=16,
+        after=after,
+    )
 
 
 def add(*xs):
@@ -374,7 +401,7 @@
 
     width = gate_act.shape[1]
     step = width * 2 // 5
-    spans = ((0, step, step // 5), (step, step, step // 5), (2 * step, width - 2 * step, width - 2 * step))
+    spans = ((0, step, step // 2), (step, step, step // 2), (2 * step, width - 2 * step, width - 2 * step))
 
     down_other = swap_cores(down_matrix)
     pair = send(cotangent, perm=PAIR)
@@ -395,60 +422,59 @@
     y3 = send(tied(slot3, y2), perm=Y_SWAP)
 
     far = (slot2, y2, slot3, y3)
-    columns, low_part = low_out_parts(meta, (cotangent, y0, pair, y1, *far), adapter_output_factor, last)
+    near = (cotangent, y0, pair, y1)
+    columns, low_sum, low = low_parts(meta, near + far, adapter_output_factor, low_in, last)
     hg_far = []
-    low_sum, low_out = low_part, low_part.astype(BF16)
     for perm, span in zip((Y_SWAP, PAIR, FAR), spans):
-        got = send(low_out, perm=perm)
-        hg_far.append(hidden_grad(meta, far, down_matrix, down_other, span, (low_out,)))
-        low_sum, low_out = add_after(meta, (low_sum, got), (hg_far[-1],), (F32, BF16))
+        got = send(low, perm=perm)
+        hg_far.append(hidden_grad(meta, far, down_matrix, down_other, span, (low,)))
+        low_sum, low = add_after(meta, (low_sum, got), (hg_far[-1],), (F32, BF16))
 
     def grads(slot, after):
         hgs = hg_far if slot >= 2 else hg_near
-        return act_grad(meta, slot, spans, hgs, gate_act, up_act, low_out, a_t, after)
+        return act_grad(meta, slot, spans, hgs, gate_act, up_act, low, a_t, after)
 
     def parts(mine, other, after):
         keep, give = input_grad_parts(meta, mine, other, gate_matrix, up_matrix, after)
         return keep, send(give, perm=Y_SWAP), give
 
     mine3 = grads(3, ())
-    low_in1 = low_in.astype(BF16)
-    got_in = send(low_in1, perm=Y_SWAP)
     other3 = swap_cores(mine3)
     mine2 = grads(2, (mine3,))
-    other2 = swap_cores(mine2)
-    low_in2, low_in2b = add_after(meta, (low_in, got_in), (mine2,), (F32, BF16))
-    got_in = send(low_in2b, perm=PAIR)
-    keep3, got3, give3 = parts(mine3, other3, (low_in2b,))
+    other2 = swap_cores(tied(mine2, other3))
+    keep3, got3, give3 = parts(mine3, other3, (mine2,))
     mine1 = grads(1, (give3,))
-    other1 = swap_cores(mine1)
-    low_in3, low_in3b = add_after(meta, (low_in2, got_in), (mine1,), (F32, BF16))
-    got_in = send(low_in3b, perm=FAR)
-    keep2, got2, give2 = parts(mine2, other2, (low_in3b,))
-    mine0 = grads(0, (give2,))
-    other0 = swap_cores(mine0)
-    sum3 = add_after(meta, (keep3, got3), (mine0,))
+    keep2, got2, give2 = parts(mine2, other2, (mine1,))
+    other1 = swap_cores(tied(mine1, other2))
+    sum3 = add_after(meta, (keep3, got3), (give2,))
     far_in = send(sum3, perm=INWARD)
-    keep1, got1, give1 = parts(mine1, other1, (sum3,))
+    mine0 = grads(0, (sum3,))
+    keep1, got1, give1 = parts(mine1, other1, (mine0,))
+    other0 = swap_cores(tied(mine0, other1))
     sum2 = add_after(meta, (keep2, got2), (give1,))
     mid_in = send(sum2, perm=INWARD)
-    far_mid = send(add_after(meta, (sum3, far_in), (sum2,)), perm=MID)
-    low_in4 = add_after(meta, (low_in3, got_in), (sum2,))
-    keep0, got0, give0 = parts(mine0, other0, (low_in4, sum2))
-    from_mid = send(add_after(meta, (sum2, mid_in), (give0,)), perm=MID)
-    from_pair = send(add_after(meta, (keep1, got1, far_mid), (give0,)), perm=PAIR)
+    sum3 = add_after(meta, (sum3, far_in), (sum2,))
+    far_mid = send(sum3, perm=MID)
+    keep0, got0, give0 = parts(mine0, other0, (sum3,))
+    sum1 = add_after(meta, (keep1, got1, far_mid), (give0,))
+    from_pair = send(sum1, perm=PAIR)
+    sum2 = add_after(meta, (sum2, mid_in), (sum1,))
+    from_mid = send(sum2, perm=MID)
     owned = adapters // 2
-    keep_a, give_a = owner_grads(meta, low_out, hidden, owned, (give0,))
-    keep_b, give_b = owner_grads(meta, low_in4, columns, owned, (keep_a,))
-    grad_a = jnp.swapaxes(add(keep_a, swap_cores(give_a)), 1, 2)
+    keep_a, give_a = owner_grads(meta, low, 0, hidden, owned, (sum2,))
+    keep_b, give_b = owner_grads(meta, low, 1, columns, owned, (keep_a,))
+    own, give = final_sum(meta, (keep0, got0, from_pair, from_mid), (keep_b,))
     grad_b = add(keep_b, swap_cores(give_b))
-    final = add_after(meta, (keep0, got0, from_pair, from_mid), (keep_b,))
-    own_rows = cotangent.shape[0]
-    got = swap_cores(final[own_rows:])
-    own = final[:own_rows]
+    shape = keep_a.shape
+    flat = (shape[0] * shape[1], shape[2])
+    grad_a = add_after(
+        meta, (keep_a.reshape(flat), swap_cores(give_a).reshape(flat)), (give,), steps=2
+    )
+    got = swap_cores(give)
     input_grad = jnp.where(
         d == 0, jnp.concatenate([own, got], axis=1), jnp.concatenate([got, own], axis=1)
     )
+    grad_a = jnp.swapaxes(grad_a.reshape(shape), 1, 2)
     return (input_grad, grad_a, grad_b)
 
 

time: 250 us -> 228 us (0.912)
  waiting for transfers between devices: 38.6 us -> 24.9 us
  Pallas kernels: 149 us -> 145 us
    ppermute x4, waiting for transfers between devices: 13.9 us -> 0.91 us  [parts(): return (keep, send(give, perm=Y_SWAP), give)]
    pallas_call x30 -> x28, Pallas kernels: 149 us -> 145 us  [call(): pl.pallas_call(run, grid_spec=pltpu.PrefetchScalarGridSpec(num_scalar_pre...]
    ppermute x14 -> x11, starting transfers between devices: 17.6 us -> 13.9 us  [the longest x1 3.29 us: grid_body(): got = swap_cores(give)]
    ppermute x1, waiting for transfers between devices: 14.4 us -> 17.7 us  [grid_body(): mid_out = send(tied(mid, low_in), perm=OUTWARD)]
    transpose x1 -> x0, other arithmetic: 2.6 us -> none  [grid_body(): grad_a = jnp.swapaxes(add(keep_a, swap_cores(give_a)), 1, 2)]
  transfers between devices with their start and end apart: 32 -> 29, of which waited for: 7 -> 6; matrix products, arithmetic and copies ran while one was open for 3% -> 4% of each run, Pallas kernels for 57% -> 59%
where the time goes in v4:
time: 228 us; the launch traced here: 227 us
  Pallas kernels  145 us (64%)
  starting transfers between devices  40 us (18%)
  waiting for transfers between devices  24.9 us (11%)
  local copies, waits for them, and re-layouts  8.45 us (4%)
  other arithmetic  7.84 us (3%)
    pallas_call x28, Pallas kernels, call(): pl.pallas_call(run, grid_spec=pltpu.PrefetchScalarGridSpec(num_scalar_pre...  145 us
    ppermute x1, waiting for transfers between devices, grid_body(): mid_out = send(tied(mid, low_in), perm=OUTWARD)  17.7 us
    unnamed x36, local copies, waits for them, and re-layouts  7.63 us
  transfers between devices with their start and end apart: 29, of which 6 were waited for; matrix products, arithmetic and copies ran while one was open for 4% of the time, Pallas kernels for 59%

profile of v4, /device:TPU:1, one launch (start us, length us, event | category | flops | bytes accessed | tf_op | source)
XLA Modules:
  0.0 227.4 jit_solution(18266803772296651522)
XLA Ops:
  0.8 2.8 %collective-permute-start.1 = (bf16[64,5120]{1,0:T(8,128)(2,1)}, bf16[64,5120]{1,0:T(8,128)(2,1)S(1)}, u32[]{:S(2)}, u32[]{:S(2)}) collective-permute-start(bf16[64,5120]{1,0:T(8,128)(2,1)} %refs_0_.9), channel_id=1, source_target_pairs={{0,4},{2,6},{4,0},{6,2},{8,12},{10,14},{12,8},{14,10},{1,5},{3,7},... | collective-permute-start | bytes 1966088 | tf_op jit(solution)/shard_map/ppermute | solution.py:407
  10.0 5.2 %shard_map.130 = (bf16[512,3200]{1,0:T(8,128)(2,1)S(1)}, f32[256,128]{1,0:T(8,128)S(1)}) custom-call(s32[19]{0:T(128)S(1)} %concatenate.10.m, bf16[512,3200]{1,0:T(8,128)(2,1)} %refs_3_.13, bf16[512,3200]{1,0:T(8,128)(2,1)} %refs_4_.13, bf16[6,64,3200]{2,1,0:T(8,128)(2,1)S(1)} %bitcast.18), custom_call_target="tpu_custom_call" | custom-call | flops 1000 | bytes 1000 | tf_op jit(solution)/shard_map/pallas_call | solution.py:46
  23.3 17.7 %collective-permute-done.5 = bf16[64,5120]{1,0:T(8,128)(2,1)} collective-permute-done((bf16[64,5120]{1,0:T(8,128)(2,1)S(1)}, bf16[64,5120]{1,0:T(8,128)(2,1)}, u32[]{:S(2)}, u32[]{:S(2)}) %collective-permute-start.5) | collective-permute-done | bytes 655392 | tf_op jit(solution)/shard_map/ppermute | solution.py:413
  43.6 8.3 %shard_map.131.refs_10_.refs_0_ = f32[256,1280]{1,0:T(8,128)S(1)} custom-call(s32[19]{0:T(128)S(1)} %concatenate.10.m, bf16[64,5120]{1,0:T(8,128)(2,1)S(1)} %copy-done.1, bf16[64,5120]{1,0:T(8,128)(2,1)S(1)} %collective-permute-done.refs_1_.refs_5_, bf16[64,5120]{1,0:T(8,128)(2,1)S(1)} %collective-permute-done.1.refs_2_.refs_6_, ...), custom_call_target="tpu_custom_call" | custom-call | flops 1000 | bytes 1000 | tf_op jit(solution)/shard_map/pallas_call | solution.py:46
  51.9 2.9 %collective-permute-done.8 = bf16[64,5120]{1,0:T(8,128)(2,1)S(1)} collective-permute-done((bf16[64,5120]{1,0:T(8,128)(2,1)S(1)}, bf16[64,5120]{1,0:T(8,128)(2,1)S(1)}, u32[]{:S(2)}, u32[]{:S(2)}) %collective-permute-start.8) | collective-permute-done | bytes 655392 | tf_op jit(solution)/shard_map/ppermute | solution.py:416
  57.7 8.3 %shard_map.132.refs_10_.refs_1_ = f32[256,1280]{1,0:T(8,128)S(1)} custom-call(s32[19]{0:T(128)S(1)} %concatenate.10.m, bf16[64,5120]{1,0:T(8,128)(2,1)S(1)} %copy-done.1, bf16[64,5120]{1,0:T(8,128)(2,1)S(1)} %collective-permute-done.refs_1_.refs_5_, bf16[64,5120]{1,0:T(8,128)(2,1)S(1)} %collective-permute-done.1.refs_2_.refs_6_, ...), custom_call_target="tpu_custom_call" | custom-call | flops 1000 | bytes 1000 | tf_op jit(solution)/shard_map/pallas_call | solution.py:46
  65.9 5.8 %shard_map.133.refs_10_.refs_2_ = f32[256,640]{1,0:T(8,128)S(1)} custom-call(s32[19]{0:T(128)S(1)} %concatenate.10.m, bf16[64,5120]{1,0:T(8,128)(2,1)S(1)} %copy-done.1, bf16[64,5120]{1,0:T(8,128)(2,1)S(1)} %collective-permute-done.refs_1_.refs_5_, bf16[64,5120]{1,0:T(8,128)(2,1)S(1)} %collective-permute-done.1.refs_2_.refs_6_, ...), custom_call_target="tpu_custom_call" | custom-call | flops 1000 | bytes 1000 | tf_op jit(solution)/shard_map/pallas_call | solution.py:46
  76.8 8.6 %shard_map.135.refs_2_.refs_0_ = f32[256,1280]{1,0:T(8,128)S(1)} custom-call(s32[19]{0:T(128)S(1)} %concatenate.10.m, bf16[64,5120]{1,0:T(8,128)(2,1)S(1)} %broadcast_select_fusion.1.refs_4_.refs_0_, bf16[64,5120]{1,0:T(8,128)(2,1)S(1)} %collective-permute-done.6.refs_5_.refs_1_, bf16[64,5120]{1,0:T(8,128)(2,1)} %broadcast_select_fusion.refs_6_.refs_2_, ...), custom_call_target="tpu_custom_call" | custom-call | flops 1000 | bytes 1000 | tf_op jit(solution)/shard_map/pallas_call | solution.py:46
  86.4 8.6 %shard_map.137.refs_2_.refs_1_ = f32[256,1280]{1,0:T(8,128)S(1)} custom-call(s32[19]{0:T(128)S(1)} %concatenate.10.m, bf16[64,5120]{1,0:T(8,128)(2,1)S(1)} %broadcast_select_fusion.1.refs_4_.refs_0_, bf16[64,5120]{1,0:T(8,128)(2,1)S(1)} %collective-permute-done.6.refs_5_.refs_1_, bf16[64,5120]{1,0:T(8,128)(2,1)} %broadcast_select_fusion.refs_6_.refs_2_, ...), custom_call_target="tpu_custom_call" | custom-call | flops 1000 | bytes 1000 | tf_op jit(solution)/shard_map/pallas_call | solution.py:46
  97.5 6.0 %shard_map.139.refs_2_ = f32[256,640]{1,0:T(8,128)S(1)} custom-call(s32[19]{0:T(128)S(1)} %concatenate.10.m, bf16[64,5120]{1,0:T(8,128)(2,1)S(1)} %broadcast_select_fusion.1.refs_4_.refs_0_, bf16[64,5120]{1,0:T(8,128)(2,1)S(1)} %collective-permute-done.6.refs_5_.refs_1_, bf16[64,5120]{1,0:T(8,128)(2,1)} %broadcast_select_fusion.refs_6_.refs_2_, ...), custom_call_target="tpu_custom_call" | custom-call | flops 1000 | bytes 1000 | tf_op jit(solution)/shard_map/pallas_call | solution.py:46
  104.7 3.3 %shard_map.141.refs_7_.refs_0_ = bf16[2,128,3200]{2,1,0:T(8,128)(2,1)S(1)} custom-call(s32[19]{0:T(128)S(1)} %concatenate.10.m, f32[256,1280]{1,0:T(8,128)S(1)} %shard_map.135.refs_2_.refs_0_, f32[256,1280]{1,0:T(8,128)S(1)} %shard_map.137.refs_2_.refs_1_, f32[256,640]{1,0:T(8,128)S(1)} %shard_map.139.refs_2_, bf16[512,3200]{1,0:T(8,128)(2,1)} %refs_3_.13, ...), custom_call_target="tpu_custom_call" | custom-call | flops 1000 | bytes 1000 | tf_op jit(solution)/shard_map/pallas_call | solution.py:46
  108.0 3.9 %collective-permute-start.13 = (bf16[2,128,3200]{2,1,0:T(8,128)(2,1)S(1)}, bf16[2,128,3200]{2,1,0:T(8,128)(2,1)S(1)}, u32[]{:S(2)}, u32[]{:S(2)}) collective-permute-start(bf16[2,128,3200]{2,1,0:T(8,128)(2,1)S(1)} %shard_map.141.refs_7_.refs_0_), channel_id=1, source_target_pairs={{0,1},{1,0},{2,3},{3,2},{4,5},{5,4},{6,7},{7,6},{8,9},{9,8},{10,11... | collective-permute-start | bytes 4915208 | tf_op jit(solution)/shard_map/ppermute | solution.py:442
  111.9 3.3 %shard_map.142.refs_4_.refs_0_ = bf16[2,128,3200]{2,1,0:T(8,128)(2,1)S(1)} custom-call(s32[19]{0:T(128)S(1)} %concatenate.10.m, f32[256,1280]{1,0:T(8,128)S(1)} %shard_map.135.refs_2_.refs_0_, f32[256,1280]{1,0:T(8,128)S(1)} %shard_map.137.refs_2_.refs_1_, f32[256,640]{1,0:T(8,128)S(1)} %shard_map.139.refs_2_, bf16[512,3200]{1,0:T(8,128)(2,1)} %refs_3_.13, ...), custom_call_target="tpu_custom_call" | custom-call | flops 1000 | bytes 1000 | tf_op jit(solution)/shard_map/pallas_call | solution.py:46
  117.9 15.4 %shard_map.143 = (bf16[128,2560]{1,0:T(8,128)(2,1)S(1)}, bf16[128,2560]{1,0:T(8,128)(2,1)S(1)}) custom-call(s32[19]{0:T(128)S(1)} %concatenate.10.m, bf16[2,128,3200]{2,1,0:T(8,128)(2,1)S(1)} %copy-done.5, bf16[2,128,3200]{2,1,0:T(8,128)(2,1)S(1)} %collective-permute-done.13.refs_1_, bf16[2560,3200]{1,0:T(8,128)(2,1)} %refs_2_.7, ...), custom_call_target="tpu_custom_call" | custom-call | flops 1000 | bytes 1000 | tf_op jit(solution)/shard_map/pallas_call | solution.py:46
  133.3 3.3 %shard_map.144.refs_4_.refs_0_ = bf16[2,128,3200]{2,1,0:T(8,128)(2,1)S(1)} custom-call(s32[19]{0:T(128)S(1)} %concatenate.10.m, f32[256,1280]{1,0:T(8,128)S(1)} %shard_map.131.refs_10_.refs_0_, f32[256,1280]{1,0:T(8,128)S(1)} %shard_map.132.refs_10_.refs_1_, f32[256,640]{1,0:T(8,128)S(1)} %copy-done.13, bf16[512,3200]{1,0:T(8,128)(2,1)} %refs_3_.13, ...), custom_call_target="tpu_custom_call" | custom-call | flops 1000 | bytes 1000 | tf_op jit(solution)/shard_map/pallas_call | solution.py:46
  139.1 15.5 %shard_map.145 = (bf16[128,2560]{1,0:T(8,128)(2,1)S(1)}, bf16[128,2560]{1,0:T(8,128)(2,1)S(1)}) custom-call(s32[19]{0:T(128)S(1)} %concatenate.10.m, bf16[2,128,3200]{2,1,0:T(8,128)(2,1)S(1)} %copy-done.7, bf16[2,128,3200]{2,1,0:T(8,128)(2,1)S(1)} %collective-permute-done.15.refs_1_, bf16[2560,3200]{1,0:T(8,128)(2,1)} %refs_2_.7, ...), custom_call_target="tpu_custom_call" | custom-call | flops 1000 | bytes 1000 | tf_op jit(solution)/shard_map/pallas_call | solution.py:46
  155.3 3.3 %shard_map.147.refs_4_.refs_0_ = bf16[2,128,3200]{2,1,0:T(8,128)(2,1)S(1)} custom-call(s32[19]{0:T(128)S(1)} %concatenate.10.m, f32[256,1280]{1,0:T(8,128)S(1)} %shard_map.131.refs_10_.refs_0_, f32[256,1280]{1,0:T(8,128)S(1)} %shard_map.132.refs_10_.refs_1_, f32[256,640]{1,0:T(8,128)S(1)} %copy-done.13, bf16[512,3200]{1,0:T(8,128)(2,1)} %refs_3_.13, ...), custom_call_target="tpu_custom_call" | custom-call | flops 1000 | bytes 1000 | tf_op jit(solution)/shard_map/pallas_call | solution.py:46
  160.4 2.6 %collective-permute-start.18 = (bf16[128,2560]{1,0:T(8,128)(2,1)S(1)}, bf16[128,2560]{1,0:T(8,128)(2,1)S(1)}, u32[]{:S(2)}, u32[]{:S(2)}) collective-permute-start(bf16[128,2560]{1,0:T(8,128)(2,1)S(1)} %shard_map.146.refs_7_.refs_0_), channel_id=1, source_target_pairs={{0,4},{2,6},{12,8},{14,10},{1,5},{3,7},{13,9},{15,11},{16,20},{18,... | collective-permute-start | bytes 1966088 | tf_op jit(solution)/shard_map/ppermute | solution.py:450
  163.0 15.5 %shard_map.148 = (bf16[128,2560]{1,0:T(8,128)(2,1)S(1)}, bf16[128,2560]{1,0:T(8,128)(2,1)S(1)}) custom-call(s32[19]{0:T(128)S(1)} %concatenate.10.m, bf16[2,128,3200]{2,1,0:T(8,128)(2,1)S(1)} %copy-done.11, bf16[2,128,3200]{2,1,0:T(8,128)(2,1)S(1)} %collective-permute-done.16.refs_1_, bf16[2560,3200]{1,0:T(8,128)(2,1)} %refs_2_.7, ...), custom_call_target="tpu_custom_call" | custom-call | flops 1000 | bytes 1000 | tf_op jit(solution)/shard_map/pallas_call | solution.py:46
  180.9 3.7 %collective-permute-start.24 = (bf16[128,2560]{1,0:T(8,128)(2,1)S(1)}, bf16[128,2560]{1,0:T(8,128)(2,1)S(1)}, u32[]{:S(2)}, u32[]{:S(2)}) collective-permute-start(bf16[128,2560]{1,0:T(8,128)(2,1)S(1)} %shard_map.149.refs_2_.refs_0_), channel_id=1, source_target_pairs={{0,4},{2,6},{12,8},{14,10},{1,5},{3,7},{13,9},{15,11},{16,20},{18,... | collective-permute-start | bytes 1966088 | tf_op jit(solution)/shard_map/ppermute | solution.py:455
  184.6 15.7 %shard_map.151 = (bf16[128,2560]{1,0:T(8,128)(2,1)S(1)}, bf16[128,2560]{1,0:T(8,128)(2,1)S(1)}) custom-call(s32[19]{0:T(128)S(1)} %concatenate.10.m, bf16[2,128,3200]{2,1,0:T(8,128)(2,1)S(1)} %copy-done.9, bf16[2,128,3200]{2,1,0:T(8,128)(2,1)S(1)} %collective-permute-done.17.refs_1_, bf16[2560,3200]{1,0:T(8,128)(2,1)} %refs_2_.7, ...), custom_call_target="tpu_custom_call" | custom-call | flops 1000 | bytes 1000 | tf_op jit(solution)/shard_map/pallas_call | solution.py:46
  205.0 6.5 %shard_map.154 = (bf16[3,64,3200]{2,1,0:T(8,128)(2,1)S(1)}, bf16[3,64,3200]{2,1,0:T(8,128)(2,1)}) custom-call(s32[19]{0:T(128)S(1)} %concatenate.10.m, bf16[512,128]{1,0:T(8,128)(2,1)S(1)} %get-tuple-element.49.refs_5_.refs_0_, bf16[512,3200]{1,0:T(8,128)(2,1)} %copy-done.14, bf16[128,2560]{1,0:T(8,128)(2,1)S(1)} %shard_map.153.refs_2_), custom_call_target="tpu_custom_call" | custom-call | flops 1000 | bytes 1000 | tf_op jit(solution)/shard_map/pallas_call | solution.py:46
  211.5 2.6 %collective-permute-start.27 = (bf16[3,64,3200]{2,1,0:T(8,128)(2,1)}, bf16[3,64,3200]{2,1,0:T(8,128)(2,1)S(1)}, u32[]{:S(2)}, u32[]{:S(2)}) collective-permute-start(bf16[3,64,3200]{2,1,0:T(8,128)(2,1)} %get-tuple-element.67), channel_id=1, source_target_pairs={{0,1},{1,0},{2,3},{3,2},{4,5},{5,4},{6,7},{7,6},{8,9},{9,8},{10,11... | collective-permute-start | bytes 3686408 | tf_op jit(solution)/shard_map/ppermute | solution.py:471
  218.5 3.3 %collective-permute-start.26 = (bf16[64,2560]{1,0:T(8,128)(2,1)S(1)}, bf16[64,2560]{1,0:T(8,128)(2,1)}, u32[]{:S(2)}, u32[]{:S(2)}) collective-permute-start(bf16[64,2560]{1,0:T(8,128)(2,1)S(1)} %get-tuple-element.66.refs_2_), channel_id=1, source_target_pairs={{0,1},{1,0},{2,3},{3,2},{4,5},{5,4},{6,7},{7,6},{8,9},{9,8},{10,11... | collective-permute-start | bytes 983048 | tf_op jit(solution)/shard_map/ppermute | solution.py:473
  (108 shorter events, 54.2 us)
Async XLA Ops:
  0.6 42.9 %collective-permute-start.3 = (bf16[2560,3200]{1,0:T(8,128)(2,1)}, bf16[2560,3200]{1,0:T(8,128)(2,1)}, u32[]{:S(2)}, u32[]{:S(2)}) collective-permute-start(bf16[2560,3200]{1,0:T(8,128)(2,1)} %refs_8_.13), channel_id=1, source_target_pairs={{0,1},{1,0},{2,3},{3,2},{4,5},{5,4},{6,7},{7,6},{8,9},{9,8},{10,11... | collective-permute-start | bytes 49152008 | tf_op jit(solution)/shard_map/ppermute | solution.py:406
  0.8 18.0 %collective-permute-start.1 = (bf16[64,5120]{1,0:T(8,128)(2,1)}, bf16[64,5120]{1,0:T(8,128)(2,1)S(1)}, u32[]{:S(2)}, u32[]{:S(2)}) collective-permute-start(bf16[64,5120]{1,0:T(8,128)(2,1)} %refs_0_.9), channel_id=1, source_target_pairs={{0,4},{2,6},{4,0},{6,2},{8,12},{10,14},{12,8},{14,10},{1,5},{3,7},... | collective-permute-start | bytes 1966088 | tf_op jit(solution)/shard_map/ppermute | solution.py:407
  3.5 15.2 %collective-permute-start.4 = (bf16[64,5120]{1,0:T(8,128)(2,1)}, bf16[64,5120]{1,0:T(8,128)(2,1)S(1)}, u32[]{:S(2)}, u32[]{:S(2)}) collective-permute-start(bf16[64,5120]{1,0:T(8,128)(2,1)} %refs_0_.9), channel_id=1, source_target_pairs={{4,8},{6,10},{8,4},{10,6},{5,9},{7,11},{9,5},{11,7},{20,24},{22,26... | collective-permute-start | bytes 1966088 | tf_op jit(solution)/shard_map/ppermute | solution.py:408
  4.2 16.5 %collective-permute-start = (bf16[64,5120]{1,0:T(8,128)(2,1)}, bf16[64,5120]{1,0:T(8,128)(2,1)S(1)}, u32[]{:S(2)}, u32[]{:S(2)}) collective-permute-start(bf16[64,5120]{1,0:T(8,128)(2,1)} %refs_0_.9), channel_id=1, source_target_pairs={{0,2},{2,0},{4,6},{6,4},{8,10},{10,8},{12,14},{14,12},{1,3},{3,1},... | collective-permute-start | bytes 1966088 | tf_op jit(solution)/shard_map/ppermute | solution.py:409
  19.4 21.6 %collective-permute-start.5 = (bf16[64,5120]{1,0:T(8,128)(2,1)S(1)}, bf16[64,5120]{1,0:T(8,128)(2,1)}, u32[]{:S(2)}, u32[]{:S(2)}) collective-permute-start(bf16[64,5120]{1,0:T(8,128)(2,1)S(1)} %collective-permute-done.4), channel_id=1, source_target_pairs={{4,0},{6,2},{8,12},{10,14},{5,1},{7,3},{9,13},{11,15},{20,16},{22,... | collective-permute-start | bytes 1966088 | tf_op jit(solution)/shard_map/ppermute | solution.py:413
  20.8 21.5 %collective-permute-start.2 = (bf16[64,5120]{1,0:T(8,128)(2,1)S(1)}, bf16[64,5120]{1,0:T(8,128)(2,1)S(1)}, u32[]{:S(2)}, u32[]{:S(2)}) collective-permute-start(bf16[64,5120]{1,0:T(8,128)(2,1)S(1)} %collective-permute-done.1.refs_2_.refs_6_), channel_id=1, source_target_pairs={{0,2},{2,0},{4,6},{6,4},{8,10},{10,8},{12,14},{14,12},{1,3},{3,1},... | collective-permute-start | bytes 1966088 | tf_op jit(solution)/shard_map/ppermute | solution.py:411
  22.0 32.8 %collective-permute-start.8 = (bf16[64,5120]{1,0:T(8,128)(2,1)S(1)}, bf16[64,5120]{1,0:T(8,128)(2,1)S(1)}, u32[]{:S(2)}, u32[]{:S(2)}) collective-permute-start(bf16[64,5120]{1,0:T(8,128)(2,1)S(1)} %collective-permute-done.7), channel_id=1, source_target_pairs={{4,0},{6,2},{8,12},{10,14},{5,1},{7,3},{9,13},{11,15},{20,16},{22,... | collective-permute-start | bytes 1966088 | tf_op jit(solution)/shard_map/ppermute | solution.py:416
  42.2 14.2 %collective-permute-start.6 = (bf16[64,5120]{1,0:T(8,128)(2,1)S(1)}, bf16[64,5120]{1,0:T(8,128)(2,1)S(1)}, u32[]{:S(2)}, u32[]{:S(2)}) collective-permute-start(bf16[64,5120]{1,0:T(8,128)(2,1)S(1)} %broadcast_select_fusion.1.refs_4_.refs_0_), channel_id=1, source_target_pairs={{0,2},{2,0},{4,6},{6,4},{8,10},{10,8},{12,14},{14,12},{1,3},{3,1},... | collective-permute-start | bytes 1966088 | tf_op jit(solution)/shard_map/ppermute | solution.py:415
  56.4 16.2 %collective-permute-start.9 = (bf16[64,5120]{1,0:T(8,128)(2,1)}, bf16[64,5120]{1,0:T(8,128)(2,1)S(1)}, u32[]{:S(2)}, u32[]{:S(2)}) collective-permute-start(bf16[64,5120]{1,0:T(8,128)(2,1)} %broadcast_select_fusion.refs_6_.refs_2_), channel_id=1, source_target_pairs={{0,2},{2,0},{4,6},{6,4},{8,10},{10,8},{12,14},{14,12},{1,3},{3,1},... | collective-permute-start | bytes 1966088 | tf_op jit(solution)/shard_map/ppermute | solution.py:422
  75.4 10.0 %collective-permute-start.10 = (bf16[512,128]{1,0:T(8,128)(2,1)S(1)}, bf16[512,128]{1,0:T(8,128)(2,1)S(1)}, u32[]{:S(2)}, u32[]{:S(2)}) collective-permute-start(bf16[512,128]{1,0:T(8,128)(2,1)S(1)} %get-tuple-element.44.refs_10_), channel_id=1, source_target_pairs={{0,2},{2,0},{4,6},{6,4},{8,10},{10,8},{12,14},{14,12},{1,3},{3,1},... | collective-permute-start | bytes 393224 | tf_op jit(solution)/shard_map/ppermute | solution.py:429
  86.0 9.0 %collective-permute-start.11 = (bf16[512,128]{1,0:T(8,128)(2,1)S(1)}, bf16[512,128]{1,0:T(8,128)(2,1)S(1)}, u32[]{:S(2)}, u32[]{:S(2)}) collective-permute-start(bf16[512,128]{1,0:T(8,128)(2,1)S(1)} %get-tuple-element.46.refs_10_), channel_id=1, source_target_pairs={{0,4},{2,6},{4,0},{6,2},{8,12},{10,14},{12,8},{14,10},{1,5},{3,7},... | collective-permute-start | bytes 393224 | tf_op jit(solution)/shard_map/ppermute | solution.py:429
  115.3 21.4 %collective-permute-start.15 = (bf16[2,128,3200]{2,1,0:T(8,128)(2,1)S(1)}, bf16[2,128,3200]{2,1,0:T(8,128)(2,1)S(1)}, u32[]{:S(2)}, u32[]{:S(2)}) collective-permute-start(bf16[2,128,3200]{2,1,0:T(8,128)(2,1)S(1)} %shard_map.142.refs_4_.refs_0_), channel_id=1, source_target_pairs={{0,1},{1,0},{2,3},{3,2},{4,5},{5,4},{6,7},{7,6},{8,9},{9,8},{10,11... | collective-permute-start | bytes 4915208 | tf_op jit(solution)/shard_map/ppermute | solution.py:444
  136.7 21.9 %collective-permute-start.16 = (bf16[2,128,3200]{2,1,0:T(8,128)(2,1)S(1)}, bf16[2,128,3200]{2,1,0:T(8,128)(2,1)S(1)}, u32[]{:S(2)}, u32[]{:S(2)}) collective-permute-start(bf16[2,128,3200]{2,1,0:T(8,128)(2,1)S(1)} %shard_map.144.refs_4_.refs_0_), channel_id=1, source_target_pairs={{0,1},{1,0},{2,3},{3,2},{4,5},{5,4},{6,7},{7,6},{8,9},{9,8},{10,11... | collective-permute-start | bytes 4915208 | tf_op jit(solution)/shard_map/ppermute | solution.py:448
  137.9 16.7 %collective-permute-start.14 = (bf16[128,2560]{1,0:T(8,128)(2,1)S(1)}, bf16[128,2560]{1,0:T(8,128)(2,1)S(1)}, u32[]{:S(2)}, u32[]{:S(2)}) collective-permute-start(bf16[128,2560]{1,0:T(8,128)(2,1)S(1)} %get-tuple-element.51.refs_7_), channel_id=1, source_target_pairs={{0,2},{2,0},{4,6},{6,4},{8,10},{10,8},{12,14},{14,12},{1,3},{3,1},... | collective-permute-start | bytes 1966088 | tf_op jit(solution)/shard_map/ppermute | solution.py:439
  158.6 25.9 %collective-permute-start.17 = (bf16[2,128,3200]{2,1,0:T(8,128)(2,1)S(1)}, bf16[2,128,3200]{2,1,0:T(8,128)(2,1)S(1)}, u32[]{:S(2)}, u32[]{:S(2)}) collective-permute-start(bf16[2,128,3200]{2,1,0:T(8,128)(2,1)S(1)} %shard_map.147.refs_4_.refs_0_), channel_id=1, source_target_pairs={{0,1},{1,0},{2,3},{3,2},{4,5},{5,4},{6,7},{7,6},{8,9},{9,8},{10,11... | collective-permute-start | bytes 4915208 | tf_op jit(solution)/shard_map/ppermute | solution.py:453
  159.1 19.3 %collective-permute-start.19 = (bf16[128,2560]{1,0:T(8,128)(2,1)S(1)}, bf16[128,2560]{1,0:T(8,128)(2,1)S(1)}, u32[]{:S(2)}, u32[]{:S(2)}) collective-permute-start(bf16[128,2560]{1,0:T(8,128)(2,1)S(1)} %get-tuple-element.53.refs_2_), channel_id=1, source_target_pairs={{0,2},{2,0},{4,6},{6,4},{8,10},{10,8},{12,14},{14,12},{1,3},{3,1},... | collective-permute-start | bytes 1966088 | tf_op jit(solution)/shard_map/ppermute | solution.py:439
  160.4 18.8 %collective-permute-start.18 = (bf16[128,2560]{1,0:T(8,128)(2,1)S(1)}, bf16[128,2560]{1,0:T(8,128)(2,1)S(1)}, u32[]{:S(2)}, u32[]{:S(2)}) collective-permute-start(bf16[128,2560]{1,0:T(8,128)(2,1)S(1)} %shard_map.146.refs_7_.refs_0_), channel_id=1, source_target_pairs={{0,4},{2,6},{12,8},{14,10},{1,5},{3,7},{13,9},{15,11},{16,20},{18,... | collective-permute-start | bytes 1966088 | tf_op jit(solution)/shard_map/ppermute | solution.py:450
  179.9 20.4 %collective-permute-start.22 = (bf16[128,2560]{1,0:T(8,128)(2,1)S(1)}, bf16[128,2560]{1,0:T(8,128)(2,1)S(1)}, u32[]{:S(2)}, u32[]{:S(2)}) collective-permute-start(bf16[128,2560]{1,0:T(8,128)(2,1)S(1)} %shard_map.150.refs_4_), channel_id=1, source_target_pairs={{4,8},{6,10},{8,4},{10,6},{5,9},{7,11},{9,5},{11,7},{20,24},{22,26... | collective-permute-start | bytes 1966088 | tf_op jit(solution)/shard_map/ppermute | solution.py:457
  180.6 19.7 %collective-permute-start.21 = (bf16[128,2560]{1,0:T(8,128)(2,1)S(1)}, bf16[128,2560]{1,0:T(8,128)(2,1)S(1)}, u32[]{:S(2)}, u32[]{:S(2)}) collective-permute-start(bf16[128,2560]{1,0:T(8,128)(2,1)S(1)} %get-tuple-element.57.refs_2_), channel_id=1, source_target_pairs={{0,2},{2,0},{4,6},{6,4},{8,10},{10,8},{12,14},{14,12},{1,3},{3,1},... | collective-permute-start | bytes 1966088 | tf_op jit(solution)/shard_map/ppermute | solution.py:439
  180.9 20.2 %collective-permute-start.24 = (bf16[128,2560]{1,0:T(8,128)(2,1)S(1)}, bf16[128,2560]{1,0:T(8,128)(2,1)S(1)}, u32[]{:S(2)}, u32[]{:S(2)}) collective-permute-start(bf16[128,2560]{1,0:T(8,128)(2,1)S(1)} %shard_map.149.refs_2_.refs_0_), channel_id=1, source_target_pairs={{0,4},{2,6},{12,8},{14,10},{1,5},{3,7},{13,9},{15,11},{16,20},{18,... | collective-permute-start | bytes 1966088 | tf_op jit(solution)/shard_map/ppermute | solution.py:455
  201.8 14.2 %collective-permute-start.25 = (bf16[128,2560]{1,0:T(8,128)(2,1)S(1)}, bf16[128,2560]{1,0:T(8,128)(2,1)S(1)}, u32[]{:S(2)}, u32[]{:S(2)}) collective-permute-start(bf16[128,2560]{1,0:T(8,128)(2,1)S(1)} %shard_map.153.refs_2_), channel_id=1, source_target_pairs={{4,8},{6,10},{8,4},{10,6},{5,9},{7,11},{9,5},{11,7},{20,24},{22,26... | collective-permute-start | bytes 1966088 | tf_op jit(solution)/shard_map/ppermute | solution.py:462
  202.5 14.3 %collective-permute-start.23 = (bf16[128,2560]{1,0:T(8,128)(2,1)S(1)}, bf16[128,2560]{1,0:T(8,128)(2,1)S(1)}, u32[]{:S(2)}, u32[]{:S(2)}) collective-permute-start(bf16[128,2560]{1,0:T(8,128)(2,1)S(1)} %shard_map.152.refs_2_), channel_id=1, source_target_pairs={{0,4},{2,6},{4,0},{6,2},{8,12},{10,14},{12,8},{14,10},{1,5},{3,7},... | collective-permute-start | bytes 1966088 | tf_op jit(solution)/shard_map/ppermute | solution.py:460
  203.7 13.9 %collective-permute-start.20 = (bf16[128,2560]{1,0:T(8,128)(2,1)S(1)}, bf16[128,2560]{1,0:T(8,128)(2,1)S(1)}, u32[]{:S(2)}, u32[]{:S(2)}) collective-permute-start(bf16[128,2560]{1,0:T(8,128)(2,1)S(1)} %get-tuple-element.59.refs_3_), channel_id=1, source_target_pairs={{0,2},{2,0},{4,6},{6,4},{8,10},{10,8},{12,14},{14,12},{1,3},{3,1},... | collective-permute-start | bytes 1966088 | tf_op jit(solution)/shard_map/ppermute | solution.py:439
  211.5 14.2 %collective-permute-start.27 = (bf16[3,64,3200]{2,1,0:T(8,128)(2,1)}, bf16[3,64,3200]{2,1,0:T(8,128)(2,1)S(1)}, u32[]{:S(2)}, u32[]{:S(2)}) collective-permute-start(bf16[3,64,3200]{2,1,0:T(8,128)(2,1)} %get-tuple-element.67), channel_id=1, source_target_pairs={{0,1},{1,0},{2,3},{3,2},{4,5},{5,4},{6,7},{7,6},{8,9},{9,8},{10,11... | collective-permute-start | bytes 3686408 | tf_op jit(solution)/shard_map/ppermute | solution.py:471
  (23 other events, 142.2 us)

commit v5 on v4

--- a/solution.py
+++ b/solution.py
@@ -36,7 +36,7 @@
 
 
 def call(
-    kernel, meta, args, grid, in_specs, out_specs, out_shape, scratch=(), vmem=48, after=(), cost=(1000, 1000)
+    kernel, meta, args, grid, in_specs, out_specs, out_shape, scratch=(), vmem=26, after=(), cost=(1000, 1000)
 ):
     first, extra = len(args), len(after)
 

time: 228 us -> 218 us (0.956)
  Pallas kernels: 145 us -> 121 us
  local copies, waits for them, and re-layouts: 8.45 us -> 20.2 us
  starting transfers between devices: 40 us -> 44.7 us
    pallas_call x28, Pallas kernels: 145 us -> 121 us  [call(): pl.pallas_call(run, grid_spec=pltpu.PrefetchScalarGridSpec(num_scalar_pre...]
    unnamed x36 -> x72, local copies, waits for them, and re-layouts: 7.63 us -> 19.4 us
    ppermute x1, waiting for transfers between devices: 2.94 us -> 0.01 us  [grid_body(): far_out = send(pair_mid, perm=OUTWARD)]
    ppermute x1, starting transfers between devices: 3.65 us -> 6.28 us  [grid_body(): mid_in = send(sum2, perm=INWARD)]
    ppermute x4, waiting for transfers between devices: 0.91 us -> 3.48 us  [parts(): return (keep, send(give, perm=Y_SWAP), give)]
  transfers between devices with their start and end apart: 29 -> 29, of which waited for: 6 -> 6; matrix products, arithmetic and copies ran while one was open for 4% -> 4% of each run, Pallas kernels for 59% -> 52%
where the time goes in v5:
time: 218 us; the launch traced here: 217 us
  Pallas kernels  121 us (56%)
  starting transfers between devices  44.7 us (21%)
  waiting for transfers between devices  22.7 us (10%)
  local copies, waits for them, and re-layouts  20.2 us (9%)
  other arithmetic  6.93 us (3%)
    pallas_call x28, Pallas kernels, call(): pl.pallas_call(run, grid_spec=pltpu.PrefetchScalarGridSpec(num_scalar_pre...  121 us
    unnamed x72, local copies, waits for them, and re-layouts  19.4 us
    ppermute x1, waiting for transfers between devices, grid_body(): mid_out = send(tied(mid, low_in), perm=OUTWARD)  17.2 us
    ppermute x1, starting transfers between devices, grid_body(): mid_in = send(sum2, perm=INWARD)  6.28 us
  transfers between devices with their start and end apart: 29, of which 6 were waited for; matrix products, arithmetic and copies ran while one was open for 4% of the time, Pallas kernels for 52%

profile of v5, /device:TPU:1, one launch (start us, length us, event | category | flops | bytes accessed | tf_op | source)
XLA Modules:
  0.0 216.9 jit_solution(15673044149149778541)
XLA Ops:
  0.8 2.8 %collective-permute-start.1 = (bf16[64,5120]{1,0:T(8,128)(2,1)}, bf16[64,5120]{1,0:T(8,128)(2,1)S(1)}, u32[]{:S(2)}, u32[]{:S(2)}) collective-permute-start(bf16[64,5120]{1,0:T(8,128)(2,1)} %refs_0_.9), channel_id=1, source_target_pairs={{0,4},{2,6},{4,0},{6,2},{8,12},{10,14},{12,8},{14,10},{1,5},{3,7},... | collective-permute-start | bytes 1966088 | tf_op jit(solution)/shard_map/ppermute | solution.py:407
  14.6 2.9 %shard_map.130 = (bf16[512,3200]{1,0:T(8,128)(2,1)S(1)}, f32[256,128]{1,0:T(8,128)S(1)}) custom-call(s32[19]{0:T(128)S(1)} %concatenate.10.m, bf16[512,3200]{1,0:T(8,128)(2,1)S(1)} %copy-done.2, bf16[512,3200]{1,0:T(8,128)(2,1)S(1)} %copy-done.5, bf16[6,64,3200]{2,1,0:T(8,128)(2,1)S(1)} %bitcast.16), custom_call_target="tpu_custom_call" | custom-call | flops 1000 | bytes 1000 | tf_op jit(solution)/shard_map/pallas_call | solution.py:46
  24.2 17.2 %collective-permute-done.5 = bf16[64,5120]{1,0:T(8,128)(2,1)} collective-permute-done((bf16[64,5120]{1,0:T(8,128)(2,1)}, bf16[64,5120]{1,0:T(8,128)(2,1)}, u32[]{:S(2)}, u32[]{:S(2)}) %collective-permute-start.5) | collective-permute-done | bytes 655392 | tf_op jit(solution)/shard_map/ppermute | solution.py:413
  43.9 5.6 %copy-done = bf16[2560,3200]{1,0:T(8,128)(2,1)S(1)} copy-done((bf16[2560,3200]{1,0:T(8,128)(2,1)S(1)}, bf16[2560,3200]{1,0:T(8,128)(2,1)}, u32[]{:S(2)}) %copy-start) | copy-done | bytes 16384024
  51.7 7.9 %shard_map.131.refs_10_.refs_0_ = f32[256,1280]{1,0:T(8,128)S(1)} custom-call(s32[19]{0:T(128)S(1)} %concatenate.10.m, bf16[64,5120]{1,0:T(8,128)(2,1)S(1)} %copy-done.11, bf16[64,5120]{1,0:T(8,128)(2,1)S(1)} %copy-done.16, bf16[64,5120]{1,0:T(8,128)(2,1)S(1)} %copy-done.13, bf16[64,5120]{1,0:T(8,128)(2,1)S(1)} %collective-permute-done.2.refs_3_.refs_7_, ...), custom_call_target="tpu_custom_call" | custom-call | flops 1000 | bytes 1000 | tf_op jit(solution)/shard_map/pallas_call | solution.py:46
  62.7 7.5 %shard_map.132.refs_10_.refs_1_ = f32[256,1280]{1,0:T(8,128)S(1)} custom-call(s32[19]{0:T(128)S(1)} %concatenate.10.m, bf16[64,5120]{1,0:T(8,128)(2,1)S(1)} %copy-done.11, bf16[64,5120]{1,0:T(8,128)(2,1)S(1)} %copy-done.17, bf16[64,5120]{1,0:T(8,128)(2,1)S(1)} %copy-done.14, bf16[64,5120]{1,0:T(8,128)(2,1)S(1)} %collective-permute-done.2.refs_3_.refs_7_, ...), custom_call_target="tpu_custom_call" | custom-call | flops 1000 | bytes 1000 | tf_op jit(solution)/shard_map/pallas_call | solution.py:46
  70.2 5.1 %shard_map.133.refs_10_.refs_2_ = f32[256,640]{1,0:T(8,128)S(1)} custom-call(s32[19]{0:T(128)S(1)} %concatenate.10.m, bf16[64,5120]{1,0:T(8,128)(2,1)S(1)} %copy-done.11, bf16[64,5120]{1,0:T(8,128)(2,1)S(1)} %copy-done.17, bf16[64,5120]{1,0:T(8,128)(2,1)S(1)} %copy-done.14, bf16[64,5120]{1,0:T(8,128)(2,1)S(1)} %collective-permute-done.2.refs_3_.refs_7_, ...), custom_call_target="tpu_custom_call" | custom-call | flops 1000 | bytes 1000 | tf_op jit(solution)/shard_map/pallas_call | solution.py:46
  77.2 7.5 %shard_map.135.refs_2_.refs_0_ = f32[256,1280]{1,0:T(8,128)S(1)} custom-call(s32[19]{0:T(128)S(1)} %concatenate.10.m, bf16[64,5120]{1,0:T(8,128)(2,1)S(1)} %broadcast_select_fusion.1.refs_4_.refs_0_, bf16[64,5120]{1,0:T(8,128)(2,1)S(1)} %collective-permute-done.6.refs_5_.refs_1_, bf16[64,5120]{1,0:T(8,128)(2,1)S(1)} %broadcast_select_fusion.refs_6_.refs_2_, ...), custom_call_target="tpu_custom_call" | custom-call | flops 1000 | bytes 1000 | tf_op jit(solution)/shard_map/pallas_call | solution.py:46
  86.7 7.7 %shard_map.137.refs_2_.refs_1_ = f32[256,1280]{1,0:T(8,128)S(1)} custom-call(s32[19]{0:T(128)S(1)} %concatenate.10.m, bf16[64,5120]{1,0:T(8,128)(2,1)S(1)} %broadcast_select_fusion.1.refs_4_.refs_0_, bf16[64,5120]{1,0:T(8,128)(2,1)S(1)} %collective-permute-done.6.refs_5_.refs_1_, bf16[64,5120]{1,0:T(8,128)(2,1)S(1)} %broadcast_select_fusion.refs_6_.refs_2_, ...), custom_call_target="tpu_custom_call" | custom-call | flops 1000 | bytes 1000 | tf_op jit(solution)/shard_map/pallas_call | solution.py:46
  95.6 5.6 %shard_map.139.refs_2_ = f32[256,640]{1,0:T(8,128)S(1)} custom-call(s32[19]{0:T(128)S(1)} %concatenate.10.m, bf16[64,5120]{1,0:T(8,128)(2,1)S(1)} %broadcast_select_fusion.1.refs_4_.refs_0_, bf16[64,5120]{1,0:T(8,128)(2,1)S(1)} %copy-done.19, bf16[64,5120]{1,0:T(8,128)(2,1)S(1)} %broadcast_select_fusion.refs_6_.refs_2_, ...), custom_call_target="tpu_custom_call" | custom-call | flops 1000 | bytes 1000 | tf_op jit(solution)/shard_map/pallas_call | solution.py:46
  104.6 4.3 %collective-permute-start.13 = (bf16[2,128,3200]{2,1,0:T(8,128)(2,1)S(1)}, bf16[2,128,3200]{2,1,0:T(8,128)(2,1)S(1)}, u32[]{:S(2)}, u32[]{:S(2)}) collective-permute-start(bf16[2,128,3200]{2,1,0:T(8,128)(2,1)S(1)} %shard_map.141.refs_7_.refs_0_), channel_id=1, source_target_pairs={{0,1},{1,0},{2,3},{3,2},{4,5},{5,4},{6,7},{7,6},{8,9},{9,8},{10,11... | collective-permute-start | bytes 4915208 | tf_op jit(solution)/shard_map/ppermute | solution.py:442
  108.9 2.8 %shard_map.142.refs_4_.refs_0_ = bf16[2,128,3200]{2,1,0:T(8,128)(2,1)} custom-call(s32[19]{0:T(128)S(1)} %concatenate.10.m, f32[256,1280]{1,0:T(8,128)S(1)} %shard_map.135.refs_2_.refs_0_, f32[256,1280]{1,0:T(8,128)S(1)} %shard_map.137.refs_2_.refs_1_, f32[256,640]{1,0:T(8,128)S(1)} %shard_map.139.refs_2_, bf16[512,3200]{1,0:T(8,128)(2,1)S(1)} %copy-done.3, ...), custom_call_target="tpu_custom_call" | custom-call | flops 1000 | bytes 1000 | tf_op jit(solution)/shard_map/pallas_call | solution.py:46
  113.9 12.9 %shard_map.143 = (bf16[128,2560]{1,0:T(8,128)(2,1)S(1)}, bf16[128,2560]{1,0:T(8,128)(2,1)S(1)}) custom-call(s32[19]{0:T(128)S(1)} %concatenate.10.m, bf16[2,128,3200]{2,1,0:T(8,128)(2,1)S(1)} %copy-done.26, bf16[2,128,3200]{2,1,0:T(8,128)(2,1)S(1)} %collective-permute-done.13.refs_1_, bf16[2560,3200]{1,0:T(8,128)(2,1)S(1)} %bitcast.15, ...), custom_call_target="tpu_custom_call" | custom-call | flops 1000 | bytes 1000 | tf_op jit(solution)/shard_map/pallas_call | solution.py:46
  130.6 13.9 %shard_map.145 = (bf16[128,2560]{1,0:T(8,128)(2,1)S(1)}, bf16[128,2560]{1,0:T(8,128)(2,1)S(1)}) custom-call(s32[19]{0:T(128)S(1)} %concatenate.10.m, bf16[2,128,3200]{2,1,0:T(8,128)(2,1)} %shard_map.142.refs_4_.refs_0_, bf16[2,128,3200]{2,1,0:T(8,128)(2,1)} %collective-permute-done.15.refs_1_, bf16[2560,3200]{1,0:T(8,128)(2,1)S(1)} %bitcast.15, ...), custom_call_target="tpu_custom_call" | custom-call | flops 1000 | bytes 1000 | tf_op jit(solution)/shard_map/pallas_call | solution.py:46
  147.2 2.0 shard_map.147.refs_4_.refs_0_
  150.6 2.7 %collective-permute-start.18 = (bf16[128,2560]{1,0:T(8,128)(2,1)S(1)}, bf16[128,2560]{1,0:T(8,128)(2,1)S(1)}, u32[]{:S(2)}, u32[]{:S(2)}) collective-permute-start(bf16[128,2560]{1,0:T(8,128)(2,1)S(1)} %shard_map.146.refs_7_.refs_0_), channel_id=1, source_target_pairs={{0,4},{2,6},{12,8},{14,10},{1,5},{3,7},{13,9},{15,11},{16,20},{18,... | collective-permute-start | bytes 1966088 | tf_op jit(solution)/shard_map/ppermute | solution.py:450
  153.2 12.6 %shard_map.148 = (bf16[128,2560]{1,0:T(8,128)(2,1)S(1)}, bf16[128,2560]{1,0:T(8,128)(2,1)S(1)}) custom-call(s32[19]{0:T(128)S(1)} %concatenate.10.m, bf16[2,128,3200]{2,1,0:T(8,128)(2,1)S(1)} %shard_map.144.refs_4_.refs_0_, bf16[2,128,3200]{2,1,0:T(8,128)(2,1)S(1)} %collective-permute-done.16.refs_1_, bf16[2560,3200]{1,0:T(8,128)(2,1)S(1)} %bitcast.15, ...), custom_call_target="tpu_custom_call" | custom-call | flops 1000 | bytes 1000 | tf_op jit(solution)/shard_map/pallas_call | solution.py:46
  169.4 6.3 %collective-permute-start.24 = (bf16[128,2560]{1,0:T(8,128)(2,1)S(1)}, bf16[128,2560]{1,0:T(8,128)(2,1)S(1)}, u32[]{:S(2)}, u32[]{:S(2)}) collective-permute-start(bf16[128,2560]{1,0:T(8,128)(2,1)S(1)} %shard_map.149.refs_2_.refs_0_), channel_id=1, source_target_pairs={{0,4},{2,6},{12,8},{14,10},{1,5},{3,7},{13,9},{15,11},{16,20},{18,... | collective-permute-start | bytes 1966088 | tf_op jit(solution)/shard_map/ppermute | solution.py:455
  175.7 12.8 %shard_map.151 = (bf16[128,2560]{1,0:T(8,128)(2,1)S(1)}, bf16[128,2560]{1,0:T(8,128)(2,1)S(1)}) custom-call(s32[19]{0:T(128)S(1)} %concatenate.10.m, bf16[2,128,3200]{2,1,0:T(8,128)(2,1)S(1)} %shard_map.147.refs_4_.refs_0_, bf16[2,128,3200]{2,1,0:T(8,128)(2,1)S(1)} %collective-permute-done.17.refs_1_, bf16[2560,3200]{1,0:T(8,128)(2,1)S(1)} %bitcast.15, ...), custom_call_target="tpu_custom_call" | custom-call | flops 1000 | bytes 1000 | tf_op jit(solution)/shard_map/pallas_call | solution.py:46
  190.7 2.6 %collective-permute-start.23 = (bf16[128,2560]{1,0:T(8,128)(2,1)S(1)}, bf16[128,2560]{1,0:T(8,128)(2,1)S(1)}, u32[]{:S(2)}, u32[]{:S(2)}) collective-permute-start(bf16[128,2560]{1,0:T(8,128)(2,1)S(1)} %shard_map.152.refs_2_), channel_id=1, source_target_pairs={{0,4},{2,6},{4,0},{6,2},{8,12},{10,14},{12,8},{14,10},{1,5},{3,7},... | collective-permute-start | bytes 1966088 | tf_op jit(solution)/shard_map/ppermute | solution.py:460
  193.8 4.6 %shard_map.154 = (bf16[3,64,3200]{2,1,0:T(8,128)(2,1)S(1)}, bf16[3,64,3200]{2,1,0:T(8,128)(2,1)}) custom-call(s32[19]{0:T(128)S(1)} %concatenate.10.m, bf16[512,128]{1,0:T(8,128)(2,1)S(1)} %get-tuple-element.49.refs_5_.refs_0_, bf16[512,3200]{1,0:T(8,128)(2,1)S(1)} %copy-done.28, bf16[128,2560]{1,0:T(8,128)(2,1)S(1)} %shard_map.153.refs_2_), custom_call_target="tpu_custom_call" | custom-call | flops 1000 | bytes 1000 | tf_op jit(solution)/shard_map/pallas_call | solution.py:46
  198.4 3.5 %collective-permute-start.27 = (bf16[3,64,3200]{2,1,0:T(8,128)(2,1)}, bf16[3,64,3200]{2,1,0:T(8,128)(2,1)S(1)}, u32[]{:S(2)}, u32[]{:S(2)}) collective-permute-start(bf16[3,64,3200]{2,1,0:T(8,128)(2,1)} %get-tuple-element.67), channel_id=1, source_target_pairs={{0,1},{1,0},{2,3},{3,2},{4,5},{5,4},{6,7},{7,6},{8,9},{9,8},{10,11... | collective-permute-start | bytes 3686408 | tf_op jit(solution)/shard_map/ppermute | solution.py:471
  207.2 4.2 %collective-permute-start.26 = (bf16[64,2560]{1,0:T(8,128)(2,1)S(1)}, bf16[64,2560]{1,0:T(8,128)(2,1)}, u32[]{:S(2)}, u32[]{:S(2)}) collective-permute-start(bf16[64,2560]{1,0:T(8,128)(2,1)S(1)} %get-tuple-element.66.refs_2_), channel_id=1, source_target_pairs={{0,1},{1,0},{2,3},{3,2},{4,5},{5,4},{6,7},{7,6},{8,9},{9,8},{10,11... | collective-permute-start | bytes 983048 | tf_op jit(solution)/shard_map/ppermute | solution.py:473
  213.1 2.1 maximum_select_fusion
  (145 shorter events, 58.8 us)
Async XLA Ops:
  0.6 43.2 %collective-permute-start.3 = (bf16[2560,3200]{1,0:T(8,128)(2,1)}, bf16[2560,3200]{1,0:T(8,128)(2,1)}, u32[]{:S(2)}, u32[]{:S(2)}) collective-permute-start(bf16[2560,3200]{1,0:T(8,128)(2,1)} %refs_8_.13), channel_id=1, source_target_pairs={{0,1},{1,0},{2,3},{3,2},{4,5},{5,4},{6,7},{7,6},{8,9},{9,8},{10,11... | collective-permute-start | bytes 49152008 | tf_op jit(solution)/shard_map/ppermute | solution.py:406
  0.8 18.4 %collective-permute-start.1 = (bf16[64,5120]{1,0:T(8,128)(2,1)}, bf16[64,5120]{1,0:T(8,128)(2,1)S(1)}, u32[]{:S(2)}, u32[]{:S(2)}) collective-permute-start(bf16[64,5120]{1,0:T(8,128)(2,1)} %refs_0_.9), channel_id=1, source_target_pairs={{0,4},{2,6},{4,0},{6,2},{8,12},{10,14},{12,8},{14,10},{1,5},{3,7},... | collective-permute-start | bytes 1966088 | tf_op jit(solution)/shard_map/ppermute | solution.py:407
  3.5 15.6 %collective-permute-start.4 = (bf16[64,5120]{1,0:T(8,128)(2,1)}, bf16[64,5120]{1,0:T(8,128)(2,1)}, u32[]{:S(2)}, u32[]{:S(2)}) collective-permute-start(bf16[64,5120]{1,0:T(8,128)(2,1)} %refs_0_.9), channel_id=1, source_target_pairs={{4,8},{6,10},{8,4},{10,6},{5,9},{7,11},{9,5},{11,7},{20,24},{22,26... | collective-permute-start | bytes 1966088 | tf_op jit(solution)/shard_map/ppermute | solution.py:408
  5.0 17.1 %collective-permute-start = (bf16[64,5120]{1,0:T(8,128)(2,1)}, bf16[64,5120]{1,0:T(8,128)(2,1)S(1)}, u32[]{:S(2)}, u32[]{:S(2)}) collective-permute-start(bf16[64,5120]{1,0:T(8,128)(2,1)} %refs_0_.9), channel_id=1, source_target_pairs={{0,2},{2,0},{4,6},{6,4},{8,10},{10,8},{12,14},{14,12},{1,3},{3,1},... | collective-permute-start | bytes 1966088 | tf_op jit(solution)/shard_map/ppermute | solution.py:409
  20.8 20.6 %collective-permute-start.5 = (bf16[64,5120]{1,0:T(8,128)(2,1)}, bf16[64,5120]{1,0:T(8,128)(2,1)}, u32[]{:S(2)}, u32[]{:S(2)}) collective-permute-start(bf16[64,5120]{1,0:T(8,128)(2,1)} %collective-permute-done.4), channel_id=1, source_target_pairs={{4,0},{6,2},{8,12},{10,14},{5,1},{7,3},{9,13},{11,15},{20,16},{22,... | collective-permute-start | bytes 1966088 | tf_op jit(solution)/shard_map/ppermute | solution.py:413
  22.1 20.4 %collective-permute-start.2 = (bf16[64,5120]{1,0:T(8,128)(2,1)S(1)}, bf16[64,5120]{1,0:T(8,128)(2,1)S(1)}, u32[]{:S(2)}, u32[]{:S(2)}) collective-permute-start(bf16[64,5120]{1,0:T(8,128)(2,1)S(1)} %collective-permute-done.1.refs_2_.refs_6_), channel_id=1, source_target_pairs={{0,2},{2,0},{4,6},{6,4},{8,10},{10,8},{12,14},{14,12},{1,3},{3,1},... | collective-permute-start | bytes 1966088 | tf_op jit(solution)/shard_map/ppermute | solution.py:411
  22.9 36.8 %collective-permute-start.8 = (bf16[64,5120]{1,0:T(8,128)(2,1)}, bf16[64,5120]{1,0:T(8,128)(2,1)S(1)}, u32[]{:S(2)}, u32[]{:S(2)}) collective-permute-start(bf16[64,5120]{1,0:T(8,128)(2,1)} %collective-permute-done.7), channel_id=1, source_target_pairs={{4,0},{6,2},{8,12},{10,14},{5,1},{7,3},{9,13},{11,15},{20,16},{22,... | collective-permute-start | bytes 1966088 | tf_op jit(solution)/shard_map/ppermute | solution.py:416
  42.5 17.2 %collective-permute-start.6 = (bf16[64,5120]{1,0:T(8,128)(2,1)S(1)}, bf16[64,5120]{1,0:T(8,128)(2,1)S(1)}, u32[]{:S(2)}, u32[]{:S(2)}) collective-permute-start(bf16[64,5120]{1,0:T(8,128)(2,1)S(1)} %broadcast_select_fusion.1.refs_4_.refs_0_), channel_id=1, source_target_pairs={{0,2},{2,0},{4,6},{6,4},{8,10},{10,8},{12,14},{14,12},{1,3},{3,1},... | collective-permute-start | bytes 1966088 | tf_op jit(solution)/shard_map/ppermute | solution.py:415
  60.7 14.7 %collective-permute-start.9 = (bf16[64,5120]{1,0:T(8,128)(2,1)S(1)}, bf16[64,5120]{1,0:T(8,128)(2,1)S(1)}, u32[]{:S(2)}, u32[]{:S(2)}) collective-permute-start(bf16[64,5120]{1,0:T(8,128)(2,1)S(1)} %broadcast_select_fusion.refs_6_.refs_2_), channel_id=1, source_target_pairs={{0,2},{2,0},{4,6},{6,4},{8,10},{10,8},{12,14},{14,12},{1,3},{3,1},... | collective-permute-start | bytes 1966088 | tf_op jit(solution)/shard_map/ppermute | solution.py:422
  76.4 8.4 %collective-permute-start.10 = (bf16[512,128]{1,0:T(8,128)(2,1)S(1)}, bf16[512,128]{1,0:T(8,128)(2,1)S(1)}, u32[]{:S(2)}, u32[]{:S(2)}) collective-permute-start(bf16[512,128]{1,0:T(8,128)(2,1)S(1)} %get-tuple-element.44.refs_10_), channel_id=1, source_target_pairs={{0,2},{2,0},{4,6},{6,4},{8,10},{10,8},{12,14},{14,12},{1,3},{3,1},... | collective-permute-start | bytes 393224 | tf_op jit(solution)/shard_map/ppermute | solution.py:429
  85.3 9.1 %collective-permute-start.11 = (bf16[512,128]{1,0:T(8,128)(2,1)S(1)}, bf16[512,128]{1,0:T(8,128)(2,1)S(1)}, u32[]{:S(2)}, u32[]{:S(2)}) collective-permute-start(bf16[512,128]{1,0:T(8,128)(2,1)S(1)} %get-tuple-element.46.refs_10_), channel_id=1, source_target_pairs={{0,4},{2,6},{4,0},{6,2},{8,12},{10,14},{12,8},{14,10},{1,5},{3,7},... | collective-permute-start | bytes 393224 | tf_op jit(solution)/shard_map/ppermute | solution.py:429
  112.0 16.8 %collective-permute-start.15 = (bf16[2,128,3200]{2,1,0:T(8,128)(2,1)}, bf16[2,128,3200]{2,1,0:T(8,128)(2,1)}, u32[]{:S(2)}, u32[]{:S(2)}) collective-permute-start(bf16[2,128,3200]{2,1,0:T(8,128)(2,1)} %shard_map.142.refs_4_.refs_0_), channel_id=1, source_target_pairs={{0,1},{1,0},{2,3},{3,2},{4,5},{5,4},{6,7},{7,6},{8,9},{9,8},{10,11... | collective-permute-start | bytes 4915208 | tf_op jit(solution)/shard_map/ppermute | solution.py:444
  128.8 20.4 %collective-permute-start.16 = (bf16[2,128,3200]{2,1,0:T(8,128)(2,1)S(1)}, bf16[2,128,3200]{2,1,0:T(8,128)(2,1)S(1)}, u32[]{:S(2)}, u32[]{:S(2)}) collective-permute-start(bf16[2,128,3200]{2,1,0:T(8,128)(2,1)S(1)} %shard_map.144.refs_4_.refs_0_), channel_id=1, source_target_pairs={{0,1},{1,0},{2,3},{3,2},{4,5},{5,4},{6,7},{7,6},{8,9},{9,8},{10,11... | collective-permute-start | bytes 4915208 | tf_op jit(solution)/shard_map/ppermute | solution.py:448
  130.1 16.3 %collective-permute-start.14 = (bf16[128,2560]{1,0:T(8,128)(2,1)S(1)}, bf16[128,2560]{1,0:T(8,128)(2,1)S(1)}, u32[]{:S(2)}, u32[]{:S(2)}) collective-permute-start(bf16[128,2560]{1,0:T(8,128)(2,1)S(1)} %get-tuple-element.51.refs_7_), channel_id=1, source_target_pairs={{0,2},{2,0},{4,6},{6,4},{8,10},{10,8},{12,14},{14,12},{1,3},{3,1},... | collective-permute-start | bytes 1966088 | tf_op jit(solution)/shard_map/ppermute | solution.py:439
  149.2 26.5 %collective-permute-start.17 = (bf16[2,128,3200]{2,1,0:T(8,128)(2,1)S(1)}, bf16[2,128,3200]{2,1,0:T(8,128)(2,1)S(1)}, u32[]{:S(2)}, u32[]{:S(2)}) collective-permute-start(bf16[2,128,3200]{2,1,0:T(8,128)(2,1)S(1)} %shard_map.147.refs_4_.refs_0_), channel_id=1, source_target_pairs={{0,1},{1,0},{2,3},{3,2},{4,5},{5,4},{6,7},{7,6},{8,9},{9,8},{10,11... | collective-permute-start | bytes 4915208 | tf_op jit(solution)/shard_map/ppermute | solution.py:453
  150.1 16.3 %collective-permute-start.19 = (bf16[128,2560]{1,0:T(8,128)(2,1)S(1)}, bf16[128,2560]{1,0:T(8,128)(2,1)S(1)}, u32[]{:S(2)}, u32[]{:S(2)}) collective-permute-start(bf16[128,2560]{1,0:T(8,128)(2,1)S(1)} %get-tuple-element.53.refs_2_), channel_id=1, source_target_pairs={{0,2},{2,0},{4,6},{6,4},{8,10},{10,8},{12,14},{14,12},{1,3},{3,1},... | collective-permute-start | bytes 1966088 | tf_op jit(solution)/shard_map/ppermute | solution.py:439
  150.6 16.6 %collective-permute-start.18 = (bf16[128,2560]{1,0:T(8,128)(2,1)S(1)}, bf16[128,2560]{1,0:T(8,128)(2,1)S(1)}, u32[]{:S(2)}, u32[]{:S(2)}) collective-permute-start(bf16[128,2560]{1,0:T(8,128)(2,1)S(1)} %shard_map.146.refs_7_.refs_0_), channel_id=1, source_target_pairs={{0,4},{2,6},{12,8},{14,10},{1,5},{3,7},{13,9},{15,11},{16,20},{18,... | collective-permute-start | bytes 1966088 | tf_op jit(solution)/shard_map/ppermute | solution.py:450
  167.8 20.7 %collective-permute-start.22 = (bf16[128,2560]{1,0:T(8,128)(2,1)S(1)}, bf16[128,2560]{1,0:T(8,128)(2,1)S(1)}, u32[]{:S(2)}, u32[]{:S(2)}) collective-permute-start(bf16[128,2560]{1,0:T(8,128)(2,1)S(1)} %shard_map.150.refs_4_), channel_id=1, source_target_pairs={{4,8},{6,10},{8,4},{10,6},{5,9},{7,11},{9,5},{11,7},{20,24},{22,26... | collective-permute-start | bytes 1966088 | tf_op jit(solution)/shard_map/ppermute | solution.py:457
  168.5 20.0 %collective-permute-start.21 = (bf16[128,2560]{1,0:T(8,128)(2,1)S(1)}, bf16[128,2560]{1,0:T(8,128)(2,1)S(1)}, u32[]{:S(2)}, u32[]{:S(2)}) collective-permute-start(bf16[128,2560]{1,0:T(8,128)(2,1)S(1)} %get-tuple-element.57.refs_2_), channel_id=1, source_target_pairs={{0,2},{2,0},{4,6},{6,4},{8,10},{10,8},{12,14},{14,12},{1,3},{3,1},... | collective-permute-start | bytes 1966088 | tf_op jit(solution)/shard_map/ppermute | solution.py:439
  169.4 19.9 %collective-permute-start.24 = (bf16[128,2560]{1,0:T(8,128)(2,1)S(1)}, bf16[128,2560]{1,0:T(8,128)(2,1)S(1)}, u32[]{:S(2)}, u32[]{:S(2)}) collective-permute-start(bf16[128,2560]{1,0:T(8,128)(2,1)S(1)} %shard_map.149.refs_2_.refs_0_), channel_id=1, source_target_pairs={{0,4},{2,6},{12,8},{14,10},{1,5},{3,7},{13,9},{15,11},{16,20},{18,... | collective-permute-start | bytes 1966088 | tf_op jit(solution)/shard_map/ppermute | solution.py:455
  190.0 13.8 %collective-permute-start.25 = (bf16[128,2560]{1,0:T(8,128)(2,1)S(1)}, bf16[128,2560]{1,0:T(8,128)(2,1)S(1)}, u32[]{:S(2)}, u32[]{:S(2)}) collective-permute-start(bf16[128,2560]{1,0:T(8,128)(2,1)S(1)} %shard_map.153.refs_2_), channel_id=1, source_target_pairs={{4,8},{6,10},{8,4},{10,6},{5,9},{7,11},{9,5},{11,7},{20,24},{22,26... | collective-permute-start | bytes 1966088 | tf_op jit(solution)/shard_map/ppermute | solution.py:462
  190.7 14.7 %collective-permute-start.23 = (bf16[128,2560]{1,0:T(8,128)(2,1)S(1)}, bf16[128,2560]{1,0:T(8,128)(2,1)S(1)}, u32[]{:S(2)}, u32[]{:S(2)}) collective-permute-start(bf16[128,2560]{1,0:T(8,128)(2,1)S(1)} %shard_map.152.refs_2_), channel_id=1, source_target_pairs={{0,4},{2,6},{4,0},{6,2},{8,12},{10,14},{12,8},{14,10},{1,5},{3,7},... | collective-permute-start | bytes 1966088 | tf_op jit(solution)/shard_map/ppermute | solution.py:460
  193.3 13.0 %collective-permute-start.20 = (bf16[128,2560]{1,0:T(8,128)(2,1)S(1)}, bf16[128,2560]{1,0:T(8,128)(2,1)S(1)}, u32[]{:S(2)}, u32[]{:S(2)}) collective-permute-start(bf16[128,2560]{1,0:T(8,128)(2,1)S(1)} %get-tuple-element.59.refs_3_), channel_id=1, source_target_pairs={{0,2},{2,0},{4,6},{6,4},{8,10},{10,8},{12,14},{14,12},{1,3},{3,1},... | collective-permute-start | bytes 1966088 | tf_op jit(solution)/shard_map/ppermute | solution.py:439
  198.4 16.8 %collective-permute-start.27 = (bf16[3,64,3200]{2,1,0:T(8,128)(2,1)}, bf16[3,64,3200]{2,1,0:T(8,128)(2,1)S(1)}, u32[]{:S(2)}, u32[]{:S(2)}) collective-permute-start(bf16[3,64,3200]{2,1,0:T(8,128)(2,1)} %get-tuple-element.67), channel_id=1, source_target_pairs={{0,1},{1,0},{2,3},{3,2},{4,5},{5,4},{6,7},{7,6},{8,9},{9,8},{10,11... | collective-permute-start | bytes 3686408 | tf_op jit(solution)/shard_map/ppermute | solution.py:471
  (41 other events, 328.5 us)

commit v6 on v5

--- a/solution.py
+++ b/solution.py
@@ -222,36 +222,43 @@
     )
 
 
-def input_grad_kernel(m, mine_ref, other_ref, gate_ref, up_ref, keep_ref, send_ref, lhs):
-    rows = mine_ref.shape[1] // 2
+def input_grad_kernel(count, m, *refs):
+    mine, other = refs[:count], refs[count : 2 * count]
+    gate_ref, up_ref = refs[2 * count : 2 * count + 2]
+    outs, lhs = refs[2 * count + 2 : -1], refs[-1]
+    rows = mine[0].shape[1] // 2
 
     @pl.when(pl.program_id(0) == 0)
     def _():
-        for i in range(2):
-            for y in range(2):
-                lhs[i, (2 * y) * rows : (2 * y + 1) * rows] = mine_ref[i, y * rows : (y + 1) * rows]
-                lhs[i, (2 * y + 1) * rows : (2 * y + 2) * rows] = other_ref[i, y * rows : (y + 1) * rows]
+        for s in range(count):
+            for i in range(2):
+                for y in range(2):
+                    for k, ref in enumerate((mine[s], other[s])):
+                        to = (4 * s + 2 * y + k) * rows
+                        lhs[i, to : to + rows] = ref[i, y * rows : (y + 1) * rows]
 
     total = nt_dot(lhs[0], gate_ref[...]) + nt_dot(lhs[1], up_ref[...])
-    keep_ref[...] = total[: 2 * rows].astype(BF16)
-    send_ref[...] = total[2 * rows :].astype(BF16)
+    for k, ref in enumerate(outs):
+        ref[...] = total[2 * k * rows : 2 * (k + 1) * rows].astype(BF16)
 
 
 def input_grad_parts(meta, mine, other, gate, up, after=()):
-    rows, width = mine.shape[1:]
+    count = len(mine)
+    rows, width = mine[0].shape[1:]
     half = gate.shape[0]
-    step = 512
+    step = 512 // count
+    one = pl.Buffered(1) if count > 1 else None
     out = jax.ShapeDtypeStruct((rows, half), BF16)
     return call(
-        input_grad_kernel,
-        meta,
-        (mine, other, gate, up),
+        functools.partial(input_grad_kernel, count),
+        meta,
+        (*mine, *other, gate, up),
         (half // step,),
-        [pl.BlockSpec((2, rows, width), lambda n, m: (0, 0, 0))] * 2
+        [pl.BlockSpec((2, rows, width), lambda n, m: (0, 0, 0), pipeline_mode=one)] * (2 * count)
         + [pl.BlockSpec((step, width), lambda n, m: (n, 0))] * 2,
-        [pl.BlockSpec((rows, step), lambda n, m: (0, n))] * 2,
-        [out, out],
-        scratch=[pltpu.VMEM((2, 2 * rows, width), BF16)],
+        [pl.BlockSpec((rows, step), lambda n, m: (0, n))] * (2 * count),
+        [out] * (2 * count),
+        scratch=[pltpu.VMEM((2, 2 * count * rows, width), BF16)],
         after=after,
     )
 
@@ -435,46 +442,50 @@
         return act_grad(meta, slot, spans, hgs, gate_act, up_act, low, a_t, after)
 
     def parts(mine, other, after):
-        keep, give = input_grad_parts(meta, mine, other, gate_matrix, up_matrix, after)
-        return keep, send(give, perm=Y_SWAP), give
+        return input_grad_parts(meta, mine, other, gate_matrix, up_matrix, after)
 
     mine3 = grads(3, ())
     other3 = swap_cores(mine3)
     mine2 = grads(2, (mine3,))
     other2 = swap_cores(tied(mine2, other3))
-    keep3, got3, give3 = parts(mine3, other3, (mine2,))
-    mine1 = grads(1, (give3,))
-    keep2, got2, give2 = parts(mine2, other2, (mine1,))
+    mine1 = grads(1, (mine2,))
     other1 = swap_cores(tied(mine1, other2))
+    keep3, give3 = parts((mine3,), (other3,), (mine1,))
+    got3 = send(give3, perm=Y_SWAP)
+    keep2, give2, keep1, give1 = parts((mine2, mine1), (other2, other1), (give3,))
+    got2 = send(give2, perm=Y_SWAP)
     sum3 = add_after(meta, (keep3, got3), (give2,))
     far_in = send(sum3, perm=INWARD)
     mine0 = grads(0, (sum3,))
-    keep1, got1, give1 = parts(mine1, other1, (mine0,))
-    other0 = swap_cores(tied(mine0, other1))
-    sum2 = add_after(meta, (keep2, got2), (give1,))
+    other0 = swap_cores(mine0)
+    owned = adapters // 2
+    keep_a, give_a = owner_grads(meta, low, 0, hidden, owned, (mine0,))
+    keep_b, give_b = owner_grads(meta, low, 1, columns, owned, (keep_a,))
+    got_a, got_b = swap_cores(give_a), swap_cores(give_b)
+    sum2 = add_after(meta, (keep2, got2), (keep_b,))
     mid_in = send(sum2, perm=INWARD)
     sum3 = add_after(meta, (sum3, far_in), (sum2,))
     far_mid = send(sum3, perm=MID)
-    keep0, got0, give0 = parts(mine0, other0, (sum3,))
+    got1 = send(give1, perm=Y_SWAP)
+    keep0, give0 = parts((mine0,), (other0,), (sum3, got_a, got_b))
+    got0 = send(give0, perm=Y_SWAP)
     sum1 = add_after(meta, (keep1, got1, far_mid), (give0,))
     from_pair = send(sum1, perm=PAIR)
     sum2 = add_after(meta, (sum2, mid_in), (sum1,))
     from_mid = send(sum2, perm=MID)
-    owned = adapters // 2
-    keep_a, give_a = owner_grads(meta, low, 0, hidden, owned, (sum2,))
-    keep_b, give_b = owner_grads(meta, low, 1, columns, owned, (keep_a,))
-    own, give = final_sum(meta, (keep0, got0, from_pair, from_mid), (keep_b,))
-    grad_b = add(keep_b, swap_cores(give_b))
-    shape = keep_a.shape
-    flat = (shape[0] * shape[1], shape[2])
-    grad_a = add_after(
-        meta, (keep_a.reshape(flat), swap_cores(give_a).reshape(flat)), (give,), steps=2
-    )
+
+    def owner_sum(keep, got):
+        flat = (keep.shape[0] * keep.shape[1], keep.shape[2])
+        out = add_after(meta, (keep.reshape(flat), got.reshape(flat)), (sum2,), steps=2)
+        return out.reshape(keep.shape)
+
+    grad_a, grad_b = owner_sum(keep_a, got_a), owner_sum(keep_b, got_b)
+    own, give = final_sum(meta, (keep0, got0, from_pair, from_mid), (grad_a, grad_b))
     got = swap_cores(give)
     input_grad = jnp.where(
         d == 0, jnp.concatenate([own, got], axis=1), jnp.concatenate([got, own], axis=1)
     )
-    grad_a = jnp.swapaxes(grad_a.reshape(shape), 1, 2)
+    grad_a = jnp.swapaxes(grad_a, 1, 2)
     return (input_grad, grad_a, grad_b)
 
 

time: 218 us -> 248 us (1.14)
  local copies, waits for them, and re-layouts: 20.2 us -> 47.4 us
  waiting for transfers between devices: 22.7 us -> 36.1 us
  starting transfers between devices: 44.7 us -> 39.9 us
  Pallas kernels: 121 us -> 118 us
  other arithmetic: 6.93 us -> 4.16 us
    unnamed x72 -> x132, local copies, waits for them, and re-layouts: 19.4 us -> 46.6 us
    ppermute x1, waiting for transfers between devices: 1.59 us -> 8.74 us  [grid_body(): from_pair = send(sum1, perm=PAIR)]
    ppermute x7, waiting for transfers between devices: 3.48 us -> 7.52 us  [the longest x1 6.61 us: grid_body(): got2 = send(give2, perm=Y_SWAP)]
    pallas_call x28, Pallas kernels: 121 us -> 118 us  [call(): pl.pallas_call(run, grid_spec=pltpu.PrefetchScalarGridSpec(num_scalar_pre...]
  transfers between devices with their start and end apart: 29 -> 29, of which waited for: 6 -> 6; matrix products, arithmetic and copies ran while one was open for 4% -> 2% of each run, Pallas kernels for 52% -> 43%
where the time goes in v6:
time: 248 us; the launch traced here: 247 us
  Pallas kernels  118 us (48%)
  local copies, waits for them, and re-layouts  47.4 us (19%)
  starting transfers between devices  39.9 us (16%)
  waiting for transfers between devices  36.1 us (15%)
  other arithmetic  4.16 us (2%)
    pallas_call x28, Pallas kernels, call(): pl.pallas_call(run, grid_spec=pltpu.PrefetchScalarGridSpec(num_scalar_pre...  118 us
    unnamed x132, local copies, waits for them, and re-layouts  46.6 us
    ppermute x1, waiting for transfers between devices, grid_body(): mid_out = send(tied(mid, low_in), perm=OUTWARD)  17.2 us
    ppermute x1, waiting for transfers between devices, grid_body(): from_pair = send(sum1, perm=PAIR)  8.74 us
    ppermute x1, waiting for transfers between devices, grid_body(): got2 = send(give2, perm=Y_SWAP)  6.61 us
    ppermute x1, starting transfers between devices, grid_body(): mid_in = send(sum2, perm=INWARD)  5.51 us
  transfers between devices with their start and end apart: 29, of which 6 were waited for; matrix products, arithmetic and copies ran while one was open for 2% of the time, Pallas kernels for 43%

profile of v6, /device:TPU:1, one launch (start us, length us, event | category | flops | bytes accessed | tf_op | source)
XLA Modules:
  0.0 246.7 jit_solution(1636600501710579587)
XLA Ops:
  0.8 2.8 %collective-permute-start.1 = (bf16[64,5120]{1,0:T(8,128)(2,1)}, bf16[64,5120]{1,0:T(8,128)(2,1)S(1)}, u32[]{:S(2)}, u32[]{:S(2)}) collective-permute-start(bf16[64,5120]{1,0:T(8,128)(2,1)} %refs_0_.9), channel_id=1, source_target_pairs={{0,4},{2,6},{4,0},{6,2},{8,12},{10,14},{12,8},{14,10},{1,5},{3,7},... | collective-permute-start | bytes 1966088 | tf_op jit(solution)/shard_map/ppermute | solution.py:414
  14.6 2.9 %shard_map.130 = (bf16[512,3200]{1,0:T(8,128)(2,1)S(1)}, f32[256,128]{1,0:T(8,128)S(1)}) custom-call(s32[19]{0:T(128)S(1)} %concatenate.10.m, bf16[512,3200]{1,0:T(8,128)(2,1)S(1)} %copy-done.3, bf16[512,3200]{1,0:T(8,128)(2,1)S(1)} %copy-done.6, bf16[6,64,3200]{2,1,0:T(8,128)(2,1)S(1)} %bitcast.21), custom_call_target="tpu_custom_call" | custom-call | flops 1000 | bytes 1000 | tf_op jit(solution)/shard_map/pallas_call | solution.py:46
  24.1 17.2 %collective-permute-done.5 = bf16[64,5120]{1,0:T(8,128)(2,1)} collective-permute-done((bf16[64,5120]{1,0:T(8,128)(2,1)}, bf16[64,5120]{1,0:T(8,128)(2,1)}, u32[]{:S(2)}, u32[]{:S(2)}) %collective-permute-start.5) | collective-permute-done | bytes 655392 | tf_op jit(solution)/shard_map/ppermute | solution.py:420
  43.9 5.6 %copy-done = bf16[2560,3200]{1,0:T(8,128)(2,1)S(1)} copy-done((bf16[2560,3200]{1,0:T(8,128)(2,1)S(1)}, bf16[2560,3200]{1,0:T(8,128)(2,1)}, u32[]{:S(2)}) %copy-start) | copy-done | bytes 16384024
  51.7 7.9 %shard_map.131.refs_10_.refs_0_ = f32[256,1280]{1,0:T(8,128)S(1)} custom-call(s32[19]{0:T(128)S(1)} %concatenate.10.m, bf16[64,5120]{1,0:T(8,128)(2,1)S(1)} %copy-done.12, bf16[64,5120]{1,0:T(8,128)(2,1)S(1)} %copy-done.17, bf16[64,5120]{1,0:T(8,128)(2,1)S(1)} %copy-done.14, bf16[64,5120]{1,0:T(8,128)(2,1)S(1)} %collective-permute-done.2.refs_3_.refs_7_, ...), custom_call_target="tpu_custom_call" | custom-call | flops 1000 | bytes 1000 | tf_op jit(solution)/shard_map/pallas_call | solution.py:46
  62.7 7.5 %shard_map.132.refs_10_.refs_1_ = f32[256,1280]{1,0:T(8,128)S(1)} custom-call(s32[19]{0:T(128)S(1)} %concatenate.10.m, bf16[64,5120]{1,0:T(8,128)(2,1)S(1)} %copy-done.12, bf16[64,5120]{1,0:T(8,128)(2,1)S(1)} %copy-done.18, bf16[64,5120]{1,0:T(8,128)(2,1)S(1)} %copy-done.15, bf16[64,5120]{1,0:T(8,128)(2,1)S(1)} %collective-permute-done.2.refs_3_.refs_7_, ...), custom_call_target="tpu_custom_call" | custom-call | flops 1000 | bytes 1000 | tf_op jit(solution)/shard_map/pallas_call | solution.py:46
  70.2 5.1 %shard_map.133.refs_10_.refs_2_ = f32[256,640]{1,0:T(8,128)S(1)} custom-call(s32[19]{0:T(128)S(1)} %concatenate.10.m, bf16[64,5120]{1,0:T(8,128)(2,1)S(1)} %copy-done.12, bf16[64,5120]{1,0:T(8,128)(2,1)S(1)} %copy-done.18, bf16[64,5120]{1,0:T(8,128)(2,1)S(1)} %copy-done.15, bf16[64,5120]{1,0:T(8,128)(2,1)S(1)} %collective-permute-done.2.refs_3_.refs_7_, ...), custom_call_target="tpu_custom_call" | custom-call | flops 1000 | bytes 1000 | tf_op jit(solution)/shard_map/pallas_call | solution.py:46
  77.3 7.5 %shard_map.135.refs_2_.refs_0_ = f32[256,1280]{1,0:T(8,128)S(1)} custom-call(s32[19]{0:T(128)S(1)} %concatenate.10.m, bf16[64,5120]{1,0:T(8,128)(2,1)S(1)} %broadcast_select_fusion.1.refs_4_.refs_0_, bf16[64,5120]{1,0:T(8,128)(2,1)S(1)} %collective-permute-done.6.refs_5_.refs_1_, bf16[64,5120]{1,0:T(8,128)(2,1)S(1)} %broadcast_select_fusion.refs_6_.refs_2_, ...), custom_call_target="tpu_custom_call" | custom-call | flops 1000 | bytes 1000 | tf_op jit(solution)/shard_map/pallas_call | solution.py:46
  86.7 7.7 %shard_map.137.refs_2_.refs_1_ = f32[256,1280]{1,0:T(8,128)S(1)} custom-call(s32[19]{0:T(128)S(1)} %concatenate.10.m, bf16[64,5120]{1,0:T(8,128)(2,1)S(1)} %broadcast_select_fusion.1.refs_4_.refs_0_, bf16[64,5120]{1,0:T(8,128)(2,1)S(1)} %collective-permute-done.6.refs_5_.refs_1_, bf16[64,5120]{1,0:T(8,128)(2,1)S(1)} %broadcast_select_fusion.refs_6_.refs_2_, ...), custom_call_target="tpu_custom_call" | custom-call | flops 1000 | bytes 1000 | tf_op jit(solution)/shard_map/pallas_call | solution.py:46
  96.0 5.6 %shard_map.139.refs_2_ = f32[256,640]{1,0:T(8,128)S(1)} custom-call(s32[19]{0:T(128)S(1)} %concatenate.10.m, bf16[64,5120]{1,0:T(8,128)(2,1)S(1)} %broadcast_select_fusion.1.refs_4_.refs_0_, bf16[64,5120]{1,0:T(8,128)(2,1)S(1)} %copy-done.20, bf16[64,5120]{1,0:T(8,128)(2,1)S(1)} %broadcast_select_fusion.refs_6_.refs_2_, ...), custom_call_target="tpu_custom_call" | custom-call | flops 1000 | bytes 1000 | tf_op jit(solution)/shard_map/pallas_call | solution.py:46
  104.9 4.1 %collective-permute-start.13 = (bf16[2,128,3200]{2,1,0:T(8,128)(2,1)S(1)}, bf16[2,128,3200]{2,1,0:T(8,128)(2,1)S(1)}, u32[]{:S(2)}, u32[]{:S(2)}) collective-permute-start(bf16[2,128,3200]{2,1,0:T(8,128)(2,1)S(1)} %shard_map.141.refs_7_.refs_0_), channel_id=1, source_target_pairs={{0,1},{1,0},{2,3},{3,2},{4,5},{5,4},{6,7},{7,6},{8,9},{9,8},{10,11... | collective-permute-start | bytes 4915208 | tf_op jit(solution)/shard_map/ppermute | solution.py:448
  113.8 2.0 shard_map.143.refs_4_.refs_1_
  119.1 13.2 %shard_map.144 = (bf16[128,2560]{1,0:T(8,128)(2,1)S(1)}, bf16[128,2560]{1,0:T(8,128)(2,1)}) custom-call(s32[19]{0:T(128)S(1)} %concatenate.10.m, bf16[2,128,3200]{2,1,0:T(8,128)(2,1)S(1)} %shard_map.141.refs_7_.refs_0_, bf16[2,128,3200]{2,1,0:T(8,128)(2,1)S(1)} %collective-permute-done.13.refs_1_, bf16[2560,3200]{1,0:T(8,128)(2,1)S(1)} %bitcast.18, ...), custom_call_target="tpu_custom_call" | custom-call | flops 1000 | bytes 1000 | tf_op jit(solution)/shard_map/pallas_call | solution.py:46
  134.9 5.7 %copy-done.2 = bf16[2560,3200]{1,0:T(8,128)(2,1)S(1)} copy-done((bf16[2560,3200]{1,0:T(8,128)(2,1)S(1)}, bf16[2560,3200]{1,0:T(8,128)(2,1)}, u32[]{:S(2)}) %copy-start.2) | copy-done | bytes 16384024
  144.8 22.5 %shard_map.145 = (bf16[128,2560]{1,0:T(8,128)(2,1)S(1)}, bf16[128,2560]{1,0:T(8,128)(2,1)S(1)}, bf16[128,2560]{1,0:T(8,128)(2,1)S(1)}, bf16[128,2560]{1,0:T(8,128)(2,1)S(1)}) custom-call(s32[19]{0:T(128)S(1)} %concatenate.10.m, bf16[2,128,3200]{2,1,0:T(8,128)(2,1)S(1)} %copy-done.32, bf16[2,128,3200]{2,1,0:T(8,128)(2,1)S(1)} %copy-done.34, ...), custom_call_target="tpu_custom_call" | custom-call | flops 1000 | bytes 1000 | tf_op jit(solution)/shard_map/pallas_call | solution.py:46
  180.1 2.0 shard_map.147.refs_2_.refs_0_
  183.6 2.5 %collective-permute-start.18 = (bf16[128,2560]{1,0:T(8,128)(2,1)S(1)}, bf16[128,2560]{1,0:T(8,128)(2,1)S(1)}, u32[]{:S(2)}, u32[]{:S(2)}) collective-permute-start(bf16[128,2560]{1,0:T(8,128)(2,1)S(1)} %shard_map.146.refs_7_.refs_0_), channel_id=1, source_target_pairs={{0,4},{2,6},{12,8},{14,10},{1,5},{3,7},{13,9},{15,11},{16,20},{18,... | collective-permute-start | bytes 1966088 | tf_op jit(solution)/shard_map/ppermute | solution.py:458
  186.1 3.8 %shard_map.148 = (bf16[3,64,3200]{2,1,0:T(8,128)(2,1)S(1)}, bf16[3,64,3200]{2,1,0:T(8,128)(2,1)S(1)}) custom-call(s32[19]{0:T(128)S(1)} %concatenate.10.m, bf16[512,128]{1,0:T(8,128)(2,1)S(1)} %get-tuple-element.48.refs_5_.refs_0_, bf16[512,3200]{1,0:T(8,128)(2,1)S(1)} %copy-done.39, bf16[2,128,3200]{2,1,0:T(8,128)(2,1)S(1)} %shard_map.147.refs_2_.refs_0_), custom_call_target="tpu_custom_call" | custom-call | flops 1000 | bytes 1000 | tf_op jit(solution)/shard_map/pallas_call | solution.py:46
  192.1 6.6 %collective-permute-done.19.refs_1_ = bf16[128,2560]{1,0:T(8,128)(2,1)S(1)} collective-permute-done((bf16[128,2560]{1,0:T(8,128)(2,1)S(1)}, bf16[128,2560]{1,0:T(8,128)(2,1)S(1)}, u32[]{:S(2)}, u32[]{:S(2)}) %collective-permute-start.19) | collective-permute-done | bytes 655392 | tf_op jit(solution)/shard_map/ppermute | solution.py:456
  202.1 5.5 %collective-permute-start.26 = (bf16[128,2560]{1,0:T(8,128)(2,1)S(1)}, bf16[128,2560]{1,0:T(8,128)(2,1)S(1)}, u32[]{:S(2)}, u32[]{:S(2)}) collective-permute-start(bf16[128,2560]{1,0:T(8,128)(2,1)S(1)} %shard_map.150.refs_2_.refs_0_), channel_id=1, source_target_pairs={{0,4},{2,6},{12,8},{14,10},{1,5},{3,7},{13,9},{15,11},{16,20},{18,... | collective-permute-start | bytes 1966088 | tf_op jit(solution)/shard_map/ppermute | solution.py:466
  207.7 12.8 %shard_map.152 = (bf16[128,2560]{1,0:T(8,128)(2,1)S(1)}, bf16[128,2560]{1,0:T(8,128)(2,1)S(1)}) custom-call(s32[19]{0:T(128)S(1)} %concatenate.10.m, bf16[2,128,3200]{2,1,0:T(8,128)(2,1)S(1)} %shard_map.147.refs_2_.refs_0_, bf16[2,128,3200]{2,1,0:T(8,128)(2,1)S(1)} %collective-permute-done.17.refs_1_, bf16[2560,3200]{1,0:T(8,128)(2,1)S(1)} %bitcast.20, ...), custom_call_target="tpu_custom_call" | custom-call | flops 1000 | bytes 1000 | tf_op jit(solution)/shard_map/pallas_call | solution.py:46
  222.7 2.7 %collective-permute-start.25 = (bf16[128,2560]{1,0:T(8,128)(2,1)S(1)}, bf16[128,2560]{1,0:T(8,128)(2,1)S(1)}, u32[]{:S(2)}, u32[]{:S(2)}) collective-permute-start(bf16[128,2560]{1,0:T(8,128)(2,1)S(1)} %shard_map.153.refs_2_), channel_id=1, source_target_pairs={{0,4},{2,6},{4,0},{6,2},{8,12},{10,14},{12,8},{14,10},{1,5},{3,7},... | collective-permute-start | bytes 1966088 | tf_op jit(solution)/shard_map/ppermute | solution.py:473
  228.9 8.7 %collective-permute-done.25.refs_2_ = bf16[128,2560]{1,0:T(8,128)(2,1)S(1)} collective-permute-done((bf16[128,2560]{1,0:T(8,128)(2,1)S(1)}, bf16[128,2560]{1,0:T(8,128)(2,1)S(1)}, u32[]{:S(2)}, u32[]{:S(2)}) %collective-permute-start.25) | collective-permute-done | bytes 655392 | tf_op jit(solution)/shard_map/ppermute | solution.py:473
  240.4 4.0 %collective-permute-start.28 = (bf16[64,2560]{1,0:T(8,128)(2,1)S(1)}, bf16[64,2560]{1,0:T(8,128)(2,1)S(1)}, u32[]{:S(2)}, u32[]{:S(2)}) collective-permute-start(bf16[64,2560]{1,0:T(8,128)(2,1)S(1)} %get-tuple-element.66), channel_id=1, source_target_pairs={{0,1},{1,0},{2,3},{3,2},{4,5},{5,4},{6,7},{7,6},{8,9},{9,8},{10,11... | collective-permute-start | bytes 983048 | tf_op jit(solution)/shard_map/ppermute | solution.py:484
  (205 shorter events, 79.3 us)
Async XLA Ops:
  0.6 43.2 %collective-permute-start.3 = (bf16[2560,3200]{1,0:T(8,128)(2,1)}, bf16[2560,3200]{1,0:T(8,128)(2,1)}, u32[]{:S(2)}, u32[]{:S(2)}) collective-permute-start(bf16[2560,3200]{1,0:T(8,128)(2,1)} %refs_8_.13), channel_id=1, source_target_pairs={{0,1},{1,0},{2,3},{3,2},{4,5},{5,4},{6,7},{7,6},{8,9},{9,8},{10,11... | collective-permute-start | bytes 49152008 | tf_op jit(solution)/shard_map/ppermute | solution.py:413
  0.8 18.4 %collective-permute-start.1 = (bf16[64,5120]{1,0:T(8,128)(2,1)}, bf16[64,5120]{1,0:T(8,128)(2,1)S(1)}, u32[]{:S(2)}, u32[]{:S(2)}) collective-permute-start(bf16[64,5120]{1,0:T(8,128)(2,1)} %refs_0_.9), channel_id=1, source_target_pairs={{0,4},{2,6},{4,0},{6,2},{8,12},{10,14},{12,8},{14,10},{1,5},{3,7},... | collective-permute-start | bytes 1966088 | tf_op jit(solution)/shard_map/ppermute | solution.py:414
  3.5 15.6 %collective-permute-start.4 = (bf16[64,5120]{1,0:T(8,128)(2,1)}, bf16[64,5120]{1,0:T(8,128)(2,1)}, u32[]{:S(2)}, u32[]{:S(2)}) collective-permute-start(bf16[64,5120]{1,0:T(8,128)(2,1)} %refs_0_.9), channel_id=1, source_target_pairs={{4,8},{6,10},{8,4},{10,6},{5,9},{7,11},{9,5},{11,7},{20,24},{22,26... | collective-permute-start | bytes 1966088 | tf_op jit(solution)/shard_map/ppermute | solution.py:415
  5.0 17.1 %collective-permute-start = (bf16[64,5120]{1,0:T(8,128)(2,1)}, bf16[64,5120]{1,0:T(8,128)(2,1)S(1)}, u32[]{:S(2)}, u32[]{:S(2)}) collective-permute-start(bf16[64,5120]{1,0:T(8,128)(2,1)} %refs_0_.9), channel_id=1, source_target_pairs={{0,2},{2,0},{4,6},{6,4},{8,10},{10,8},{12,14},{14,12},{1,3},{3,1},... | collective-permute-start | bytes 1966088 | tf_op jit(solution)/shard_map/ppermute | solution.py:416
  20.8 20.6 %collective-permute-start.5 = (bf16[64,5120]{1,0:T(8,128)(2,1)}, bf16[64,5120]{1,0:T(8,128)(2,1)}, u32[]{:S(2)}, u32[]{:S(2)}) collective-permute-start(bf16[64,5120]{1,0:T(8,128)(2,1)} %collective-permute-done.4), channel_id=1, source_target_pairs={{4,0},{6,2},{8,12},{10,14},{5,1},{7,3},{9,13},{11,15},{20,16},{22,... | collective-permute-start | bytes 1966088 | tf_op jit(solution)/shard_map/ppermute | solution.py:420
  22.1 20.4 %collective-permute-start.2 = (bf16[64,5120]{1,0:T(8,128)(2,1)S(1)}, bf16[64,5120]{1,0:T(8,128)(2,1)S(1)}, u32[]{:S(2)}, u32[]{:S(2)}) collective-permute-start(bf16[64,5120]{1,0:T(8,128)(2,1)S(1)} %collective-permute-done.1.refs_2_.refs_6_), channel_id=1, source_target_pairs={{0,2},{2,0},{4,6},{6,4},{8,10},{10,8},{12,14},{14,12},{1,3},{3,1},... | collective-permute-start | bytes 1966088 | tf_op jit(solution)/shard_map/ppermute | solution.py:418
  22.9 36.8 %collective-permute-start.8 = (bf16[64,5120]{1,0:T(8,128)(2,1)}, bf16[64,5120]{1,0:T(8,128)(2,1)S(1)}, u32[]{:S(2)}, u32[]{:S(2)}) collective-permute-start(bf16[64,5120]{1,0:T(8,128)(2,1)} %collective-permute-done.7), channel_id=1, source_target_pairs={{4,0},{6,2},{8,12},{10,14},{5,1},{7,3},{9,13},{11,15},{20,16},{22,... | collective-permute-start | bytes 1966088 | tf_op jit(solution)/shard_map/ppermute | solution.py:423
  42.5 17.2 %collective-permute-start.6 = (bf16[64,5120]{1,0:T(8,128)(2,1)S(1)}, bf16[64,5120]{1,0:T(8,128)(2,1)S(1)}, u32[]{:S(2)}, u32[]{:S(2)}) collective-permute-start(bf16[64,5120]{1,0:T(8,128)(2,1)S(1)} %broadcast_select_fusion.1.refs_4_.refs_0_), channel_id=1, source_target_pairs={{0,2},{2,0},{4,6},{6,4},{8,10},{10,8},{12,14},{14,12},{1,3},{3,1},... | collective-permute-start | bytes 1966088 | tf_op jit(solution)/shard_map/ppermute | solution.py:422
  60.7 14.7 %collective-permute-start.9 = (bf16[64,5120]{1,0:T(8,128)(2,1)S(1)}, bf16[64,5120]{1,0:T(8,128)(2,1)S(1)}, u32[]{:S(2)}, u32[]{:S(2)}) collective-permute-start(bf16[64,5120]{1,0:T(8,128)(2,1)S(1)} %broadcast_select_fusion.refs_6_.refs_2_), channel_id=1, source_target_pairs={{0,2},{2,0},{4,6},{6,4},{8,10},{10,8},{12,14},{14,12},{1,3},{3,1},... | collective-permute-start | bytes 1966088 | tf_op jit(solution)/shard_map/ppermute | solution.py:429
  76.4 8.4 %collective-permute-start.10 = (bf16[512,128]{1,0:T(8,128)(2,1)S(1)}, bf16[512,128]{1,0:T(8,128)(2,1)S(1)}, u32[]{:S(2)}, u32[]{:S(2)}) collective-permute-start(bf16[512,128]{1,0:T(8,128)(2,1)S(1)} %get-tuple-element.43.refs_10_), channel_id=1, source_target_pairs={{0,2},{2,0},{4,6},{6,4},{8,10},{10,8},{12,14},{14,12},{1,3},{3,1},... | collective-permute-start | bytes 393224 | tf_op jit(solution)/shard_map/ppermute | solution.py:436
  85.4 9.0 %collective-permute-start.11 = (bf16[512,128]{1,0:T(8,128)(2,1)S(1)}, bf16[512,128]{1,0:T(8,128)(2,1)S(1)}, u32[]{:S(2)}, u32[]{:S(2)}) collective-permute-start(bf16[512,128]{1,0:T(8,128)(2,1)S(1)} %get-tuple-element.45.refs_10_), channel_id=1, source_target_pairs={{0,4},{2,6},{4,0},{6,2},{8,12},{10,14},{12,8},{14,10},{1,5},{3,7},... | collective-permute-start | bytes 393224 | tf_op jit(solution)/shard_map/ppermute | solution.py:436
  104.9 8.8 %collective-permute-start.13 = (bf16[2,128,3200]{2,1,0:T(8,128)(2,1)S(1)}, bf16[2,128,3200]{2,1,0:T(8,128)(2,1)S(1)}, u32[]{:S(2)}, u32[]{:S(2)}) collective-permute-start(bf16[2,128,3200]{2,1,0:T(8,128)(2,1)S(1)} %shard_map.141.refs_7_.refs_0_), channel_id=1, source_target_pairs={{0,1},{1,0},{2,3},{3,2},{4,5},{5,4},{6,7},{7,6},{8,9},{9,8},{10,11... | collective-permute-start | bytes 4915208 | tf_op jit(solution)/shard_map/ppermute | solution.py:448
  117.2 16.5 %collective-permute-start.16 = (bf16[2,128,3200]{2,1,0:T(8,128)(2,1)S(1)}, bf16[2,128,3200]{2,1,0:T(8,128)(2,1)S(1)}, u32[]{:S(2)}, u32[]{:S(2)}) collective-permute-start(bf16[2,128,3200]{2,1,0:T(8,128)(2,1)S(1)} %shard_map.143.refs_4_.refs_1_), channel_id=1, source_target_pairs={{0,1},{1,0},{2,3},{3,2},{4,5},{5,4},{6,7},{7,6},{8,9},{9,8},{10,11... | collective-permute-start | bytes 4915208 | tf_op jit(solution)/shard_map/ppermute | solution.py:452
  133.2 36.7 %collective-permute-start.14 = (bf16[128,2560]{1,0:T(8,128)(2,1)}, bf16[128,2560]{1,0:T(8,128)(2,1)}, u32[]{:S(2)}, u32[]{:S(2)}) collective-permute-start(bf16[128,2560]{1,0:T(8,128)(2,1)} %get-tuple-element.50.refs_6_), channel_id=1, source_target_pairs={{0,2},{2,0},{4,6},{6,4},{8,10},{10,8},{12,14},{14,12},{1,3},{3,1},... | collective-permute-start | bytes 1966088 | tf_op jit(solution)/shard_map/ppermute | solution.py:454
  182.1 25.5 %collective-permute-start.17 = (bf16[2,128,3200]{2,1,0:T(8,128)(2,1)S(1)}, bf16[2,128,3200]{2,1,0:T(8,128)(2,1)S(1)}, u32[]{:S(2)}, u32[]{:S(2)}) collective-permute-start(bf16[2,128,3200]{2,1,0:T(8,128)(2,1)S(1)} %shard_map.147.refs_2_.refs_0_), channel_id=1, source_target_pairs={{0,1},{1,0},{2,3},{3,2},{4,5},{5,4},{6,7},{7,6},{8,9},{9,8},{10,11... | collective-permute-start | bytes 4915208 | tf_op jit(solution)/shard_map/ppermute | solution.py:460
  182.6 16.2 %collective-permute-start.19 = (bf16[128,2560]{1,0:T(8,128)(2,1)S(1)}, bf16[128,2560]{1,0:T(8,128)(2,1)S(1)}, u32[]{:S(2)}, u32[]{:S(2)}) collective-permute-start(bf16[128,2560]{1,0:T(8,128)(2,1)S(1)} %copy-done.52), channel_id=1, source_target_pairs={{0,2},{2,0},{4,6},{6,4},{8,10},{10,8},{12,14},{14,12},{1,3},{3,1},... | collective-permute-start | bytes 1966088 | tf_op jit(solution)/shard_map/ppermute | solution.py:456
  183.6 16.9 %collective-permute-start.18 = (bf16[128,2560]{1,0:T(8,128)(2,1)S(1)}, bf16[128,2560]{1,0:T(8,128)(2,1)S(1)}, u32[]{:S(2)}, u32[]{:S(2)}) collective-permute-start(bf16[128,2560]{1,0:T(8,128)(2,1)S(1)} %shard_map.146.refs_7_.refs_0_), channel_id=1, source_target_pairs={{0,4},{2,6},{12,8},{14,10},{1,5},{3,7},{13,9},{15,11},{16,20},{18,... | collective-permute-start | bytes 1966088 | tf_op jit(solution)/shard_map/ppermute | solution.py:458
  190.0 17.6 %collective-permute-start.20 = (bf16[3,64,3200]{2,1,0:T(8,128)(2,1)S(1)}, bf16[3,64,3200]{2,1,0:T(8,128)(2,1)S(1)}, u32[]{:S(2)}, u32[]{:S(2)}) collective-permute-start(bf16[3,64,3200]{2,1,0:T(8,128)(2,1)S(1)} %get-tuple-element.59), channel_id=1, source_target_pairs={{0,1},{1,0},{2,3},{3,2},{4,5},{5,4},{6,7},{7,6},{8,9},{9,8},{10,11... | collective-permute-start | bytes 3686408 | tf_op jit(solution)/shard_map/ppermute | solution.py:464
  192.0 10.0 %collective-permute-start.21 = (bf16[3,64,640]{2,1,0:T(8,128)(2,1)S(1)}, bf16[3,64,640]{2,1,0:T(8,128)(2,1)S(1)}, u32[]{:S(2)}, u32[]{:S(2)}) collective-permute-start(bf16[3,64,640]{2,1,0:T(8,128)(2,1)S(1)} %get-tuple-element.60), channel_id=1, source_target_pairs={{0,1},{1,0},{2,3},{3,2},{4,5},{5,4},{6,7},{7,6},{8,9},{9,8},{10,11... | collective-permute-start | bytes 737288 | tf_op jit(solution)/shard_map/ppermute | solution.py:464
  198.7 21.8 %collective-permute-start.23 = (bf16[128,2560]{1,0:T(8,128)(2,1)S(1)}, bf16[128,2560]{1,0:T(8,128)(2,1)S(1)}, u32[]{:S(2)}, u32[]{:S(2)}) collective-permute-start(bf16[128,2560]{1,0:T(8,128)(2,1)S(1)} %copy-done.57), channel_id=1, source_target_pairs={{0,2},{2,0},{4,6},{6,4},{8,10},{10,8},{12,14},{14,12},{1,3},{3,1},... | collective-permute-start | bytes 1966088 | tf_op jit(solution)/shard_map/ppermute | solution.py:469
  201.2 19.3 %collective-permute-start.24 = (bf16[128,2560]{1,0:T(8,128)(2,1)S(1)}, bf16[128,2560]{1,0:T(8,128)(2,1)S(1)}, u32[]{:S(2)}, u32[]{:S(2)}) collective-permute-start(bf16[128,2560]{1,0:T(8,128)(2,1)S(1)} %shard_map.151.refs_4_), channel_id=1, source_target_pairs={{4,8},{6,10},{8,4},{10,6},{5,9},{7,11},{9,5},{11,7},{20,24},{22,26... | collective-permute-start | bytes 1966088 | tf_op jit(solution)/shard_map/ppermute | solution.py:468
  202.1 19.2 %collective-permute-start.26 = (bf16[128,2560]{1,0:T(8,128)(2,1)S(1)}, bf16[128,2560]{1,0:T(8,128)(2,1)S(1)}, u32[]{:S(2)}, u32[]{:S(2)}) collective-permute-start(bf16[128,2560]{1,0:T(8,128)(2,1)S(1)} %shard_map.150.refs_2_.refs_0_), channel_id=1, source_target_pairs={{0,4},{2,6},{12,8},{14,10},{1,5},{3,7},{13,9},{15,11},{16,20},{18,... | collective-permute-start | bytes 1966088 | tf_op jit(solution)/shard_map/ppermute | solution.py:466
  222.7 15.0 %collective-permute-start.25 = (bf16[128,2560]{1,0:T(8,128)(2,1)S(1)}, bf16[128,2560]{1,0:T(8,128)(2,1)S(1)}, u32[]{:S(2)}, u32[]{:S(2)}) collective-permute-start(bf16[128,2560]{1,0:T(8,128)(2,1)S(1)} %shard_map.153.refs_2_), channel_id=1, source_target_pairs={{0,4},{2,6},{4,0},{6,2},{8,12},{10,14},{12,8},{14,10},{1,5},{3,7},... | collective-permute-start | bytes 1966088 | tf_op jit(solution)/shard_map/ppermute | solution.py:473
  225.4 13.2 %collective-permute-start.22 = (bf16[128,2560]{1,0:T(8,128)(2,1)S(1)}, bf16[128,2560]{1,0:T(8,128)(2,1)S(1)}, u32[]{:S(2)}, u32[]{:S(2)}) collective-permute-start(bf16[128,2560]{1,0:T(8,128)(2,1)S(1)} %get-tuple-element.62.refs_3_), channel_id=1, source_target_pairs={{0,2},{2,0},{4,6},{6,4},{8,10},{10,8},{12,14},{14,12},{1,3},{3,1},... | collective-permute-start | bytes 1966088 | tf_op jit(solution)/shard_map/ppermute | solution.py:471
  (71 other events, 711.8 us)

commit v7 on v5

--- a/solution.py
+++ b/solution.py
@@ -36,7 +36,7 @@
 
 
 def call(
-    kernel, meta, args, grid, in_specs, out_specs, out_shape, scratch=(), vmem=26, after=(), cost=(1000, 1000)
+    kernel, meta, args, grid, in_specs, out_specs, out_shape, scratch=(), vmem=24, after=(), cost=(1000, 1000)
 ):
     first, extra = len(args), len(after)
 

time: 218 us -> 214 us (0.982)
  local copies, waits for them, and re-layouts: 20.2 us -> 15.3 us
  starting transfers between devices: 44.7 us -> 47.2 us
    unnamed x72 -> x58, local copies, waits for them, and re-layouts: 19.4 us -> 14.5 us
  transfers between devices with their start and end apart: 29 -> 29, of which waited for: 6 -> 8; matrix products, arithmetic and copies ran while one was open for 4% -> 4% of each run, Pallas kernels for 52% -> 53%
where the time goes in v7:
time: 214 us
  Pallas kernels  121 us (57%)
  starting transfers between devices  47.2 us (22%)
  waiting for transfers between devices  22.2 us (10%)
  local copies, waits for them, and re-layouts  15.3 us (7%)
  other arithmetic  6.98 us (3%)
    pallas_call x28, Pallas kernels, call(): pl.pallas_call(run, grid_spec=pltpu.PrefetchScalarGridSpec(num_scalar_pre...  121 us
    ppermute x1, waiting for transfers between devices, grid_body(): mid_out = send(tied(mid, low_in), perm=OUTWARD)  16.9 us
    unnamed x58, local copies, waits for them, and re-layouts  14.5 us
    ppermute x1, starting transfers between devices, grid_body(): mid_in = send(sum2, perm=INWARD)  6.03 us
    ppermute x1, starting transfers between devices, grid_body(): other3 = swap_cores(mine3)  4.55 us
  transfers between devices with their start and end apart: 29, of which 8 were waited for; matrix products, arithmetic and copies ran while one was open for 4% of the time, Pallas kernels for 53%

profile of v7, /device:TPU:1, one launch (start us, length us, event | category | flops | bytes accessed | tf_op | source)
XLA Modules:
  0.0 213.6 jit_solution(7963597025200573578)
XLA Ops:
  0.8 2.8 %collective-permute-start.1 = (bf16[64,5120]{1,0:T(8,128)(2,1)}, bf16[64,5120]{1,0:T(8,128)(2,1)S(1)}, u32[]{:S(2)}, u32[]{:S(2)}) collective-permute-start(bf16[64,5120]{1,0:T(8,128)(2,1)} %refs_0_.9), channel_id=1, source_target_pairs={{0,4},{2,6},{4,0},{6,2},{8,12},{10,14},{12,8},{14,10},{1,5},{3,7},... | collective-permute-start | bytes 1966088 | tf_op jit(solution)/shard_map/ppermute | solution.py:407
  13.8 2.9 %shard_map.130 = (bf16[512,3200]{1,0:T(8,128)(2,1)S(1)}, f32[256,128]{1,0:T(8,128)S(1)}) custom-call(s32[19]{0:T(128)S(1)} %concatenate.10.m, bf16[512,3200]{1,0:T(8,128)(2,1)S(1)} %copy-done.2, bf16[512,3200]{1,0:T(8,128)(2,1)S(1)} %copy-done.5, bf16[6,64,3200]{2,1,0:T(8,128)(2,1)S(1)} %bitcast.16), custom_call_target="tpu_custom_call" | custom-call | flops 1000 | bytes 1000 | tf_op jit(solution)/shard_map/pallas_call | solution.py:46
  24.1 16.9 %collective-permute-done.5 = bf16[64,5120]{1,0:T(8,128)(2,1)} collective-permute-done((bf16[64,5120]{1,0:T(8,128)(2,1)S(1)}, bf16[64,5120]{1,0:T(8,128)(2,1)}, u32[]{:S(2)}, u32[]{:S(2)}) %collective-permute-start.5) | collective-permute-done | bytes 655392 | tf_op jit(solution)/shard_map/ppermute | solution.py:413
  43.5 5.7 %copy-done = bf16[2560,3200]{1,0:T(8,128)(2,1)S(1)} copy-done((bf16[2560,3200]{1,0:T(8,128)(2,1)S(1)}, bf16[2560,3200]{1,0:T(8,128)(2,1)}, u32[]{:S(2)}) %copy-start) | copy-done | bytes 16384024
  49.2 7.9 %shard_map.131.refs_10_.refs_0_ = f32[256,1280]{1,0:T(8,128)S(1)} custom-call(s32[19]{0:T(128)S(1)} %concatenate.10.m, bf16[64,5120]{1,0:T(8,128)(2,1)S(1)} %copy-done.11, bf16[64,5120]{1,0:T(8,128)(2,1)S(1)} %collective-permute-done.refs_1_.refs_5_, bf16[64,5120]{1,0:T(8,128)(2,1)S(1)} %collective-permute-done.1.refs_2_.refs_6_, ...), custom_call_target="tpu_custom_call" | custom-call | flops 1000 | bytes 1000 | tf_op jit(solution)/shard_map/pallas_call | solution.py:46
  57.7 7.5 %shard_map.132.refs_10_.refs_1_ = f32[256,1280]{1,0:T(8,128)S(1)} custom-call(s32[19]{0:T(128)S(1)} %concatenate.10.m, bf16[64,5120]{1,0:T(8,128)(2,1)S(1)} %copy-done.11, bf16[64,5120]{1,0:T(8,128)(2,1)S(1)} %collective-permute-done.refs_1_.refs_5_, bf16[64,5120]{1,0:T(8,128)(2,1)S(1)} %collective-permute-done.1.refs_2_.refs_6_, ...), custom_call_target="tpu_custom_call" | custom-call | flops 1000 | bytes 1000 | tf_op jit(solution)/shard_map/pallas_call | solution.py:46
  65.2 5.1 %shard_map.133.refs_10_.refs_2_ = f32[256,640]{1,0:T(8,128)S(1)} custom-call(s32[19]{0:T(128)S(1)} %concatenate.10.m, bf16[64,5120]{1,0:T(8,128)(2,1)S(1)} %copy-done.11, bf16[64,5120]{1,0:T(8,128)(2,1)S(1)} %collective-permute-done.refs_1_.refs_5_, bf16[64,5120]{1,0:T(8,128)(2,1)S(1)} %collective-permute-done.1.refs_2_.refs_6_, ...), custom_call_target="tpu_custom_call" | custom-call | flops 1000 | bytes 1000 | tf_op jit(solution)/shard_map/pallas_call | solution.py:46
  72.5 7.5 %shard_map.135.refs_2_.refs_0_ = f32[256,1280]{1,0:T(8,128)S(1)} custom-call(s32[19]{0:T(128)S(1)} %concatenate.10.m, bf16[64,5120]{1,0:T(8,128)(2,1)S(1)} %broadcast_select_fusion.1.refs_4_.refs_0_, bf16[64,5120]{1,0:T(8,128)(2,1)S(1)} %collective-permute-done.6.refs_5_.refs_1_, bf16[64,5120]{1,0:T(8,128)(2,1)S(1)} %broadcast_select_fusion.refs_6_.refs_2_, ...), custom_call_target="tpu_custom_call" | custom-call | flops 1000 | bytes 1000 | tf_op jit(solution)/shard_map/pallas_call | solution.py:46
  80.6 2.3 %collective-permute-start.11 = (bf16[512,128]{1,0:T(8,128)(2,1)S(1)}, bf16[512,128]{1,0:T(8,128)(2,1)S(1)}, u32[]{:S(2)}, u32[]{:S(2)}) collective-permute-start(bf16[512,128]{1,0:T(8,128)(2,1)S(1)} %get-tuple-element.46.refs_10_), channel_id=1, source_target_pairs={{0,4},{2,6},{4,0},{6,2},{8,12},{10,14},{12,8},{14,10},{1,5},{3,7},... | collective-permute-start | bytes 393224 | tf_op jit(solution)/shard_map/ppermute | solution.py:429
  82.9 7.7 %shard_map.137.refs_2_.refs_1_ = f32[256,1280]{1,0:T(8,128)S(1)} custom-call(s32[19]{0:T(128)S(1)} %concatenate.10.m, bf16[64,5120]{1,0:T(8,128)(2,1)S(1)} %broadcast_select_fusion.1.refs_4_.refs_0_, bf16[64,5120]{1,0:T(8,128)(2,1)S(1)} %collective-permute-done.6.refs_5_.refs_1_, bf16[64,5120]{1,0:T(8,128)(2,1)S(1)} %broadcast_select_fusion.refs_6_.refs_2_, ...), custom_call_target="tpu_custom_call" | custom-call | flops 1000 | bytes 1000 | tf_op jit(solution)/shard_map/pallas_call | solution.py:46
  91.7 5.6 %shard_map.139.refs_2_ = f32[256,640]{1,0:T(8,128)S(1)} custom-call(s32[19]{0:T(128)S(1)} %concatenate.10.m, bf16[64,5120]{1,0:T(8,128)(2,1)S(1)} %broadcast_select_fusion.1.refs_4_.refs_0_, bf16[64,5120]{1,0:T(8,128)(2,1)S(1)} %copy-done.13, bf16[64,5120]{1,0:T(8,128)(2,1)S(1)} %broadcast_select_fusion.refs_6_.refs_2_, ...), custom_call_target="tpu_custom_call" | custom-call | flops 1000 | bytes 1000 | tf_op jit(solution)/shard_map/pallas_call | solution.py:46
  100.7 4.6 %collective-permute-start.13 = (bf16[2,128,3200]{2,1,0:T(8,128)(2,1)S(1)}, bf16[2,128,3200]{2,1,0:T(8,128)(2,1)S(1)}, u32[]{:S(2)}, u32[]{:S(2)}) collective-permute-start(bf16[2,128,3200]{2,1,0:T(8,128)(2,1)S(1)} %shard_map.141.refs_7_.refs_0_), channel_id=1, source_target_pairs={{0,1},{1,0},{2,3},{3,2},{4,5},{5,4},{6,7},{7,6},{8,9},{9,8},{10,11... | collective-permute-start | bytes 4915208 | tf_op jit(solution)/shard_map/ppermute | solution.py:442
  105.2 2.8 %shard_map.142.refs_4_.refs_0_ = bf16[2,128,3200]{2,1,0:T(8,128)(2,1)} custom-call(s32[19]{0:T(128)S(1)} %concatenate.10.m, f32[256,1280]{1,0:T(8,128)S(1)} %shard_map.135.refs_2_.refs_0_, f32[256,1280]{1,0:T(8,128)S(1)} %shard_map.137.refs_2_.refs_1_, f32[256,640]{1,0:T(8,128)S(1)} %shard_map.139.refs_2_, bf16[512,3200]{1,0:T(8,128)(2,1)S(1)} %copy-done.3, ...), custom_call_target="tpu_custom_call" | custom-call | flops 1000 | bytes 1000 | tf_op jit(solution)/shard_map/pallas_call | solution.py:46
  110.2 12.9 %shard_map.143 = (bf16[128,2560]{1,0:T(8,128)(2,1)S(1)}, bf16[128,2560]{1,0:T(8,128)(2,1)S(1)}) custom-call(s32[19]{0:T(128)S(1)} %concatenate.10.m, bf16[2,128,3200]{2,1,0:T(8,128)(2,1)S(1)} %copy-done.19, bf16[2,128,3200]{2,1,0:T(8,128)(2,1)S(1)} %collective-permute-done.13.refs_1_, bf16[2560,3200]{1,0:T(8,128)(2,1)S(1)} %bitcast.15, ...), custom_call_target="tpu_custom_call" | custom-call | flops 1000 | bytes 1000 | tf_op jit(solution)/shard_map/pallas_call | solution.py:46
  127.7 13.4 %shard_map.145 = (bf16[128,2560]{1,0:T(8,128)(2,1)S(1)}, bf16[128,2560]{1,0:T(8,128)(2,1)S(1)}) custom-call(s32[19]{0:T(128)S(1)} %concatenate.10.m, bf16[2,128,3200]{2,1,0:T(8,128)(2,1)} %shard_map.142.refs_4_.refs_0_, bf16[2,128,3200]{2,1,0:T(8,128)(2,1)S(1)} %collective-permute-done.15.refs_1_, bf16[2560,3200]{1,0:T(8,128)(2,1)S(1)} %bitcast.15, ...), custom_call_target="tpu_custom_call" | custom-call | flops 1000 | bytes 1000 | tf_op jit(solution)/shard_map/pallas_call | solution.py:46
  147.7 2.9 %collective-permute-start.18 = (bf16[128,2560]{1,0:T(8,128)(2,1)S(1)}, bf16[128,2560]{1,0:T(8,128)(2,1)S(1)}, u32[]{:S(2)}, u32[]{:S(2)}) collective-permute-start(bf16[128,2560]{1,0:T(8,128)(2,1)S(1)} %shard_map.146.refs_7_.refs_0_), channel_id=1, source_target_pairs={{0,4},{2,6},{12,8},{14,10},{1,5},{3,7},{13,9},{15,11},{16,20},{18,... | collective-permute-start | bytes 1966088 | tf_op jit(solution)/shard_map/ppermute | solution.py:450
  150.6 12.6 %shard_map.148 = (bf16[128,2560]{1,0:T(8,128)(2,1)S(1)}, bf16[128,2560]{1,0:T(8,128)(2,1)S(1)}) custom-call(s32[19]{0:T(128)S(1)} %concatenate.10.m, bf16[2,128,3200]{2,1,0:T(8,128)(2,1)S(1)} %shard_map.144.refs_4_.refs_0_, bf16[2,128,3200]{2,1,0:T(8,128)(2,1)S(1)} %collective-permute-done.16.refs_1_, bf16[2560,3200]{1,0:T(8,128)(2,1)S(1)} %bitcast.15, ...), custom_call_target="tpu_custom_call" | custom-call | flops 1000 | bytes 1000 | tf_op jit(solution)/shard_map/pallas_call | solution.py:46
  166.2 6.0 %collective-permute-start.24 = (bf16[128,2560]{1,0:T(8,128)(2,1)S(1)}, bf16[128,2560]{1,0:T(8,128)(2,1)S(1)}, u32[]{:S(2)}, u32[]{:S(2)}) collective-permute-start(bf16[128,2560]{1,0:T(8,128)(2,1)S(1)} %shard_map.149.refs_2_.refs_0_), channel_id=1, source_target_pairs={{0,4},{2,6},{12,8},{14,10},{1,5},{3,7},{13,9},{15,11},{16,20},{18,... | collective-permute-start | bytes 1966088 | tf_op jit(solution)/shard_map/ppermute | solution.py:455
  172.2 12.8 %shard_map.151 = (bf16[128,2560]{1,0:T(8,128)(2,1)S(1)}, bf16[128,2560]{1,0:T(8,128)(2,1)S(1)}) custom-call(s32[19]{0:T(128)S(1)} %concatenate.10.m, bf16[2,128,3200]{2,1,0:T(8,128)(2,1)S(1)} %shard_map.147.refs_4_.refs_0_, bf16[2,128,3200]{2,1,0:T(8,128)(2,1)S(1)} %collective-permute-done.17.refs_1_, bf16[2560,3200]{1,0:T(8,128)(2,1)S(1)} %bitcast.15, ...), custom_call_target="tpu_custom_call" | custom-call | flops 1000 | bytes 1000 | tf_op jit(solution)/shard_map/pallas_call | solution.py:46
  187.3 2.7 %collective-permute-start.23 = (bf16[128,2560]{1,0:T(8,128)(2,1)S(1)}, bf16[128,2560]{1,0:T(8,128)(2,1)S(1)}, u32[]{:S(2)}, u32[]{:S(2)}) collective-permute-start(bf16[128,2560]{1,0:T(8,128)(2,1)S(1)} %shard_map.152.refs_2_), channel_id=1, source_target_pairs={{0,4},{2,6},{4,0},{6,2},{8,12},{10,14},{12,8},{14,10},{1,5},{3,7},... | collective-permute-start | bytes 1966088 | tf_op jit(solution)/shard_map/ppermute | solution.py:460
  191.2 4.6 %shard_map.154 = (bf16[3,64,3200]{2,1,0:T(8,128)(2,1)S(1)}, bf16[3,64,3200]{2,1,0:T(8,128)(2,1)}) custom-call(s32[19]{0:T(128)S(1)} %concatenate.10.m, bf16[512,128]{1,0:T(8,128)(2,1)S(1)} %get-tuple-element.49.refs_5_.refs_0_, bf16[512,3200]{1,0:T(8,128)(2,1)S(1)} %copy-done.21, bf16[128,2560]{1,0:T(8,128)(2,1)S(1)} %shard_map.153.refs_2_), custom_call_target="tpu_custom_call" | custom-call | flops 1000 | bytes 1000 | tf_op jit(solution)/shard_map/pallas_call | solution.py:46
  195.8 3.5 %collective-permute-start.27 = (bf16[3,64,3200]{2,1,0:T(8,128)(2,1)}, bf16[3,64,3200]{2,1,0:T(8,128)(2,1)S(1)}, u32[]{:S(2)}, u32[]{:S(2)}) collective-permute-start(bf16[3,64,3200]{2,1,0:T(8,128)(2,1)} %get-tuple-element.67), channel_id=1, source_target_pairs={{0,1},{1,0},{2,3},{3,2},{4,5},{5,4},{6,7},{7,6},{8,9},{9,8},{10,11... | collective-permute-start | bytes 3686408 | tf_op jit(solution)/shard_map/ppermute | solution.py:471
  203.8 4.2 %collective-permute-start.26 = (bf16[64,2560]{1,0:T(8,128)(2,1)S(1)}, bf16[64,2560]{1,0:T(8,128)(2,1)}, u32[]{:S(2)}, u32[]{:S(2)}) collective-permute-start(bf16[64,2560]{1,0:T(8,128)(2,1)S(1)} %get-tuple-element.66.refs_2_), channel_id=1, source_target_pairs={{0,1},{1,0},{2,3},{3,2},{4,5},{5,4},{6,7},{7,6},{8,9},{9,8},{10,11... | collective-permute-start | bytes 983048 | tf_op jit(solution)/shard_map/ppermute | solution.py:473
  209.8 2.1 maximum_select_fusion
  (131 shorter events, 55.6 us)
Async XLA Ops:
  0.6 42.9 %collective-permute-start.3 = (bf16[2560,3200]{1,0:T(8,128)(2,1)}, bf16[2560,3200]{1,0:T(8,128)(2,1)}, u32[]{:S(2)}, u32[]{:S(2)}) collective-permute-start(bf16[2560,3200]{1,0:T(8,128)(2,1)} %refs_8_.13), channel_id=1, source_target_pairs={{0,1},{1,0},{2,3},{3,2},{4,5},{5,4},{6,7},{7,6},{8,9},{9,8},{10,11... | collective-permute-start | bytes 49152008 | tf_op jit(solution)/shard_map/ppermute | solution.py:406
  0.8 18.0 %collective-permute-start.1 = (bf16[64,5120]{1,0:T(8,128)(2,1)}, bf16[64,5120]{1,0:T(8,128)(2,1)S(1)}, u32[]{:S(2)}, u32[]{:S(2)}) collective-permute-start(bf16[64,5120]{1,0:T(8,128)(2,1)} %refs_0_.9), channel_id=1, source_target_pairs={{0,4},{2,6},{4,0},{6,2},{8,12},{10,14},{12,8},{14,10},{1,5},{3,7},... | collective-permute-start | bytes 1966088 | tf_op jit(solution)/shard_map/ppermute | solution.py:407
  3.5 15.2 %collective-permute-start.4 = (bf16[64,5120]{1,0:T(8,128)(2,1)}, bf16[64,5120]{1,0:T(8,128)(2,1)S(1)}, u32[]{:S(2)}, u32[]{:S(2)}) collective-permute-start(bf16[64,5120]{1,0:T(8,128)(2,1)} %refs_0_.9), channel_id=1, source_target_pairs={{4,8},{6,10},{8,4},{10,6},{5,9},{7,11},{9,5},{11,7},{20,24},{22,26... | collective-permute-start | bytes 1966088 | tf_op jit(solution)/shard_map/ppermute | solution.py:408
  4.2 17.3 %collective-permute-start = (bf16[64,5120]{1,0:T(8,128)(2,1)}, bf16[64,5120]{1,0:T(8,128)(2,1)S(1)}, u32[]{:S(2)}, u32[]{:S(2)}) collective-permute-start(bf16[64,5120]{1,0:T(8,128)(2,1)} %refs_0_.9), channel_id=1, source_target_pairs={{0,2},{2,0},{4,6},{6,4},{8,10},{10,8},{12,14},{14,12},{1,3},{3,1},... | collective-permute-start | bytes 1966088 | tf_op jit(solution)/shard_map/ppermute | solution.py:409
  20.2 20.8 %collective-permute-start.5 = (bf16[64,5120]{1,0:T(8,128)(2,1)S(1)}, bf16[64,5120]{1,0:T(8,128)(2,1)}, u32[]{:S(2)}, u32[]{:S(2)}) collective-permute-start(bf16[64,5120]{1,0:T(8,128)(2,1)S(1)} %collective-permute-done.4), channel_id=1, source_target_pairs={{4,0},{6,2},{8,12},{10,14},{5,1},{7,3},{9,13},{11,15},{20,16},{22,... | collective-permute-start | bytes 1966088 | tf_op jit(solution)/shard_map/ppermute | solution.py:413
  21.6 20.7 %collective-permute-start.2 = (bf16[64,5120]{1,0:T(8,128)(2,1)S(1)}, bf16[64,5120]{1,0:T(8,128)(2,1)S(1)}, u32[]{:S(2)}, u32[]{:S(2)}) collective-permute-start(bf16[64,5120]{1,0:T(8,128)(2,1)S(1)} %collective-permute-done.1.refs_2_.refs_6_), channel_id=1, source_target_pairs={{0,2},{2,0},{4,6},{6,4},{8,10},{10,8},{12,14},{14,12},{1,3},{3,1},... | collective-permute-start | bytes 1966088 | tf_op jit(solution)/shard_map/ppermute | solution.py:411
  22.8 34.2 %collective-permute-start.8 = (bf16[64,5120]{1,0:T(8,128)(2,1)}, bf16[64,5120]{1,0:T(8,128)(2,1)S(1)}, u32[]{:S(2)}, u32[]{:S(2)}) collective-permute-start(bf16[64,5120]{1,0:T(8,128)(2,1)} %collective-permute-done.7), channel_id=1, source_target_pairs={{4,0},{6,2},{8,12},{10,14},{5,1},{7,3},{9,13},{11,15},{20,16},{22,... | collective-permute-start | bytes 1966088 | tf_op jit(solution)/shard_map/ppermute | solution.py:416
  42.2 15.0 %collective-permute-start.6 = (bf16[64,5120]{1,0:T(8,128)(2,1)S(1)}, bf16[64,5120]{1,0:T(8,128)(2,1)S(1)}, u32[]{:S(2)}, u32[]{:S(2)}) collective-permute-start(bf16[64,5120]{1,0:T(8,128)(2,1)S(1)} %broadcast_select_fusion.1.refs_4_.refs_0_), channel_id=1, source_target_pairs={{0,2},{2,0},{4,6},{6,4},{8,10},{10,8},{12,14},{14,12},{1,3},{3,1},... | collective-permute-start | bytes 1966088 | tf_op jit(solution)/shard_map/ppermute | solution.py:415
  57.2 13.9 %collective-permute-start.9 = (bf16[64,5120]{1,0:T(8,128)(2,1)S(1)}, bf16[64,5120]{1,0:T(8,128)(2,1)S(1)}, u32[]{:S(2)}, u32[]{:S(2)}) collective-permute-start(bf16[64,5120]{1,0:T(8,128)(2,1)S(1)} %broadcast_select_fusion.refs_6_.refs_2_), channel_id=1, source_target_pairs={{0,2},{2,0},{4,6},{6,4},{8,10},{10,8},{12,14},{14,12},{1,3},{3,1},... | collective-permute-start | bytes 1966088 | tf_op jit(solution)/shard_map/ppermute | solution.py:422
  72.1 7.9 %collective-permute-start.10 = (bf16[512,128]{1,0:T(8,128)(2,1)S(1)}, bf16[512,128]{1,0:T(8,128)(2,1)S(1)}, u32[]{:S(2)}, u32[]{:S(2)}) collective-permute-start(bf16[512,128]{1,0:T(8,128)(2,1)S(1)} %get-tuple-element.44.refs_10_), channel_id=1, source_target_pairs={{0,2},{2,0},{4,6},{6,4},{8,10},{10,8},{12,14},{14,12},{1,3},{3,1},... | collective-permute-start | bytes 393224 | tf_op jit(solution)/shard_map/ppermute | solution.py:429
  80.6 10.0 %collective-permute-start.11 = (bf16[512,128]{1,0:T(8,128)(2,1)S(1)}, bf16[512,128]{1,0:T(8,128)(2,1)S(1)}, u32[]{:S(2)}, u32[]{:S(2)}) collective-permute-start(bf16[512,128]{1,0:T(8,128)(2,1)S(1)} %get-tuple-element.46.refs_10_), channel_id=1, source_target_pairs={{0,4},{2,6},{4,0},{6,2},{8,12},{10,14},{12,8},{14,10},{1,5},{3,7},... | collective-permute-start | bytes 393224 | tf_op jit(solution)/shard_map/ppermute | solution.py:429
  108.3 16.9 %collective-permute-start.15 = (bf16[2,128,3200]{2,1,0:T(8,128)(2,1)}, bf16[2,128,3200]{2,1,0:T(8,128)(2,1)S(1)}, u32[]{:S(2)}, u32[]{:S(2)}) collective-permute-start(bf16[2,128,3200]{2,1,0:T(8,128)(2,1)} %shard_map.142.refs_4_.refs_0_), channel_id=1, source_target_pairs={{0,1},{1,0},{2,3},{3,2},{4,5},{5,4},{6,7},{7,6},{8,9},{9,8},{10,11... | collective-permute-start | bytes 4915208 | tf_op jit(solution)/shard_map/ppermute | solution.py:444
  125.2 20.3 %collective-permute-start.16 = (bf16[2,128,3200]{2,1,0:T(8,128)(2,1)S(1)}, bf16[2,128,3200]{2,1,0:T(8,128)(2,1)S(1)}, u32[]{:S(2)}, u32[]{:S(2)}) collective-permute-start(bf16[2,128,3200]{2,1,0:T(8,128)(2,1)S(1)} %shard_map.144.refs_4_.refs_0_), channel_id=1, source_target_pairs={{0,1},{1,0},{2,3},{3,2},{4,5},{5,4},{6,7},{7,6},{8,9},{9,8},{10,11... | collective-permute-start | bytes 4915208 | tf_op jit(solution)/shard_map/ppermute | solution.py:448
  126.5 16.3 %collective-permute-start.14 = (bf16[128,2560]{1,0:T(8,128)(2,1)S(1)}, bf16[128,2560]{1,0:T(8,128)(2,1)S(1)}, u32[]{:S(2)}, u32[]{:S(2)}) collective-permute-start(bf16[128,2560]{1,0:T(8,128)(2,1)S(1)} %get-tuple-element.51.refs_7_), channel_id=1, source_target_pairs={{0,2},{2,0},{4,6},{6,4},{8,10},{10,8},{12,14},{14,12},{1,3},{3,1},... | collective-permute-start | bytes 1966088 | tf_op jit(solution)/shard_map/ppermute | solution.py:439
  145.5 26.7 %collective-permute-start.17 = (bf16[2,128,3200]{2,1,0:T(8,128)(2,1)S(1)}, bf16[2,128,3200]{2,1,0:T(8,128)(2,1)S(1)}, u32[]{:S(2)}, u32[]{:S(2)}) collective-permute-start(bf16[2,128,3200]{2,1,0:T(8,128)(2,1)S(1)} %shard_map.147.refs_4_.refs_0_), channel_id=1, source_target_pairs={{0,1},{1,0},{2,3},{3,2},{4,5},{5,4},{6,7},{7,6},{8,9},{9,8},{10,11... | collective-permute-start | bytes 4915208 | tf_op jit(solution)/shard_map/ppermute | solution.py:453
  146.4 16.8 %collective-permute-start.19 = (bf16[128,2560]{1,0:T(8,128)(2,1)S(1)}, bf16[128,2560]{1,0:T(8,128)(2,1)S(1)}, u32[]{:S(2)}, u32[]{:S(2)}) collective-permute-start(bf16[128,2560]{1,0:T(8,128)(2,1)S(1)} %get-tuple-element.53.refs_2_), channel_id=1, source_target_pairs={{0,2},{2,0},{4,6},{6,4},{8,10},{10,8},{12,14},{14,12},{1,3},{3,1},... | collective-permute-start | bytes 1966088 | tf_op jit(solution)/shard_map/ppermute | solution.py:439
  147.7 16.6 %collective-permute-start.18 = (bf16[128,2560]{1,0:T(8,128)(2,1)S(1)}, bf16[128,2560]{1,0:T(8,128)(2,1)S(1)}, u32[]{:S(2)}, u32[]{:S(2)}) collective-permute-start(bf16[128,2560]{1,0:T(8,128)(2,1)S(1)} %shard_map.146.refs_7_.refs_0_), channel_id=1, source_target_pairs={{0,4},{2,6},{12,8},{14,10},{1,5},{3,7},{13,9},{15,11},{16,20},{18,... | collective-permute-start | bytes 1966088 | tf_op jit(solution)/shard_map/ppermute | solution.py:450
  165.0 20.0 %collective-permute-start.22 = (bf16[128,2560]{1,0:T(8,128)(2,1)S(1)}, bf16[128,2560]{1,0:T(8,128)(2,1)S(1)}, u32[]{:S(2)}, u32[]{:S(2)}) collective-permute-start(bf16[128,2560]{1,0:T(8,128)(2,1)S(1)} %shard_map.150.refs_4_), channel_id=1, source_target_pairs={{4,8},{6,10},{8,4},{10,6},{5,9},{7,11},{9,5},{11,7},{20,24},{22,26... | collective-permute-start | bytes 1966088 | tf_op jit(solution)/shard_map/ppermute | solution.py:457
  165.7 19.3 %collective-permute-start.21 = (bf16[128,2560]{1,0:T(8,128)(2,1)S(1)}, bf16[128,2560]{1,0:T(8,128)(2,1)S(1)}, u32[]{:S(2)}, u32[]{:S(2)}) collective-permute-start(bf16[128,2560]{1,0:T(8,128)(2,1)S(1)} %get-tuple-element.57.refs_2_), channel_id=1, source_target_pairs={{0,2},{2,0},{4,6},{6,4},{8,10},{10,8},{12,14},{14,12},{1,3},{3,1},... | collective-permute-start | bytes 1966088 | tf_op jit(solution)/shard_map/ppermute | solution.py:439
  166.2 19.7 %collective-permute-start.24 = (bf16[128,2560]{1,0:T(8,128)(2,1)S(1)}, bf16[128,2560]{1,0:T(8,128)(2,1)S(1)}, u32[]{:S(2)}, u32[]{:S(2)}) collective-permute-start(bf16[128,2560]{1,0:T(8,128)(2,1)S(1)} %shard_map.149.refs_2_.refs_0_), channel_id=1, source_target_pairs={{0,4},{2,6},{12,8},{14,10},{1,5},{3,7},{13,9},{15,11},{16,20},{18,... | collective-permute-start | bytes 1966088 | tf_op jit(solution)/shard_map/ppermute | solution.py:455
  186.6 14.7 %collective-permute-start.25 = (bf16[128,2560]{1,0:T(8,128)(2,1)S(1)}, bf16[128,2560]{1,0:T(8,128)(2,1)S(1)}, u32[]{:S(2)}, u32[]{:S(2)}) collective-permute-start(bf16[128,2560]{1,0:T(8,128)(2,1)S(1)} %shard_map.153.refs_2_), channel_id=1, source_target_pairs={{4,8},{6,10},{8,4},{10,6},{5,9},{7,11},{9,5},{11,7},{20,24},{22,26... | collective-permute-start | bytes 1966088 | tf_op jit(solution)/shard_map/ppermute | solution.py:462
  187.3 14.8 %collective-permute-start.23 = (bf16[128,2560]{1,0:T(8,128)(2,1)S(1)}, bf16[128,2560]{1,0:T(8,128)(2,1)S(1)}, u32[]{:S(2)}, u32[]{:S(2)}) collective-permute-start(bf16[128,2560]{1,0:T(8,128)(2,1)S(1)} %shard_map.152.refs_2_), channel_id=1, source_target_pairs={{0,4},{2,6},{4,0},{6,2},{8,12},{10,14},{12,8},{14,10},{1,5},{3,7},... | collective-permute-start | bytes 1966088 | tf_op jit(solution)/shard_map/ppermute | solution.py:460
  190.0 13.0 %collective-permute-start.20 = (bf16[128,2560]{1,0:T(8,128)(2,1)S(1)}, bf16[128,2560]{1,0:T(8,128)(2,1)S(1)}, u32[]{:S(2)}, u32[]{:S(2)}) collective-permute-start(bf16[128,2560]{1,0:T(8,128)(2,1)S(1)} %get-tuple-element.59.refs_3_), channel_id=1, source_target_pairs={{0,2},{2,0},{4,6},{6,4},{8,10},{10,8},{12,14},{14,12},{1,3},{3,1},... | collective-permute-start | bytes 1966088 | tf_op jit(solution)/shard_map/ppermute | solution.py:439
  195.8 16.1 %collective-permute-start.27 = (bf16[3,64,3200]{2,1,0:T(8,128)(2,1)}, bf16[3,64,3200]{2,1,0:T(8,128)(2,1)S(1)}, u32[]{:S(2)}, u32[]{:S(2)}) collective-permute-start(bf16[3,64,3200]{2,1,0:T(8,128)(2,1)} %get-tuple-element.67), channel_id=1, source_target_pairs={{0,1},{1,0},{2,3},{3,2},{4,5},{5,4},{6,7},{7,6},{8,9},{9,8},{10,11... | collective-permute-start | bytes 3686408 | tf_op jit(solution)/shard_map/ppermute | solution.py:471
  (34 other events, 282.9 us)

commit v8 on v7

--- a/solution.py
+++ b/solution.py
@@ -97,6 +97,7 @@
             jax.ShapeDtypeStruct((rows, width), BF16),
             jax.ShapeDtypeStruct((rows // 2, 2 * rank), F32),
         ],
+        vmem=56,
     )
 
 

time: 214 us -> 214 us (level)
  local copies, waits for them, and re-layouts: 15.3 us -> 8.7 us
  Pallas kernels: 121 us -> 124 us
  waiting for transfers between devices: 22.2 us -> 25.1 us
    unnamed x58 -> x54, local copies, waits for them, and re-layouts: 14.5 us -> 7.3 us
    pallas_call x28, Pallas kernels: 121 us -> 124 us  [call(): pl.pallas_call(run, grid_spec=pltpu.PrefetchScalarGridSpec(num_scalar_pre...]
    ppermute x1, waiting for transfers between devices: 0.32 us -> 3.31 us  [grid_body(): pair = send(cotangent, perm=PAIR)]
  transfers between devices with their start and end apart: 29 -> 29, of which waited for: 8 -> 8; matrix products, arithmetic and copies ran while one was open for 4% -> 4% of each run, Pallas kernels for 53% -> 55%
where the time goes in v8:
time: 214 us
  Pallas kernels  124 us (58%)
  starting transfers between devices  47.2 us (22%)
  waiting for transfers between devices  25.1 us (12%)
  local copies, waits for them, and re-layouts  8.7 us (4%)
  other arithmetic  6.98 us (3%)
    pallas_call x28, Pallas kernels, call(): pl.pallas_call(run, grid_spec=pltpu.PrefetchScalarGridSpec(num_scalar_pre...  124 us
    ppermute x1, waiting for transfers between devices, grid_body(): mid_out = send(tied(mid, low_in), perm=OUTWARD)  16.9 us
    unnamed x54, local copies, waits for them, and re-layouts  7.3 us
    ppermute x1, starting transfers between devices, grid_body(): mid_in = send(sum2, perm=INWARD)  5.95 us
    ppermute x1, starting transfers between devices, grid_body(): other3 = swap_cores(mine3)  4.52 us
    ppermute x4, starting transfers between devices, parts(): return (keep, send(give, perm=Y_SWAP), give)  4.33 us
  transfers between devices with their start and end apart: 29, of which 8 were waited for; matrix products, arithmetic and copies ran while one was open for 4% of the time, Pallas kernels for 55%

profile of v8, /device:TPU:1, one launch (start us, length us, event | category | flops | bytes accessed | tf_op | source)
XLA Modules:
  0.0 213.6 jit_solution(7957759912231649468)
XLA Ops:
  0.8 2.8 %collective-permute-start.1 = (bf16[64,5120]{1,0:T(8,128)(2,1)}, bf16[64,5120]{1,0:T(8,128)(2,1)S(1)}, u32[]{:S(2)}, u32[]{:S(2)}) collective-permute-start(bf16[64,5120]{1,0:T(8,128)(2,1)} %refs_0_.9), channel_id=1, source_target_pairs={{0,4},{2,6},{4,0},{6,2},{8,12},{10,14},{12,8},{14,10},{1,5},{3,7},... | collective-permute-start | bytes 1966088 | tf_op jit(solution)/shard_map/ppermute | solution.py:408
  8.9 6.5 %shard_map.130 = (bf16[512,3200]{1,0:T(8,128)(2,1)}, f32[256,128]{1,0:T(8,128)}) custom-call(s32[19]{0:T(128)} %concatenate.10.m, bf16[512,3200]{1,0:T(8,128)(2,1)} %refs_3_.13, bf16[512,3200]{1,0:T(8,128)(2,1)} %refs_4_.13, bf16[6,64,3200]{2,1,0:T(8,128)(2,1)} %bitcast.16), custom_call_target="tpu_custom_call" | custom-call | flops 1000 | bytes 1000 | tf_op jit(solution)/shard_map/pallas_call | solution.py:46
  15.4 3.3 %collective-permute-done.1.refs_2_.refs_6_ = bf16[64,5120]{1,0:T(8,128)(2,1)S(1)} collective-permute-done((bf16[64,5120]{1,0:T(8,128)(2,1)}, bf16[64,5120]{1,0:T(8,128)(2,1)S(1)}, u32[]{:S(2)}, u32[]{:S(2)}) %collective-permute-start.1) | collective-permute-done | bytes 655392 | tf_op jit(solution)/shard_map/ppermute | solution.py:408
  24.1 16.9 %collective-permute-done.5 = bf16[64,5120]{1,0:T(8,128)(2,1)} collective-permute-done((bf16[64,5120]{1,0:T(8,128)(2,1)S(1)}, bf16[64,5120]{1,0:T(8,128)(2,1)}, u32[]{:S(2)}, u32[]{:S(2)}) %collective-permute-start.5) | collective-permute-done | bytes 655392 | tf_op jit(solution)/shard_map/ppermute | solution.py:414
  43.6 5.6 %copy-done = bf16[2560,3200]{1,0:T(8,128)(2,1)S(1)} copy-done((bf16[2560,3200]{1,0:T(8,128)(2,1)S(1)}, bf16[2560,3200]{1,0:T(8,128)(2,1)}, u32[]{:S(2)}) %copy-start) | copy-done | bytes 16384024
  49.2 7.9 %shard_map.131.refs_10_.refs_0_ = f32[256,1280]{1,0:T(8,128)S(1)} custom-call(s32[19]{0:T(128)S(1)} %copy-done.22, bf16[64,5120]{1,0:T(8,128)(2,1)S(1)} %copy-done.8, bf16[64,5120]{1,0:T(8,128)(2,1)S(1)} %collective-permute-done.refs_1_.refs_5_, bf16[64,5120]{1,0:T(8,128)(2,1)S(1)} %collective-permute-done.1.refs_2_.refs_6_, ...), custom_call_target="tpu_custom_call" | custom-call | flops 1000 | bytes 1000 | tf_op jit(solution)/shard_map/pallas_call | solution.py:46
  57.7 7.5 %shard_map.132.refs_10_.refs_1_ = f32[256,1280]{1,0:T(8,128)S(1)} custom-call(s32[19]{0:T(128)S(1)} %copy-done.22, bf16[64,5120]{1,0:T(8,128)(2,1)S(1)} %copy-done.8, bf16[64,5120]{1,0:T(8,128)(2,1)S(1)} %collective-permute-done.refs_1_.refs_5_, bf16[64,5120]{1,0:T(8,128)(2,1)S(1)} %collective-permute-done.1.refs_2_.refs_6_, ...), custom_call_target="tpu_custom_call" | custom-call | flops 1000 | bytes 1000 | tf_op jit(solution)/shard_map/pallas_call | solution.py:46
  65.2 5.1 %shard_map.133.refs_10_.refs_2_ = f32[256,640]{1,0:T(8,128)S(1)} custom-call(s32[19]{0:T(128)S(1)} %copy-done.22, bf16[64,5120]{1,0:T(8,128)(2,1)S(1)} %copy-done.8, bf16[64,5120]{1,0:T(8,128)(2,1)S(1)} %collective-permute-done.refs_1_.refs_5_, bf16[64,5120]{1,0:T(8,128)(2,1)S(1)} %collective-permute-done.1.refs_2_.refs_6_, ...), custom_call_target="tpu_custom_call" | custom-call | flops 1000 | bytes 1000 | tf_op jit(solution)/shard_map/pallas_call | solution.py:46
  72.5 7.5 %shard_map.135.refs_2_.refs_0_ = f32[256,1280]{1,0:T(8,128)S(1)} custom-call(s32[19]{0:T(128)S(1)} %copy-done.22, bf16[64,5120]{1,0:T(8,128)(2,1)S(1)} %broadcast_select_fusion.1.refs_4_.refs_0_, bf16[64,5120]{1,0:T(8,128)(2,1)S(1)} %collective-permute-done.6.refs_5_.refs_1_, bf16[64,5120]{1,0:T(8,128)(2,1)S(1)} %broadcast_select_fusion.refs_6_.refs_2_, ...), custom_call_target="tpu_custom_call" | custom-call | flops 1000 | bytes 1000 | tf_op jit(solution)/shard_map/pallas_call | solution.py:46
  80.7 2.3 %collective-permute-start.11 = (bf16[512,128]{1,0:T(8,128)(2,1)S(1)}, bf16[512,128]{1,0:T(8,128)(2,1)S(1)}, u32[]{:S(2)}, u32[]{:S(2)}) collective-permute-start(bf16[512,128]{1,0:T(8,128)(2,1)S(1)} %get-tuple-element.46.refs_10_), channel_id=1, source_target_pairs={{0,4},{2,6},{4,0},{6,2},{8,12},{10,14},{12,8},{14,10},{1,5},{3,7},... | collective-permute-start | bytes 393224 | tf_op jit(solution)/shard_map/ppermute | solution.py:430
  83.0 7.7 %shard_map.137.refs_2_.refs_1_ = f32[256,1280]{1,0:T(8,128)S(1)} custom-call(s32[19]{0:T(128)S(1)} %copy-done.22, bf16[64,5120]{1,0:T(8,128)(2,1)S(1)} %broadcast_select_fusion.1.refs_4_.refs_0_, bf16[64,5120]{1,0:T(8,128)(2,1)S(1)} %collective-permute-done.6.refs_5_.refs_1_, bf16[64,5120]{1,0:T(8,128)(2,1)S(1)} %broadcast_select_fusion.refs_6_.refs_2_, ...), custom_call_target="tpu_custom_call" | custom-call | flops 1000 | bytes 1000 | tf_op jit(solution)/shard_map/pallas_call | solution.py:46
  91.8 5.6 %shard_map.139.refs_2_ = f32[256,640]{1,0:T(8,128)S(1)} custom-call(s32[19]{0:T(128)S(1)} %copy-done.22, bf16[64,5120]{1,0:T(8,128)(2,1)S(1)} %broadcast_select_fusion.1.refs_4_.refs_0_, bf16[64,5120]{1,0:T(8,128)(2,1)S(1)} %copy-done.10, bf16[64,5120]{1,0:T(8,128)(2,1)S(1)} %broadcast_select_fusion.refs_6_.refs_2_, ...), custom_call_target="tpu_custom_call" | custom-call | flops 1000 | bytes 1000 | tf_op jit(solution)/shard_map/pallas_call | solution.py:46
  100.7 4.5 %collective-permute-start.13 = (bf16[2,128,3200]{2,1,0:T(8,128)(2,1)S(1)}, bf16[2,128,3200]{2,1,0:T(8,128)(2,1)S(1)}, u32[]{:S(2)}, u32[]{:S(2)}) collective-permute-start(bf16[2,128,3200]{2,1,0:T(8,128)(2,1)S(1)} %shard_map.141.refs_7_.refs_0_), channel_id=1, source_target_pairs={{0,1},{1,0},{2,3},{3,2},{4,5},{5,4},{6,7},{7,6},{8,9},{9,8},{10,11... | collective-permute-start | bytes 4915208 | tf_op jit(solution)/shard_map/ppermute | solution.py:443
  105.2 2.8 %shard_map.142.refs_4_.refs_0_ = bf16[2,128,3200]{2,1,0:T(8,128)(2,1)} custom-call(s32[19]{0:T(128)S(1)} %copy-done.22, f32[256,1280]{1,0:T(8,128)S(1)} %shard_map.135.refs_2_.refs_0_, f32[256,1280]{1,0:T(8,128)S(1)} %shard_map.137.refs_2_.refs_1_, f32[256,640]{1,0:T(8,128)S(1)} %shard_map.139.refs_2_, bf16[512,3200]{1,0:T(8,128)(2,1)S(1)} %copy-done.2, ...), custom_call_target="tpu_custom_call" | custom-call | flops 1000 | bytes 1000 | tf_op jit(solution)/shard_map/pallas_call | solution.py:46
  110.3 12.9 %shard_map.143 = (bf16[128,2560]{1,0:T(8,128)(2,1)S(1)}, bf16[128,2560]{1,0:T(8,128)(2,1)S(1)}) custom-call(s32[19]{0:T(128)S(1)} %copy-done.22, bf16[2,128,3200]{2,1,0:T(8,128)(2,1)S(1)} %copy-done.16, bf16[2,128,3200]{2,1,0:T(8,128)(2,1)S(1)} %collective-permute-done.13.refs_1_, bf16[2560,3200]{1,0:T(8,128)(2,1)S(1)} %bitcast.15, ...), custom_call_target="tpu_custom_call" | custom-call | flops 1000 | bytes 1000 | tf_op jit(solution)/shard_map/pallas_call | solution.py:46
  127.8 13.4 %shard_map.145 = (bf16[128,2560]{1,0:T(8,128)(2,1)S(1)}, bf16[128,2560]{1,0:T(8,128)(2,1)S(1)}) custom-call(s32[19]{0:T(128)S(1)} %copy-done.22, bf16[2,128,3200]{2,1,0:T(8,128)(2,1)} %shard_map.142.refs_4_.refs_0_, bf16[2,128,3200]{2,1,0:T(8,128)(2,1)S(1)} %collective-permute-done.15.refs_1_, bf16[2560,3200]{1,0:T(8,128)(2,1)S(1)} %bitcast.15, ...), custom_call_target="tpu_custom_call" | custom-call | flops 1000 | bytes 1000 | tf_op jit(solution)/shard_map/pallas_call | solution.py:46
  147.8 2.9 %collective-permute-start.18 = (bf16[128,2560]{1,0:T(8,128)(2,1)S(1)}, bf16[128,2560]{1,0:T(8,128)(2,1)S(1)}, u32[]{:S(2)}, u32[]{:S(2)}) collective-permute-start(bf16[128,2560]{1,0:T(8,128)(2,1)S(1)} %shard_map.146.refs_7_.refs_0_), channel_id=1, source_target_pairs={{0,4},{2,6},{12,8},{14,10},{1,5},{3,7},{13,9},{15,11},{16,20},{18,... | collective-permute-start | bytes 1966088 | tf_op jit(solution)/shard_map/ppermute | solution.py:451
  150.6 12.6 %shard_map.148 = (bf16[128,2560]{1,0:T(8,128)(2,1)S(1)}, bf16[128,2560]{1,0:T(8,128)(2,1)S(1)}) custom-call(s32[19]{0:T(128)S(1)} %copy-done.22, bf16[2,128,3200]{2,1,0:T(8,128)(2,1)S(1)} %shard_map.144.refs_4_.refs_0_, bf16[2,128,3200]{2,1,0:T(8,128)(2,1)S(1)} %collective-permute-done.16.refs_1_, bf16[2560,3200]{1,0:T(8,128)(2,1)S(1)} %bitcast.15, ...), custom_call_target="tpu_custom_call" | custom-call | flops 1000 | bytes 1000 | tf_op jit(solution)/shard_map/pallas_call | solution.py:46
  166.2 6.0 %collective-permute-start.24 = (bf16[128,2560]{1,0:T(8,128)(2,1)S(1)}, bf16[128,2560]{1,0:T(8,128)(2,1)S(1)}, u32[]{:S(2)}, u32[]{:S(2)}) collective-permute-start(bf16[128,2560]{1,0:T(8,128)(2,1)S(1)} %shard_map.149.refs_2_.refs_0_), channel_id=1, source_target_pairs={{0,4},{2,6},{12,8},{14,10},{1,5},{3,7},{13,9},{15,11},{16,20},{18,... | collective-permute-start | bytes 1966088 | tf_op jit(solution)/shard_map/ppermute | solution.py:456
  172.2 12.8 %shard_map.151 = (bf16[128,2560]{1,0:T(8,128)(2,1)S(1)}, bf16[128,2560]{1,0:T(8,128)(2,1)S(1)}) custom-call(s32[19]{0:T(128)S(1)} %copy-done.22, bf16[2,128,3200]{2,1,0:T(8,128)(2,1)S(1)} %shard_map.147.refs_4_.refs_0_, bf16[2,128,3200]{2,1,0:T(8,128)(2,1)S(1)} %collective-permute-done.17.refs_1_, bf16[2560,3200]{1,0:T(8,128)(2,1)S(1)} %bitcast.15, ...), custom_call_target="tpu_custom_call" | custom-call | flops 1000 | bytes 1000 | tf_op jit(solution)/shard_map/pallas_call | solution.py:46
  187.3 2.7 %collective-permute-start.23 = (bf16[128,2560]{1,0:T(8,128)(2,1)S(1)}, bf16[128,2560]{1,0:T(8,128)(2,1)S(1)}, u32[]{:S(2)}, u32[]{:S(2)}) collective-permute-start(bf16[128,2560]{1,0:T(8,128)(2,1)S(1)} %shard_map.152.refs_2_), channel_id=1, source_target_pairs={{0,4},{2,6},{4,0},{6,2},{8,12},{10,14},{12,8},{14,10},{1,5},{3,7},... | collective-permute-start | bytes 1966088 | tf_op jit(solution)/shard_map/ppermute | solution.py:461
  191.2 4.6 %shard_map.154 = (bf16[3,64,3200]{2,1,0:T(8,128)(2,1)S(1)}, bf16[3,64,3200]{2,1,0:T(8,128)(2,1)}) custom-call(s32[19]{0:T(128)S(1)} %copy-done.22, bf16[512,128]{1,0:T(8,128)(2,1)S(1)} %get-tuple-element.49.refs_5_.refs_0_, bf16[512,3200]{1,0:T(8,128)(2,1)S(1)} %copy-done.17, bf16[128,2560]{1,0:T(8,128)(2,1)S(1)} %shard_map.153.refs_2_), custom_call_target="tpu_custom_call" | custom-call | flops 1000 | bytes 1000 | tf_op jit(solution)/shard_map/pallas_call | solution.py:46
  195.8 3.5 %collective-permute-start.27 = (bf16[3,64,3200]{2,1,0:T(8,128)(2,1)}, bf16[3,64,3200]{2,1,0:T(8,128)(2,1)S(1)}, u32[]{:S(2)}, u32[]{:S(2)}) collective-permute-start(bf16[3,64,3200]{2,1,0:T(8,128)(2,1)} %get-tuple-element.67), channel_id=1, source_target_pairs={{0,1},{1,0},{2,3},{3,2},{4,5},{5,4},{6,7},{7,6},{8,9},{9,8},{10,11... | collective-permute-start | bytes 3686408 | tf_op jit(solution)/shard_map/ppermute | solution.py:472
  203.9 4.2 %collective-permute-start.26 = (bf16[64,2560]{1,0:T(8,128)(2,1)S(1)}, bf16[64,2560]{1,0:T(8,128)(2,1)}, u32[]{:S(2)}, u32[]{:S(2)}) collective-permute-start(bf16[64,2560]{1,0:T(8,128)(2,1)S(1)} %get-tuple-element.66.refs_2_), channel_id=1, source_target_pairs={{0,1},{1,0},{2,3},{3,2},{4,5},{5,4},{6,7},{7,6},{8,9},{9,8},{10,11... | collective-permute-start | bytes 983048 | tf_op jit(solution)/shard_map/ppermute | solution.py:474
  (127 shorter events, 50.8 us)
Async XLA Ops:
  0.6 42.9 %collective-permute-start.3 = (bf16[2560,3200]{1,0:T(8,128)(2,1)}, bf16[2560,3200]{1,0:T(8,128)(2,1)}, u32[]{:S(2)}, u32[]{:S(2)}) collective-permute-start(bf16[2560,3200]{1,0:T(8,128)(2,1)} %refs_8_.13), channel_id=1, source_target_pairs={{0,1},{1,0},{2,3},{3,2},{4,5},{5,4},{6,7},{7,6},{8,9},{9,8},{10,11... | collective-permute-start | bytes 49152008 | tf_op jit(solution)/shard_map/ppermute | solution.py:407
  0.8 18.0 %collective-permute-start.1 = (bf16[64,5120]{1,0:T(8,128)(2,1)}, bf16[64,5120]{1,0:T(8,128)(2,1)S(1)}, u32[]{:S(2)}, u32[]{:S(2)}) collective-permute-start(bf16[64,5120]{1,0:T(8,128)(2,1)} %refs_0_.9), channel_id=1, source_target_pairs={{0,4},{2,6},{4,0},{6,2},{8,12},{10,14},{12,8},{14,10},{1,5},{3,7},... | collective-permute-start | bytes 1966088 | tf_op jit(solution)/shard_map/ppermute | solution.py:408
  3.5 15.2 %collective-permute-start.4 = (bf16[64,5120]{1,0:T(8,128)(2,1)}, bf16[64,5120]{1,0:T(8,128)(2,1)S(1)}, u32[]{:S(2)}, u32[]{:S(2)}) collective-permute-start(bf16[64,5120]{1,0:T(8,128)(2,1)} %refs_0_.9), channel_id=1, source_target_pairs={{4,8},{6,10},{8,4},{10,6},{5,9},{7,11},{9,5},{11,7},{20,24},{22,26... | collective-permute-start | bytes 1966088 | tf_op jit(solution)/shard_map/ppermute | solution.py:409
  4.2 17.3 %collective-permute-start = (bf16[64,5120]{1,0:T(8,128)(2,1)}, bf16[64,5120]{1,0:T(8,128)(2,1)S(1)}, u32[]{:S(2)}, u32[]{:S(2)}) collective-permute-start(bf16[64,5120]{1,0:T(8,128)(2,1)} %refs_0_.9), channel_id=1, source_target_pairs={{0,2},{2,0},{4,6},{6,4},{8,10},{10,8},{12,14},{14,12},{1,3},{3,1},... | collective-permute-start | bytes 1966088 | tf_op jit(solution)/shard_map/ppermute | solution.py:410
  20.2 20.8 %collective-permute-start.5 = (bf16[64,5120]{1,0:T(8,128)(2,1)S(1)}, bf16[64,5120]{1,0:T(8,128)(2,1)}, u32[]{:S(2)}, u32[]{:S(2)}) collective-permute-start(bf16[64,5120]{1,0:T(8,128)(2,1)S(1)} %collective-permute-done.4), channel_id=1, source_target_pairs={{4,0},{6,2},{8,12},{10,14},{5,1},{7,3},{9,13},{11,15},{20,16},{22,... | collective-permute-start | bytes 1966088 | tf_op jit(solution)/shard_map/ppermute | solution.py:414
  21.5 20.7 %collective-permute-start.2 = (bf16[64,5120]{1,0:T(8,128)(2,1)S(1)}, bf16[64,5120]{1,0:T(8,128)(2,1)S(1)}, u32[]{:S(2)}, u32[]{:S(2)}) collective-permute-start(bf16[64,5120]{1,0:T(8,128)(2,1)S(1)} %collective-permute-done.1.refs_2_.refs_6_), channel_id=1, source_target_pairs={{0,2},{2,0},{4,6},{6,4},{8,10},{10,8},{12,14},{14,12},{1,3},{3,1},... | collective-permute-start | bytes 1966088 | tf_op jit(solution)/shard_map/ppermute | solution.py:412
  22.8 34.3 %collective-permute-start.8 = (bf16[64,5120]{1,0:T(8,128)(2,1)}, bf16[64,5120]{1,0:T(8,128)(2,1)S(1)}, u32[]{:S(2)}, u32[]{:S(2)}) collective-permute-start(bf16[64,5120]{1,0:T(8,128)(2,1)} %collective-permute-done.7), channel_id=1, source_target_pairs={{4,0},{6,2},{8,12},{10,14},{5,1},{7,3},{9,13},{11,15},{20,16},{22,... | collective-permute-start | bytes 1966088 | tf_op jit(solution)/shard_map/ppermute | solution.py:417
  42.2 15.0 %collective-permute-start.6 = (bf16[64,5120]{1,0:T(8,128)(2,1)S(1)}, bf16[64,5120]{1,0:T(8,128)(2,1)S(1)}, u32[]{:S(2)}, u32[]{:S(2)}) collective-permute-start(bf16[64,5120]{1,0:T(8,128)(2,1)S(1)} %broadcast_select_fusion.1.refs_4_.refs_0_), channel_id=1, source_target_pairs={{0,2},{2,0},{4,6},{6,4},{8,10},{10,8},{12,14},{14,12},{1,3},{3,1},... | collective-permute-start | bytes 1966088 | tf_op jit(solution)/shard_map/ppermute | solution.py:416
  57.2 13.9 %collective-permute-start.9 = (bf16[64,5120]{1,0:T(8,128)(2,1)S(1)}, bf16[64,5120]{1,0:T(8,128)(2,1)S(1)}, u32[]{:S(2)}, u32[]{:S(2)}) collective-permute-start(bf16[64,5120]{1,0:T(8,128)(2,1)S(1)} %broadcast_select_fusion.refs_6_.refs_2_), channel_id=1, source_target_pairs={{0,2},{2,0},{4,6},{6,4},{8,10},{10,8},{12,14},{14,12},{1,3},{3,1},... | collective-permute-start | bytes 1966088 | tf_op jit(solution)/shard_map/ppermute | solution.py:423
  72.1 7.9 %collective-permute-start.10 = (bf16[512,128]{1,0:T(8,128)(2,1)S(1)}, bf16[512,128]{1,0:T(8,128)(2,1)S(1)}, u32[]{:S(2)}, u32[]{:S(2)}) collective-permute-start(bf16[512,128]{1,0:T(8,128)(2,1)S(1)} %get-tuple-element.44.refs_10_), channel_id=1, source_target_pairs={{0,2},{2,0},{4,6},{6,4},{8,10},{10,8},{12,14},{14,12},{1,3},{3,1},... | collective-permute-start | bytes 393224 | tf_op jit(solution)/shard_map/ppermute | solution.py:430
  80.7 10.0 %collective-permute-start.11 = (bf16[512,128]{1,0:T(8,128)(2,1)S(1)}, bf16[512,128]{1,0:T(8,128)(2,1)S(1)}, u32[]{:S(2)}, u32[]{:S(2)}) collective-permute-start(bf16[512,128]{1,0:T(8,128)(2,1)S(1)} %get-tuple-element.46.refs_10_), channel_id=1, source_target_pairs={{0,4},{2,6},{4,0},{6,2},{8,12},{10,14},{12,8},{14,10},{1,5},{3,7},... | collective-permute-start | bytes 393224 | tf_op jit(solution)/shard_map/ppermute | solution.py:430
  108.4 16.8 %collective-permute-start.15 = (bf16[2,128,3200]{2,1,0:T(8,128)(2,1)}, bf16[2,128,3200]{2,1,0:T(8,128)(2,1)S(1)}, u32[]{:S(2)}, u32[]{:S(2)}) collective-permute-start(bf16[2,128,3200]{2,1,0:T(8,128)(2,1)} %shard_map.142.refs_4_.refs_0_), channel_id=1, source_target_pairs={{0,1},{1,0},{2,3},{3,2},{4,5},{5,4},{6,7},{7,6},{8,9},{9,8},{10,11... | collective-permute-start | bytes 4915208 | tf_op jit(solution)/shard_map/ppermute | solution.py:445
  125.2 20.3 %collective-permute-start.16 = (bf16[2,128,3200]{2,1,0:T(8,128)(2,1)S(1)}, bf16[2,128,3200]{2,1,0:T(8,128)(2,1)S(1)}, u32[]{:S(2)}, u32[]{:S(2)}) collective-permute-start(bf16[2,128,3200]{2,1,0:T(8,128)(2,1)S(1)} %shard_map.144.refs_4_.refs_0_), channel_id=1, source_target_pairs={{0,1},{1,0},{2,3},{3,2},{4,5},{5,4},{6,7},{7,6},{8,9},{9,8},{10,11... | collective-permute-start | bytes 4915208 | tf_op jit(solution)/shard_map/ppermute | solution.py:449
  126.5 16.3 %collective-permute-start.14 = (bf16[128,2560]{1,0:T(8,128)(2,1)S(1)}, bf16[128,2560]{1,0:T(8,128)(2,1)S(1)}, u32[]{:S(2)}, u32[]{:S(2)}) collective-permute-start(bf16[128,2560]{1,0:T(8,128)(2,1)S(1)} %get-tuple-element.51.refs_7_), channel_id=1, source_target_pairs={{0,2},{2,0},{4,6},{6,4},{8,10},{10,8},{12,14},{14,12},{1,3},{3,1},... | collective-permute-start | bytes 1966088 | tf_op jit(solution)/shard_map/ppermute | solution.py:440
  145.5 26.7 %collective-permute-start.17 = (bf16[2,128,3200]{2,1,0:T(8,128)(2,1)S(1)}, bf16[2,128,3200]{2,1,0:T(8,128)(2,1)S(1)}, u32[]{:S(2)}, u32[]{:S(2)}) collective-permute-start(bf16[2,128,3200]{2,1,0:T(8,128)(2,1)S(1)} %shard_map.147.refs_4_.refs_0_), channel_id=1, source_target_pairs={{0,1},{1,0},{2,3},{3,2},{4,5},{5,4},{6,7},{7,6},{8,9},{9,8},{10,11... | collective-permute-start | bytes 4915208 | tf_op jit(solution)/shard_map/ppermute | solution.py:454
  146.5 16.8 %collective-permute-start.19 = (bf16[128,2560]{1,0:T(8,128)(2,1)S(1)}, bf16[128,2560]{1,0:T(8,128)(2,1)S(1)}, u32[]{:S(2)}, u32[]{:S(2)}) collective-permute-start(bf16[128,2560]{1,0:T(8,128)(2,1)S(1)} %get-tuple-element.53.refs_2_), channel_id=1, source_target_pairs={{0,2},{2,0},{4,6},{6,4},{8,10},{10,8},{12,14},{14,12},{1,3},{3,1},... | collective-permute-start | bytes 1966088 | tf_op jit(solution)/shard_map/ppermute | solution.py:440
  147.8 16.6 %collective-permute-start.18 = (bf16[128,2560]{1,0:T(8,128)(2,1)S(1)}, bf16[128,2560]{1,0:T(8,128)(2,1)S(1)}, u32[]{:S(2)}, u32[]{:S(2)}) collective-permute-start(bf16[128,2560]{1,0:T(8,128)(2,1)S(1)} %shard_map.146.refs_7_.refs_0_), channel_id=1, source_target_pairs={{0,4},{2,6},{12,8},{14,10},{1,5},{3,7},{13,9},{15,11},{16,20},{18,... | collective-permute-start | bytes 1966088 | tf_op jit(solution)/shard_map/ppermute | solution.py:451
  165.1 20.0 %collective-permute-start.22 = (bf16[128,2560]{1,0:T(8,128)(2,1)S(1)}, bf16[128,2560]{1,0:T(8,128)(2,1)S(1)}, u32[]{:S(2)}, u32[]{:S(2)}) collective-permute-start(bf16[128,2560]{1,0:T(8,128)(2,1)S(1)} %shard_map.150.refs_4_), channel_id=1, source_target_pairs={{4,8},{6,10},{8,4},{10,6},{5,9},{7,11},{9,5},{11,7},{20,24},{22,26... | collective-permute-start | bytes 1966088 | tf_op jit(solution)/shard_map/ppermute | solution.py:458
  165.8 19.3 %collective-permute-start.21 = (bf16[128,2560]{1,0:T(8,128)(2,1)S(1)}, bf16[128,2560]{1,0:T(8,128)(2,1)S(1)}, u32[]{:S(2)}, u32[]{:S(2)}) collective-permute-start(bf16[128,2560]{1,0:T(8,128)(2,1)S(1)} %get-tuple-element.57.refs_2_), channel_id=1, source_target_pairs={{0,2},{2,0},{4,6},{6,4},{8,10},{10,8},{12,14},{14,12},{1,3},{3,1},... | collective-permute-start | bytes 1966088 | tf_op jit(solution)/shard_map/ppermute | solution.py:440
  166.2 19.6 %collective-permute-start.24 = (bf16[128,2560]{1,0:T(8,128)(2,1)S(1)}, bf16[128,2560]{1,0:T(8,128)(2,1)S(1)}, u32[]{:S(2)}, u32[]{:S(2)}) collective-permute-start(bf16[128,2560]{1,0:T(8,128)(2,1)S(1)} %shard_map.149.refs_2_.refs_0_), channel_id=1, source_target_pairs={{0,4},{2,6},{12,8},{14,10},{1,5},{3,7},{13,9},{15,11},{16,20},{18,... | collective-permute-start | bytes 1966088 | tf_op jit(solution)/shard_map/ppermute | solution.py:456
  186.6 14.7 %collective-permute-start.25 = (bf16[128,2560]{1,0:T(8,128)(2,1)S(1)}, bf16[128,2560]{1,0:T(8,128)(2,1)S(1)}, u32[]{:S(2)}, u32[]{:S(2)}) collective-permute-start(bf16[128,2560]{1,0:T(8,128)(2,1)S(1)} %shard_map.153.refs_2_), channel_id=1, source_target_pairs={{4,8},{6,10},{8,4},{10,6},{5,9},{7,11},{9,5},{11,7},{20,24},{22,26... | collective-permute-start | bytes 1966088 | tf_op jit(solution)/shard_map/ppermute | solution.py:463
  187.3 14.8 %collective-permute-start.23 = (bf16[128,2560]{1,0:T(8,128)(2,1)S(1)}, bf16[128,2560]{1,0:T(8,128)(2,1)S(1)}, u32[]{:S(2)}, u32[]{:S(2)}) collective-permute-start(bf16[128,2560]{1,0:T(8,128)(2,1)S(1)} %shard_map.152.refs_2_), channel_id=1, source_target_pairs={{0,4},{2,6},{4,0},{6,2},{8,12},{10,14},{12,8},{14,10},{1,5},{3,7},... | collective-permute-start | bytes 1966088 | tf_op jit(solution)/shard_map/ppermute | solution.py:461
  190.0 13.0 %collective-permute-start.20 = (bf16[128,2560]{1,0:T(8,128)(2,1)S(1)}, bf16[128,2560]{1,0:T(8,128)(2,1)S(1)}, u32[]{:S(2)}, u32[]{:S(2)}) collective-permute-start(bf16[128,2560]{1,0:T(8,128)(2,1)S(1)} %get-tuple-element.59.refs_3_), channel_id=1, source_target_pairs={{0,2},{2,0},{4,6},{6,4},{8,10},{10,8},{12,14},{14,12},{1,3},{3,1},... | collective-permute-start | bytes 1966088 | tf_op jit(solution)/shard_map/ppermute | solution.py:440
  195.8 16.1 %collective-permute-start.27 = (bf16[3,64,3200]{2,1,0:T(8,128)(2,1)}, bf16[3,64,3200]{2,1,0:T(8,128)(2,1)S(1)}, u32[]{:S(2)}, u32[]{:S(2)}) collective-permute-start(bf16[3,64,3200]{2,1,0:T(8,128)(2,1)} %get-tuple-element.67), channel_id=1, source_target_pairs={{0,1},{1,0},{2,3},{3,2},{4,5},{5,4},{6,7},{7,6},{8,9},{9,8},{10,11... | collective-permute-start | bytes 3686408 | tf_op jit(solution)/shard_map/ppermute | solution.py:472
  (32 other events, 334.8 us)
